TPU v7x, 32 devices: a whole 2x2x4 slice. The times are simulated.
32 devices in a mesh: fsdp: 4 (over z), ctx: 2 (over x), tp: 4 (over y, core).
Axes of the slice: x: 2, y: 2, z: 4, core: 2. Of those that a mesh axis runs over, the one named last changes fastest.
Arguments:
- hidden_in: bfloat16 [4, 1024, 1024], P('fsdp', 'ctx'), may hold values from -6 to 6
- lengths: int32 [4], P('fsdp'), may hold values from 513 to 1024, as said below
- positions: int32 [4, 1024], P('fsdp', 'ctx'), may hold values from 0 to 4092, as said below
- query_weight: bfloat16 [1024, 1024], P('fsdp', 'tp'), may hold values from -0.1875 to 0.1875
- key_weight: bfloat16 [1024, 512], P('fsdp', 'tp'), may hold values from -0.1875 to 0.1875
- value_weight: bfloat16 [1024, 512], P('fsdp', 'tp'), may hold values from -0.1875 to 0.1875
- output_weight: bfloat16 [1024, 1024], P('tp', 'fsdp'), may hold values from -3 to 3
- gate_weight: bfloat16 [1024, 4608], P('fsdp', 'tp'), may hold values from -0.1875 to 0.1875
- up_weight: bfloat16 [1024, 4608], P('fsdp', 'tp'), may hold values from -0.1875 to 0.1875
- down_weight: bfloat16 [4608, 1024], P('tp', 'fsdp'), may hold values from -0.09375 to 0.09375
- attention_gain: bfloat16 [1024], P('fsdp'), may hold values from 0.099609375 to 1.8984375
- feedforward_gain: bfloat16 [1024], P('fsdp'), may hold values from 0.099609375 to 1.8984375
- query_gain: bfloat16 [64], replicated, may hold values from 0.099609375 to 1.8984375
- key_gain: bfloat16 [64], replicated, may hold values from 0.099609375 to 1.8984375
- cotangent: bfloat16 [4, 1024, 1024], P('fsdp', 'ctx'), may hold values from -6 to 6
Outputs:
- block_out: bfloat16 [4, 1024, 1024], P('fsdp', 'ctx')
- input_grad: float32 [4, 1024, 1024], P('fsdp', 'ctx')
- query_weight_grad: float32 [1024, 1024], P('fsdp', 'tp')
- key_weight_grad: float32 [1024, 512], P('fsdp', 'tp')
- value_weight_grad: float32 [1024, 512], P('fsdp', 'tp')
- output_weight_grad: float32 [1024, 1024], P('tp', 'fsdp')
- gate_weight_grad: float32 [1024, 4608], P('fsdp', 'tp')
- up_weight_grad: float32 [1024, 4608], P('fsdp', 'tp')
- down_weight_grad: float32 [4608, 1024], P('tp', 'fsdp')
- attention_gain_grad: float32 [1024], P('fsdp')
- feedforward_gain_grad: float32 [1024], P('fsdp')
- query_gain_grad: float32 [64], replicated
- key_gain_grad: float32 [64], replicated
- rms_stats: float32 [4], replicated
Inputs may be any that keep to these rules, and one draw needn't show every extreme that they name: `lengths`: slots at and after a sequence's length are padding. In every draw one sequence has 1024 valid slots and another 1024 // 2 + 1. Along a sequence positions rise by 1 to 3 from slot to slot; the first lies below 1024.
All inputs are finite; a program needn't handle non-finite values.
Results may differ from a plain program's by a relative error of at most 0.013.
Values may be sent and summed in bfloat16 or wider, within the bound.
No kernel may reach another device: no remote copies, remote signals or barrier semaphores. Data moves between devices by JAX's collectives and lax.ppermute only.
A program may use at most 128 MiB of HBM per device.

v0:
```python
import jax
import jax.numpy as jnp
from jax import lax
from jax.experimental import pallas as pl
from jax.experimental.pallas import tpu as pltpu
from jax.sharding import Mesh, PartitionSpec as P

HD = 64
epsilon = 1e-05
rope_base = 1000000.0
F32 = jnp.float32
BF16 = jnp.bfloat16
PLANE = ("ctx", "y", "core")


def swap(value, axis):
    return lax.ppermute(value, axis, [(0, 1), (1, 0)])


def hop(value, axis, step=1):
    size = lax.axis_size(axis)
    return lax.ppermute(value, axis, [(i, i ^ step) for i in range(size)])


def scatter_start(near, far):
    rows, width = near.shape[0] // 2, near.shape[1] // 2
    low, keep = ((rows, width), BF16), ((rows, width), F32)
    left_low, right_low, left, right = call(split_sum, [low, low, keep, keep], (near, far))
    return left, swap(left_low, "ctx"), right, swap(right_low, "y")


def scatter_halves(left, from_x, right, from_y):
    rows, width = left.shape[0] // 2, left.shape[1]
    low, keep = ((rows, width), BF16), ((rows, width), F32)
    return call(split_again, [keep, low, keep, low], (left, from_x, right, from_y))


def scatter_swap(left, left_low, right, right_low):
    return left, swap(left_low, "y"), right, swap(right_low, "ctx")


def scatter_next(left, from_x, right, from_y):
    return scatter_swap(*scatter_halves(left, from_x, right, from_y))


def sum_scatter(near, far):
    return scatter_next(*scatter_start(near, swap(far, "core")))


def gather_end(left, left_x, right, right_y):
    width = left.shape[1]
    left = jnp.stack([left, left_x])
    right = jnp.stack([right, right_y])
    left = jnp.stack([left, swap(left, "y")], 1)
    right = jnp.stack([right, swap(right, "ctx")], 0)
    near = jnp.concatenate([left, right], -1).reshape(-1, 2 * width)
    return near, swap(near, "core")


def gather_plane(left, right, beside):
    beside, left_x, right_y = together(swap(beside, "core"), swap(left, "ctx"), swap(right, "y"))
    return *gather_end(left, left_x, right, right_y), beside


def near_shards():
    return lax.axis_size("fsdp") <= 4


def direct(pieces):
    size = lax.axis_size("fsdp")
    return [
        piece if step == 0 else lax.ppermute(piece, "fsdp", [(i, i ^ step) for i in range(size)])
        for step, piece in enumerate(pieces)
    ]


def onward(value):
    size = lax.axis_size("fsdp")
    return lax.ppermute(value, "fsdp", [(i, (i + 1) % size) for i in range(size)])


def together(*values):
    return lax.optimization_barrier(values)


def region(flag, work, *args):
    shapes = jax.eval_shape(work, *args)
    return lax.cond(flag, work, lambda *_: jax.tree.map(lambda x: jnp.zeros(x.shape, x.dtype), shapes), *args)


def lanes(shape):
    return lax.broadcasted_iota(jnp.int32, shape, len(shape) - 1)


def nt(left, right):
    return lax.dot_general(left, right, (((1,), (1,)), ((), ())), preferred_element_type=F32)


def tn(left, right):
    return lax.dot_general(left, right, (((0,), (0,)), ((), ())), preferred_element_type=F32)


def nn(left, right):
    return lax.dot_general(left, right, (((1,), (0,)), ((), ())), preferred_element_type=F32)


def half_sums(values, low):
    first = jnp.sum(jnp.where(low, values, 0.0), axis=-1, keepdims=True)
    second = jnp.sum(jnp.where(low, 0.0, values), axis=-1, keepdims=True)
    return first, second


def turned(values):
    return jnp.where(lanes(values.shape) % HD < HD // 2, pltpu.roll(values, 96, 1), pltpu.roll(values, 32, 1))


def rows_of(own, kk, xx, yy, block):
    return pl.multiple_of((own ^ (xx * 4 + yy * 2 + kk)) * block, block)


def attention_forward(
    index, h0, h1, h2, h3, cosine, sine, query_gain, key_gain, *rest
):
    *parts, w, gains, part_low, part_high, unit, query, key, value, raw, mixed, mixed_rel, inverse = rest
    own, length = index[0], index[1]
    if len(parts) > 2:
        rows = w.shape[0] // len(parts)
        for at, part in enumerate(parts):
            to = pl.multiple_of((index[2] ^ at) * rows, rows)
            w[pl.ds(to, rows), :] = part[:rows, :]
            gains[:, pl.ds(to, rows)] = part[rows : rows + 16, :rows].astype(F32)[:8]
    else:
        w[...] = parts[0][...]
        gains[...] = parts[1][...]
    gain = gains[0:1, :]
    pair = h0.shape[0]
    block = pair // 2
    low = lanes((pair, 2 * HD)) < HD
    for at, h in enumerate((h0, h1, h2, h3)):
        kk, xx = divmod(at, 2)
        here = slice(at * pair, (at + 1) * pair)
        x = h[...].astype(F32)
        r = lax.rsqrt(jnp.mean(x * x, axis=-1, keepdims=True) + epsilon)
        u = (x * r * gain).astype(BF16)
        unit[here, :] = u
        lin = nn(u, w[:, : 4 * HD])
        raw[here, :] = lin
        q, kv = lin[:, : 2 * HD], lin[:, 2 * HD :]
        one, two = half_sums(q * q, low)
        r = jnp.where(low, lax.rsqrt(one / HD + epsilon), lax.rsqrt(two / HD + epsilon))
        y = q * r * query_gain[...]
        c, s = cosine[here, :], sine[here, :]
        q = (y * c + turned(y) * s).astype(BF16).astype(F32) * HD**-0.5
        one, _ = half_sums(kv * kv, low)
        y = kv * lax.rsqrt(one / HD + epsilon) * key_gain[...]
        kv = jnp.where(low, y * c + turned(y) * s, kv)
        other = pltpu.roll(kv, HD, 1)
        k, v = jnp.where(low, kv, other), jnp.where(low, other, kv)
        for yy in range(2):
            to = rows_of(own, kk, xx, yy, block)
            some = slice(yy * block, (yy + 1) * block)
            query[pl.ds(to, block), :] = q[some].astype(BF16)
            key[pl.ds(to, block), :] = k[some].astype(BF16)
            value[pl.ds(to, block), :] = v[some].astype(BF16)
    for at in range(4):
        here = slice(at * pair, (at + 1) * pair)
        n = (at + 1) * pair
        q = query[here, :]
        q = jnp.concatenate([jnp.where(low, q, jnp.zeros_like(q)), jnp.where(low, jnp.zeros_like(q), q)])
        e = masked_exp(q, key, at, pair, length)
        total = 1.0 / jnp.sum(e, axis=-1, keepdims=True)
        o = nn((e * total).astype(BF16), value[:n, :])
        mixed[here, :] = jnp.where(low, o[:pair], o[pair:])
        inverse[here, :] = jnp.where(low, total[:pair], total[pair:])
    for at in range(4):
        kk, xx = divmod(at, 2)
        pieces = [mixed[pl.ds(rows_of(own, kk, xx, yy, block), block), :] for yy in range(2)]
        m = jnp.concatenate(pieces).astype(BF16)
        mixed_rel[at * pair : (at + 1) * pair, :] = m
        part = nt(m, w[:, 4 * HD :]).astype(BF16)
        to = part_high if kk else part_low
        to[xx * pair : (xx + 1) * pair, :] = part


def masked_exp(query, key, at, pair, length):
    parts = []
    for past in range(at + 1):
        scores = nt(query, key[past * pair : (past + 1) * pair, :])
        columns = lax.broadcasted_iota(jnp.int32, scores.shape, 1)
        here = columns < length - past * pair
        if past == at:
            here = here & (columns <= lax.broadcasted_iota(jnp.int32, scores.shape, 0) % pair)
        parts.append(jnp.where(here, jnp.exp(scores), 0.0))
    return jnp.concatenate(parts, 1)


def attention_backward(
    index, a_low, a_high, w, query, key, value, raw, mixed, inverse, cosine, sine, query_gain, key_gain,
    first_low, first_high, back, gains, down, dq, dk, dv,
):
    own, length = index[0], index[1]
    pair = a_low.shape[0] // 2
    block = pair // 2
    low = lanes((pair, 2 * HD)) < HD
    for at in range(4):
        kk, xx = divmod(at, 2)
        a = a_high if kk else a_low
        m = nn(a[xx * pair : (xx + 1) * pair, :], w[:, 4 * HD :]).astype(BF16)
        for yy in range(2):
            down[pl.ds(rows_of(own, kk, xx, yy, block), block), :] = m[yy * block : (yy + 1) * block]
    dk[...] = jnp.zeros_like(dk)
    dv[...] = jnp.zeros_like(dv)
    for at in range(4):
        here = slice(at * pair, (at + 1) * pair)
        n = (at + 1) * pair
        q, m = query[here, :], down[here, :]
        zero = jnp.zeros_like(q)
        q = jnp.concatenate([jnp.where(low, q, zero), jnp.where(low, zero, q)])
        one, two = half_sums(m.astype(F32) * mixed[here, :], low)
        drop = jnp.concatenate([one, two])
        m = jnp.concatenate([jnp.where(low, m, zero), jnp.where(low, zero, m)])
        total = jnp.concatenate([inverse[here, 0:1], inverse[here, HD : HD + 1]])
        p = masked_exp(q, key, at, pair, length) * total
        g = (p * (nt(m, value[:n, :]) - drop)).astype(BF16)
        dv[:n, :] += tn(p.astype(BF16), m)
        dk[:n, :] += tn(g, q)
        o = nn(g, key[:n, :])
        dq[here, :] = jnp.where(low, o[:pair], o[pair:]) * HD**-0.5
    query_sum = jnp.zeros((1, 2 * HD), F32)
    key_sum = jnp.zeros((1, 2 * HD), F32)
    for at in range(4):
        kk, xx = divmod(at, 2)
        here = slice(at * pair, (at + 1) * pair)
        spots = [pl.ds(rows_of(own, kk, xx, yy, block), block) for yy in range(2)]
        c, s = cosine[here, :], sine[here, :]
        x, kv = raw[here, : 2 * HD], raw[here, 2 * HD :]
        one, two = half_sums(x * x, low)
        r = jnp.where(low, lax.rsqrt(one / HD + epsilon), lax.rsqrt(two / HD + epsilon))
        z = x * r
        y = jnp.concatenate([dq[spot, :] for spot in spots])
        y = y * c - turned(y) * s
        query_sum += jnp.sum(y * z, axis=0, keepdims=True)
        y = y * query_gain[...]
        one, two = half_sums(y * z, low)
        x = r * (y - z * jnp.where(low, one / HD, two / HD))
        one, _ = half_sums(kv * kv, low)
        r = lax.rsqrt(one / HD + epsilon)
        z = kv * r
        y = jnp.concatenate([dk[spot, :] for spot in spots])
        y = y + pltpu.roll(y, HD, 1)
        y = y * c - turned(y) * s
        key_sum += jnp.sum(y * z, axis=0, keepdims=True)
        y = y * key_gain[...]
        one, _ = half_sums(y * z, low)
        v = jnp.concatenate([dv[spot, :] for spot in spots])
        kv = jnp.where(low, r * (y - z * (one / HD)), v + pltpu.roll(v, HD, 1))
        lin = jnp.concatenate([x, kv], axis=1).astype(BF16)
        back[here, :] = lin
        part = nt(lin, w[:, : 4 * HD]).astype(BF16)
        to = first_high if kk else first_low
        to[xx * pair : (xx + 1) * pair, :] = part
    gains[0:1, :] = query_sum
    gains[1:2, :] = key_sum


def activated_gradient(index, b0, b1, b2, b3, *rest):
    *parts, down_w, back = rest
    own, length = index[0], index[1]
    count, rows = len(parts), parts[0].shape[0]
    for at, part in enumerate(parts):
        to = pl.multiple_of((index[2] + count - at) % count * rows, rows)
        down_w[pl.ds(to, rows), :] = part[...]
    pair = b0.shape[0]
    block = pair // 2
    row = lax.broadcasted_iota(jnp.int32, (pair, 1), 0)
    for at, b in enumerate((b0, b1, b2, b3)):
        kk, xx = divmod(at, 2)
        ok = (own ^ (kk + 4 * xx + jnp.where(row >= block, 2, 0))) * block + row % block < length
        back[at * pair : (at + 1) * pair, :] = jnp.where(ok, nn(b[...], down_w[...]), 0.0)


def feed_forward(index, x_low, x_high, b0, b1, b2, b3, back_all, gu_w, second_low, second_high, grad, activated, gate_up):
    own, length = index[0], index[1]
    width = x_low.shape[1]
    pair = b0.shape[0]
    block, four = pair // 2, 2 * pair
    main = gate_up.shape[1] // 2 // 128 * 128
    both = 2 * main
    wide = both + 128
    low = lanes((four, 128)) < HD
    row = lax.broadcasted_iota(jnp.int32, (four, 1), 0)
    bs = (b0, b1, b2, b3)
    for kk, (x, to) in enumerate(((x_low, second_low), (x_high, second_high))):
        here = slice(kk * four, (kk + 1) * four)
        start = own ^ (kk + jnp.where(row >= pair, 4, 0) + jnp.where(row % pair >= block, 2, 0))
        ok = start * block + row % block < length
        gu = nn(x[...], gu_w[...])
        back = back_all[here, :]
        tail = gu[:, both:]
        gate = jnp.concatenate([gu[:, :main], tail], 1)
        upper = jnp.concatenate([gu[:, main:both], pltpu.roll(tail, HD, 1)], 1)
        sigmoid = 1.0 / (1.0 + jnp.exp(-gate))
        silu = gate * sigmoid
        act = jnp.where(ok, silu * upper, 0.0)
        gate_back = back * upper * (sigmoid + silu * (1.0 - sigmoid))
        upper_back = back * silu
        activated[here, :main] = act[:, :main].astype(BF16)
        activated[here, main:] = jnp.where(low, act[:, main:], 0.0).astype(BF16)
        mix = jnp.where(low, gate_back[:, main:], pltpu.roll(upper_back[:, main:], HD, 1))
        gate_up[here, :main] = gate_back[:, :main].astype(BF16)
        gate_up[here, main:both] = upper_back[:, :main].astype(BF16)
        gate_up[here, both:] = mix.astype(BF16)
        to[...] = nt(gate_up[here, :], gu_w[...]).astype(BF16)
    step = width // 2
    for row in range(0, width, step):
        here = slice(row, row + step)
        out = tn(x_low[:, here], gate_up[:four, :]) + tn(x_high[:, here], gate_up[four:, :])
        grad[here, :wide] = out.astype(BF16)
        out = tn(b0[:, here], activated[:pair, :])
        for piece in range(1, 4):
            out += tn(bs[piece][:, here], activated[piece * pair : (piece + 1) * pair, :])
        grad[here, wide:] = out.astype(BF16)


def down_product(index, activated, down_w, branch_low, branch_high):
    four = branch_low.shape[0]
    branch_low[...] = nt(activated[:four, :], down_w[...]).astype(BF16)
    branch_high[...] = nt(activated[four:, :], down_w[...]).astype(BF16)


def split_sum(near, far, left_low, right_low, left, right):
    rows, width = left.shape
    block = rows // 2
    for xx in range(2):
        for yy in range(2):
            here = slice((2 * xx + yy) * block, (2 * xx + yy + 1) * block)
            total = near[here, :].astype(F32) + far[here, :].astype(F32)
            for to, part, sent, at in (
                ((left_low if xx else left), total[:, :width], xx, yy),
                ((right_low if yy else right), total[:, width:], yy, xx),
            ):
                to[at * block : (at + 1) * block, :] = part.astype(BF16) if sent else part


def split_again(left, from_x, right, from_y, left_out, left_low, right_out, right_low):
    block = left_out.shape[0]
    for part, other, out, low in ((left, from_x, left_out, left_low), (right, from_y, right_out, right_low)):
        total = part[...] + other[...].astype(F32)
        out[...] = total[:block]
        low[...] = total[block:].astype(BF16)


def joined(left, from_y, right, from_x):
    left = left[...] + from_y[...].astype(F32)
    return jnp.concatenate([left, right[...] + from_x[...].astype(F32)], 1)


def inverse_of(values):
    return lax.rsqrt(jnp.mean(values * values, axis=-1, keepdims=True) + epsilon)


def validity(index, block):
    row = lax.broadcasted_iota(jnp.int32, (block, 1), 0)
    return (index[0] * block + row < index[1]).astype(F32)


def halves_of(values, left, right):
    width = left.shape[1]
    left[...] = values[:, :width].astype(BF16)
    right[...] = values[:, width:].astype(BF16)


def to_middle(left, from_y, right, from_x, hidden, gains, middle, inverse, out_left, out_right):
    block = middle.shape[0]
    m = hidden[:block, :].astype(F32) + joined(left, from_y, right, from_x)
    r = inverse_of(m)
    middle[...] = m
    inverse[...] = jnp.broadcast_to(r, inverse.shape)
    halves_of(m * r * gains[1:2, :], out_left, out_right)


def to_middle_grad(
    index, left, from_y, right, from_x, middle, inverse, cotangent, gains, second, middle_grad, out_left, out_right
):
    block = middle.shape[0]
    total = joined(left, from_y, right, from_x)
    second[...] = total
    r = inverse[:, 0:1]
    u, c = middle[...] * r, total * gains[1:2, :]
    upstream = cotangent[:block, :].astype(F32) * validity(index, block)
    grad = upstream + r * (c - u * jnp.mean(c * u, axis=-1, keepdims=True))
    middle_grad[...] = grad
    halves_of(grad, out_left, out_right)


def to_output(index, left, from_y, right, from_x, middle, branch, output):
    total = joined(left, from_y, right, from_x)
    branch[...] = total
    output[...] = ((middle[...] + total) * validity(index, middle.shape[0])).astype(BF16)


def to_input_grad(left, from_y, right, from_x, middle_grad, hidden, gains, output, out):
    block = middle_grad.shape[0]
    x = hidden[:block, :].astype(F32)
    r = inverse_of(x)
    u = x * r
    c = joined(left, from_y, right, from_x) * gains[0:1, :]
    out[:block, :] = (middle_grad[...] + r * (c - u * jnp.mean(c * u, axis=-1, keepdims=True))).astype(BF16)
    out[block:, :] = output[...]


def small_sums(index, hidden, middle, branch, second, inverse, attention_sums, head_sums, out):
    block, width = middle.shape
    valid = validity(index, block)
    x, m = hidden[:block, :].astype(F32), middle[...]
    feedforward_sums = jnp.sum(second[...] * (m * inverse[:, 0:1]), axis=0, keepdims=True)
    for at in range(width // 128):
        here = slice(at * 128, (at + 1) * 128)
        out[at : at + 1, :] = feedforward_sums[:, here]
        out[width // 128 + at : width // 128 + at + 1, :] = attention_sums[0:1, here]
    lane = lanes((1, 128))
    q = head_sums[0:1, :] + pltpu.roll(head_sums[0:1, :], HD, 1)
    out[16:17, :] = jnp.where(lane < HD, q, pltpu.roll(head_sums[1:2, :], HD, 1))
    line = jnp.where(lane == 4, jnp.sum(valid), 0.0)
    for at, item in enumerate((x, m - x, m, branch[...])):
        line = jnp.where(lane == at, jnp.sum(item * item * valid), line)
    out[17:18, :] = line
    out[18:, :] = jnp.zeros((out.shape[0] - 18, 128), F32)


def attention_weights(index, unit, back, a_low, a_high, mixed_rel, w, gains, out, gain_out):
    wide = back.shape[1]
    half = a_low.shape[0]
    step = 256
    for row in range(0, out.shape[0], step):
        here = slice(row, row + step)
        grad = tn(unit[:, here], back[...])
        out[here, :wide] = grad.astype(BF16)
        grad = jnp.sum(grad * w[here, :wide].astype(F32), axis=1, keepdims=True)
        gain_out[:, here] = jnp.broadcast_to(grad, (step, 128)).T[:8] / gains[0:1, here]
        o = tn(a_low[:, here], mixed_rel[:half, :]) + tn(a_high[:, here], mixed_rel[half:, :])
        out[here, wide:] = o.astype(BF16)


def fetch(sources, targets, sems):
    copies = [pltpu.make_async_copy(one, two, sems.at[at]) for at, (one, two) in enumerate(zip(sources, targets))]
    for copy in copies:
        copy.start()
    return copies


def halves(own, source, targets, sems, base):
    block = targets[0].shape[0] // 2
    copies = []
    for kk, target in enumerate(targets):
        for yy in range(2):
            start = pl.multiple_of(((own ^ (2 * yy + kk)) & 3) * block, block)
            to = target.at[pl.ds(yy * block, block)]
            copies.append(pltpu.make_async_copy(source.at[0, pl.ds(start, block)], to, sems.at[base + len(copies)]))
    for copy in copies:
        copy.start()
    return copies


def prelude(
    index, query_from, key_from, value_from, output_from, one_from, two_from, hidden,
    out, hidden_near, hidden_far,
    query, key, value, output, one_gain, two_gain, sems,
):
    copies = fetch(
        (query_from, key_from, value_from, output_from, one_from, two_from),
        (query, key, value, output, one_gain, two_gain),
        sems,
    )
    late = halves(index[0], hidden, (hidden_near, hidden_far), sems, len(copies))
    for copy in copies:
        copy.wait()
    rows = query.shape[0]
    wide = query.shape[1] // 2
    for half in range(2):

        @pl.when(index[3] == half)
        def _():
            out[:rows, :wide] = query[:, half * wide : (half + 1) * wide]
            low = lanes((rows, 2 * HD)) < HD
            k, v = key[...].astype(F32), value[...].astype(F32)
            if half:
                kv = jnp.where(low, pltpu.roll(k, HD, 1), v)
            else:
                kv = jnp.where(low, k, pltpu.roll(v, HD, 1))
            out[:rows, wide : wide + 2 * HD] = kv.astype(BF16)
            out[:rows, wide + 2 * HD :] = output[half * wide : (half + 1) * wide, :].astype(F32).T.astype(BF16)

    one, two = one_gain[...].astype(F32)[None], two_gain[...].astype(F32)[None]
    first = lax.broadcasted_iota(jnp.int32, (16, rows), 0) == 0
    out[rows:, :rows] = jnp.where(first, one, two).astype(BF16)
    out[rows:, rows:] = jnp.zeros((16, out.shape[1] - rows), BF16)
    for copy in late:
        copy.wait()


def pack_feed_forward(index, *rest):
    cotangent, out, down_out, cotangent_near, cotangent_far, gate, upper, down, sems = rest[3:]
    copies = fetch(rest[:3], (gate, upper, down), sems)
    late = halves(index[0], cotangent, (cotangent_near, cotangent_far), sems, len(copies))
    for copy in copies:
        copy.wait()
    rows, hidden = gate.shape[0], gate.shape[1] // 2
    main = hidden // 128 * 128
    both, wide = 2 * main, 2 * hidden
    low = lanes((rows, 128)) < HD
    for half in range(2):

        @pl.when(index[3] == half)
        def _():
            tails = []
            for at, part in enumerate((gate, upper)):
                if half:
                    part = pltpu.roll(part[:, main:].astype(F32), main + HD, 1)
                else:
                    part = part[:, : main + 128].astype(F32)
                out[:, at * main : (at + 1) * main] = part[:, :main].astype(BF16)
                tails.append(part[:, main:])
            out[:, both:wide] = jnp.where(low, tails[0], pltpu.roll(tails[1], HD, 1)).astype(BF16)
            turned = down[half * hidden : (half + 1) * hidden, :].astype(F32)
            turned = jnp.concatenate([turned, jnp.zeros((HD, rows), F32)]).T
            down_out[...] = turned.astype(BF16)
    for copy in late:
        copy.wait()


def unpack_attention(index, mine, other, query, key, value, output):
    wide = query.shape[1] // 2
    low = lanes((mine.shape[0], 2 * HD)) < HD
    for half in range(2):

        @pl.when(index[3] == half)
        def _():
            first, second = (other, mine) if half else (mine, other)
            for at, part in enumerate((first, second)):
                query[:, at * wide : (at + 1) * wide] = part[:, :wide].astype(F32)
                output[at * wide : (at + 1) * wide, :] = part[:, wide + 2 * HD :].astype(F32).T
            one = first[:, wide : wide + 2 * HD].astype(F32)
            two = second[:, wide : wide + 2 * HD].astype(F32)
            key[...] = jnp.where(low, one, pltpu.roll(two, HD, 1))
            value[...] = jnp.where(low, pltpu.roll(one, HD, 1), two)


def unpack_feed_forward(index, mine, other, gate, upper, down):
    rows, hidden = mine.shape[0], gate.shape[1] // 2
    main = hidden // 128 * 128
    both, wide = 2 * main, 2 * hidden
    low = lanes((rows, 128)) < HD
    for half in range(2):

        @pl.when(index[3] == half)
        def _():
            first, second = (other, mine) if half else (mine, other)
            for at, to in enumerate((gate, upper)):
                to[:, :main] = first[:, at * main : (at + 1) * main].astype(F32)
                one = first[:, both : both + 128].astype(F32)
                two = second[:, both : both + 128].astype(F32)
                if at:
                    one = pltpu.roll(one, HD, 1)
                else:
                    two = pltpu.roll(two, HD, 1)
                end = second[:, at * main : (at + 1) * main].astype(F32)
                end = pltpu.roll(jnp.concatenate([end, jnp.zeros((rows, 128), F32)], 1), HD, 1)
                to[:, main : main + 128] = jnp.where(low, one, end[:, :128])
                to[:, main + 128 : 2 * main] = end[:, 128:main]
                to[:, 2 * main :] = jnp.where(low, end[:, main:], two)
            for at, part in enumerate((first, second)):
                turned = part[:, wide:].astype(F32).T
                down[at * hidden : (at + 1) * hidden, :] = turned[:hidden]


def small_results(index, small, feedforward_gain, attention_gain, query_gain, key_gain, stats):
    for at, to in enumerate((feedforward_gain, attention_gain)):
        line = jnp.concatenate([small[8 * at + row : 8 * at + row + 1, :] for row in range(8)], 1)
        shift = (line.shape[1] - index[2] * to.shape[0]) % line.shape[1]
        to[...] = pltpu.roll(line, shift, 1)[0, : to.shape[0]]
    query_gain[...] = small[16:17, :][0, :HD]
    key_gain[...] = pltpu.roll(small[16:17, :], HD, 1)[0, :HD]
    line = small[17:18, :]
    count = jnp.sum(jnp.where(lanes((1, 128)) == 4, line, 0.0))
    stats[...] = jnp.sqrt(line / (count * index[4].astype(F32)))[0, :4]


def unpack_rows(index, own, from_y, from_core, from_both, rows, block_rows):
    block = own.shape[0] // 2
    for at, part in enumerate((own, from_y, from_core, from_both)):
        to = pl.multiple_of(((index[0] ^ (2 * (at % 2) + at // 2)) & 3) * block, block)
        rows[pl.ds(to, block), :] = part[:block, :].astype(F32)
        block_rows[pl.ds(to, block), :] = part[block:, :]


def call(kernel, outs, args, scratch=(), limit=48, fetched=0, cost=0):
    vmem, hbm = pl.BlockSpec(memory_space=pltpu.VMEM), pl.BlockSpec(memory_space=pl.ANY)
    kinds = [
        pl.BlockSpec(memory_space=pltpu.SMEM)
        if arg.dtype == jnp.int32
        else hbm
        if fetched
        else vmem
        for arg in args
    ]
    scratch = [pltpu.VMEM(shape, kind) for shape, kind in scratch]
    if fetched:
        scratch += [pltpu.VMEM(arg.shape, arg.dtype) for arg in args[1 : 1 + fetched]]
        scratch += [pltpu.SemaphoreType.DMA((fetched + 4,))]
    return pl.pallas_call(
        kernel,
        out_shape=[jax.ShapeDtypeStruct(shape, kind) for shape, kind in outs],
        in_specs=kinds,
        out_specs=[vmem] * len(outs),
        scratch_shapes=scratch,
        compiler_params=pltpu.CompilerParams(vmem_limit_bytes=limit * 2**20),
        cost_estimate=pl.CostEstimate(flops=1000 + cost * 10**9, bytes_accessed=1000, transcendentals=0),
    )(*args)


def shards(
    hidden_in,
    lengths,
    positions,
    query_weight,
    key_weight,
    value_weight,
    output_weight,
    gate_weight,
    up_weight,
    down_weight,
    attention_gain,
    feedforward_gain,
    query_gain,
    key_gain,
    cotangent,
):
    ctx, why, core = lax.axis_index("ctx"), lax.axis_index("y"), lax.axis_index("core")
    local, width = hidden_in.shape[1:]
    block = local // 4
    every = 2 * local
    length = lengths[0]

    heads = query_weight.shape[1] // 2 // HD
    groups = key_weight.shape[1] // 2 // HD
    lane = 2 * HD
    wide = (heads + 2 * groups) * HD
    rows = query_weight.shape[0]
    hidden = gate_weight.shape[1] // 2
    main = hidden // 128 * 128
    assert hidden - main == HD and heads * HD == lane and groups == 1
    pack = 2 * hidden + main + lane
    own = ctx * 4 + why * 2 + core
    shard = lax.axis_index("fsdp")
    size = lax.axis_size("fsdp")
    index = jnp.stack([own, length, shard, ctx, jnp.int32(width)]).astype(jnp.int32)
    flag = length > 0

    attn_own, hidden_near, hidden_far = call(
        prelude,
        [((rows + 16, wide + lane), BF16)] + [((local // 2, width), BF16)] * 2,
        (
            index,
            query_weight,
            key_weight,
            value_weight,
            output_weight,
            attention_gain,
            feedforward_gain,
            hidden_in,
        ),
        limit=60,
        fetched=6,
    )
    hidden_other = swap(hidden_near, "ctx")
    if near_shards():
        attn_parts = direct([attn_own] * size)
    else:
        attn_parts = lax.all_gather(attn_own, "fsdp")
        gains = attn_parts[:, rows : rows + 8, :rows].astype(F32).transpose(1, 0, 2).reshape(8, -1)
        attn_parts = [attn_parts[:, :rows].reshape(-1, wide + lane), gains]

    def prepare(positions, gate_weight, up_weight, down_weight, cotangent):
        gu_own, down_own, *cotangent_rel = call(
            pack_feed_forward,
            [((rows, 2 * hidden), BF16), ((rows, main + lane), BF16)] + [((local // 2, width), BF16)] * 2,
            (index, gate_weight, up_weight, down_weight, cotangent),
            limit=60,
            fetched=3,
        )
        pieces = [
            lax.dynamic_slice_in_dim(positions[0], (2 * (why ^ yy) + (core ^ kk)) * block, block)
            for kk in range(2)
            for yy in range(2)
        ]
        places = jnp.concatenate(pieces).reshape(2, -1)
        places = jnp.stack([places, swap(places, "ctx")], 1).reshape(-1)
        freqs = rope_base ** (-2.0 * jnp.arange(HD // 2, dtype=F32) / HD)
        angles = places.astype(F32)[:, None] * jnp.tile(freqs, 4)[None, :]
        cosine = jnp.cos(angles)
        sine = jnp.sin(angles) * jnp.where(jnp.arange(lane) % HD < HD // 2, -1.0, 1.0)[None, :]
        return gu_own, down_own, cosine, sine, *cotangent_rel

    gu_own, down_own, cosine, sine, cotangent_near, cotangent_far = region(
        flag, prepare, positions, gate_weight, up_weight, down_weight, cotangent
    )
    attn_parts, gu_own, hidden_other, cotangent_near = together(attn_parts, gu_own, hidden_other, cotangent_near)
    gu_full = lax.all_gather(gu_own, "fsdp", axis=0, tiled=True)
    down_parts = [down_own]
    if near_shards():
        down_parts.append(onward(down_own))
    else:
        down_parts = [lax.all_gather(down_own, "fsdp", axis=0, tiled=True)]
    hidden_rel = (hidden_near, hidden_other, hidden_far, swap(hidden_other, "core"))
    cotangent_other = swap(cotangent_near, "ctx")
    query_row = jnp.tile(query_gain.astype(F32), 2)[None]
    key_row = jnp.concatenate([key_gain.astype(F32), jnp.ones((HD,), F32)])[None]

    def attend(hidden_rel, cosine, sine, query_row, key_row, attn_parts):
        attn_full, gains, near, far, unit, query, key, value, raw, mixed, mixed_rel, total = call(
            attention_forward,
            [((width, wide + lane), BF16), ((8, width), F32)]
            + [((every // 2, width), BF16)] * 2
            + [((every, width), BF16)]
            + [((every, lane), BF16)] * 3
            + [((every, 2 * lane), F32), ((every, lane), F32), ((every, lane), BF16), ((every, lane), F32)],
            (index, *hidden_rel, cosine, sine, query_row, key_row, *attn_parts),
            cost=8,
        )
        return near, far, gains, unit, mixed_rel, (attn_full, query, key, value, raw, mixed, total)

    near, far, gains, unit, mixed_rel, kept = region(
        flag, attend, hidden_rel, cosine, sine, query_row, key_row, attn_parts
    )
    kept = kept + (cosine, sine, query_row, key_row)
    near, down_parts = together(near, down_parts)
    if near_shards():
        down_parts.append(onward(down_parts[1]))
    quarter, whole = ((block, width // 2), BF16), ((block, width), F32)

    def add_attention(near, far, hidden_near, gains):
        return call(
            to_middle,
            [whole, ((block, lane), F32), quarter, quarter],
            (*sum_scatter(near, far), hidden_near, gains),
        )

    middle, inverse_two, *spread = region(flag, add_attention, near, far, hidden_near, gains)
    spread, cotangent_other, down_parts = together(spread, cotangent_other, down_parts)
    if near_shards():
        down_parts.append(onward(down_parts[2]))
    *unit_two, cotangent_last = region(flag, gather_plane, *spread, cotangent_other)
    if near_shards():
        unit_two, down_parts = together(unit_two, down_parts)

    cotangent_rel = (cotangent_near, cotangent_other, cotangent_far, cotangent_last)
    down_full, back = call(
        activated_gradient,
        [((width, main + lane), BF16), ((every, main + lane), F32)],
        (index, *cotangent_rel, *down_parts),
    )
    gu_full, back = together(gu_full, back)
    near, far, ff_grad, activated = call(
        feed_forward,
        [((every // 2, width), BF16)] * 2 + [((width, pack), BF16), ((every, main + lane), BF16)],
        (index, *unit_two, *cotangent_rel, back, gu_full),
        [((every, 2 * hidden), BF16)],
    )
    ff_grad, near = together(ff_grad, near)
    ff_share = lax.psum_scatter(ff_grad, "fsdp", scatter_dimension=0, tiled=True)

    def turn(near, far, middle, inverse_two, cotangent_near, gains, activated, down_full, unit, mixed_rel, kept):
        far, branch_parts = together(
            swap(far, "core"), call(down_product, [((every // 2, width), BF16)] * 2, (index, activated, down_full))
        )
        terms, branch_far = together(scatter_start(near, far), swap(branch_parts[1], "core"))
        second, middle_grad, left, right = call(
            to_middle_grad,
            [whole, whole, quarter, quarter],
            (index, *scatter_next(*terms), middle, inverse_two, cotangent_near, gains),
        )
        attention_grad = gather_end(left, swap(left, "ctx"), right, swap(right, "y"))
        attention_grad, branch_far = together(attention_grad, branch_far)
        branch = scatter_start(branch_parts[0], branch_far)
        near, far, back, head_sums = call(
            attention_backward,
            [((every // 2, width), BF16)] * 2 + [((every, 2 * lane), BF16), ((8, lane), F32)],
            (index, *attention_grad, *kept),
            [((every, lane), BF16)] + [((every, lane), F32)] * 3,
        )
        back, branch = together(back, branch)
        rows_of_branch = scatter_halves(*branch)
        back, rows_of_branch = together(back, rows_of_branch)
        branch = scatter_swap(*rows_of_branch)
        attn_grad, attention_sums = call(
            attention_weights,
            [((width, wide + lane), BF16), ((8, width), F32)],
            (index, unit, back, *attention_grad, mixed_rel, kept[0], gains),
        )
        attn_grad, branch = together(attn_grad, branch)
        return near, far, attn_grad, attention_sums, head_sums, branch, second, middle_grad

    near, far, attn_grad, attention_sums, head_sums, branch, second, middle_grad = region(
        flag,
        turn,
        near,
        far,
        middle,
        inverse_two,
        cotangent_near,
        gains,
        activated,
        down_full,
        unit,
        mixed_rel,
        kept,
    )
    attn_share = lax.psum_scatter(attn_grad, "fsdp", scatter_dimension=0, tiled=True)

    def sum_first(near, far, branch, middle, hidden_near, second, inverse, attention_sums, head_sums):
        far = swap(far, "core")
        branch, output = call(to_output, [whole, ((block, width), BF16)], (index, *branch, middle))
        (small,) = call(
            small_sums,
            [((24, lane), F32)],
            (index, hidden_near, middle, branch, second, inverse, attention_sums, head_sums),
        )
        far, small = together(far, small)
        terms = scatter_start(near, far)
        small = small + hop(small, "core")
        terms, more = together(terms, hop(small, "ctx"))
        small = small + more
        terms, more = together(scatter_next(*terms), hop(small, "y"))
        return terms, small + more, output

    pieces, small, output = region(
        flag,
        sum_first,
        near,
        far,
        branch,
        middle,
        hidden_near,
        second,
        inverse_two,
        attention_sums,
        head_sums,
    )
    pieces, ff_share = together(pieces, ff_share)
    ff_other = swap(ff_share, "ctx")

    def finish(pieces, middle_grad, hidden_near, gains, output, small):
        (own_rows,) = call(
            to_input_grad, [((2 * block, width), BF16)], (*pieces, middle_grad, hidden_near, gains, output)
        )
        rows_y, rows_core = swap(own_rows, "y"), swap(own_rows, "core")
        step = 1
        while step < size:
            small = small + hop(small, "fsdp", step)
            step *= 2
        rows_y, rows_core, small = together(rows_y, rows_core, small)
        return own_rows, rows_y, rows_core, small

    *three, small = region(flag, finish, pieces, middle_grad, hidden_near, gains, output, small)
    three, attn_share, ff_other = together(three, attn_share, ff_other)
    attn_other = swap(attn_share, "ctx")

    def unpack(index, three, ff_share, ff_other, small):
        last = swap(three[1], "core")
        ff_grads = call(
            unpack_feed_forward,
            [((rows, 2 * hidden), F32)] * 2 + [((2 * hidden, rows), F32)],
            (index, ff_share, ff_other),
        )
        results = call(
            small_results, [((rows,), F32)] * 2 + [((HD,), F32)] * 2 + [((4,), F32)], (index, small)
        )
        return together(last, ff_grads, results)

    last, ff_grads, results = region(flag, unpack, index, three, ff_share, ff_other, small)
    input_rows, block_rows = call(
        unpack_rows, [((local, width), F32), ((local, width), BF16)], (index, *three, last)
    )
    attn_other, input_rows = together(attn_other, input_rows)
    attn_grads = call(
        unpack_attention,
        [((rows, 2 * lane), F32)] + [((rows, lane), F32)] * 2 + [((2 * lane, rows), F32)],
        (index, attn_share, attn_other),
    )
    grads = (*attn_grads, *ff_grads)
    feedforward_share, attention_share, query_share, key_share, stats = results
    return (
        block_rows[None],
        input_rows[None],
        *grads,
        attention_share,
        feedforward_share,
        query_share,
        key_share,
        stats,
    )


def solution(mesh):
    fsdp, ctx, tp = (mesh.shape[axis] for axis in ("fsdp", "ctx", "tp"))
    assert ctx == 2 and tp == 4
    plane = Mesh(mesh.devices.reshape(fsdp, 2, 2, 2), ("fsdp", "ctx", "y", "core"))
    tp = ("y", "core")
    in_specs = (
        P("fsdp", "ctx", None),
        P("fsdp"),
        P("fsdp", "ctx"),
        P("fsdp", tp),
        P("fsdp", tp),
        P("fsdp", tp),
        P(tp, "fsdp"),
        P("fsdp", tp),
        P("fsdp", tp),
        P(tp, "fsdp"),
        P("fsdp"),
        P("fsdp"),
        P(),
        P(),
        P("fsdp", "ctx", None),
    )
    out_specs = (
        P("fsdp", "ctx", None),
        P("fsdp", "ctx", None),
        P("fsdp", tp),
        P("fsdp", tp),
        P("fsdp", tp),
        P(tp, "fsdp"),
        P("fsdp", tp),
        P("fsdp", tp),
        P(tp, "fsdp"),
        P("fsdp"),
        P("fsdp"),
        P(),
        P(),
        P(),
    )
    return jax.shard_map(shards, mesh=plane, in_specs=in_specs, out_specs=out_specs, check_vma=False)
```

profile of v0, /device:TPU:0, one launch (start us, length us, event | category | flops | bytes accessed | tf_op | source)
XLA Modules:
  0.0 243.8 jit_solution(6528342965228699045)
XLA Ops:
  13.8 3.6 %collective-permute-start.42 = (bf16[272,384]{1,0:T(8,128)(2,1)S(1)}, bf16[272,384]{1,0:T(8,128)(2,1)S(1)}, u32[]{:S(2)}, u32[]{:S(2)}) collective-permute-start(bf16[272,384]{1,0:T(8,128)(2,1)S(1)} %get-tuple-element.475), channel_id=1, source_target_pairs={{0,24},{8,16},{16,8},{24,0},{1,25},{9,17},{17,9},{25,1},{2,26},{10... | collective-permute-start | bytes 626696 | tf_op jit(solution)/shard_map/ppermute | solution.py:72
  18.2 9.6 %conditional.8 = (bf16[256,1152]{1,0:T(8,128)(2,1)S(1)}, bf16[256,640]{1,0:T(8,128)(2,1)S(1)}, f32[1024,128]{1,0:T(8,128)S(1)}, f32[1024,128]{1,0:T(8,128)S(1)},...) conditional(s32[]{:T(128)} %bitcast.30, () %tuple.97, (s32[5]{0:T(128)S(1)}, ...), branch_computations={%region_0.0_spmd, %region_1.2_spmd} | conditional | flops 267808 | bytes 3014720 | solution.py:88
  27.9 7.1 %collective-permute-done.41 = bf16[272,384]{1,0:T(8,128)(2,1)} collective-permute-done((bf16[272,384]{1,0:T(8,128)(2,1)S(1)}, bf16[272,384]{1,0:T(8,128)(2,1)}, u32[]{:S(2)}, u32[]{:S(2)}) %collective-permute-start.41) | collective-permute-done | bytes 208928 | tf_op jit(solution)/shard_map/ppermute | solution.py:72
  37.3 9.5 %conditional.9 = (bf16[512,1024]{1,0:T(8,128)(2,1)S(1)}, bf16[512,1024]{1,0:T(8,128)(2,1)S(1)}, f32[8,1024]{1,0:T(8,128)S(1)}, bf16[1024,1024]{1,0:T(8,128)(2,1)...) conditional(s32[]{:T(128)} %bitcast.30, () %tuple.96, ...), branch_computations={%region_2.3_spmd, %region_3.4_spmd} | conditional | flops 8000001024 | bytes 8159360 | solution.py:88
  38.2 8.6 %branch_1_fun.21 = (bf16[1024,384]{1,0:T(8,128)(2,1)}, f32[8,1024]{1,0:T(8,128)S(1)}, bf16[512,1024]{1,0:T(8,128)(2,1)S(1)}, bf16[512,1024]{1,0:T(8,128)(2,1)S(1...) custom-call(s32[5]{0:T(128)S(1)} %get-tuple-element.166.index, ...), custom_call_target="tpu_custom_call" | custom-call | flops 8000001024 | bytes 1000 | tf_op jit(solution)/shard_map/cond/branch_1_fun/pallas_call | solution.py:611
  47.8 19.0 %conditional.10 = ((f32[128,1024]{1,0:T(8,128)}, f32[128,128]{1,0:T(8,128)}, bf16[128,512]{1,0:T(8,128)(2,1)S(1)}, bf16[128,512]{1,0:T(8,128)(2,1)S(1)})) conditional(s32[]{:T(128)} %bitcast.30, () %tuple.95, (bf16[512,1024]{1,0:T(8,128)(2,1)S(1)}, bf16[512,1024]{1,0:T(8,128)(2,1)S(1)}, bf16[256,1024]{1,0:T(8,128)(2,1)S(1)}, ...), branch_computations={%region_4.5_spmd, %region_5.6_spmd} | conditional | flops 3000 | bytes 7343240 | solution.py:88
  52.5 6.7 %collective-permute-done.1.from_x = bf16[256,512]{1,0:T(8,128)(2,1)S(1)} collective-permute-done((bf16[256,512]{1,0:T(8,128)(2,1)S(1)}, bf16[256,512]{1,0:T(8,128)(2,1)S(1)}, u32[]{:S(2)}, u32[]{:S(2)}) %collective-permute-start.1) | collective-permute-done | bytes 262176 | tf_op jit(solution)/shard_map/cond/branch_1_fun/ppermute | solution.py:17
  70.2 20.8 %conditional.11 = (bf16[512,1024]{1,0:T(8,128)(2,1)}, bf16[512,1024]{1,0:T(8,128)(2,1)}, bf16[256,1024]{1,0:T(8,128)(2,1)}) conditional(s32[]{:T(128)} %bitcast.30, () %tuple.94, (bf16[128,512]{1,0:T(8,128)(2,1)S(1)}, bf16[256,1024]{1,0:T(8,128)(2,1)}, bf16[128,512]{1,0:T(8,128)(2,1)S(1)}) %tuple.104), branch_computations={%region_6.7_spmd, %region_7.8_spmd} | conditional | flops 4456448 | bytes 13107464 | solution.py:88
  80.0 5.7 %collective-permute-done.22 = bf16[2,128,512]{2,1,0:T(8,128)(2,1)S(1)} collective-permute-done((bf16[2,128,512]{2,1,0:T(8,128)(2,1)S(1)}, bf16[2,128,512]{2,1,0:T(8,128)(2,1)S(1)}, u32[]{:S(2)}, u32[]{:S(2)}) %collective-permute-start.22) | collective-permute-done | bytes 262176 | tf_op jit(solution)/shard_map/cond/branch_1_fun/ppermute | solution.py:17
  92.8 3.5 %shard_map.260 = (bf16[1024,640]{1,0:T(8,128)(2,1)}, f32[1024,640]{1,0:T(8,128)S(1)}) custom-call(s32[5]{0:T(128)S(1)} %stack.93.index, bf16[256,1024]{1,0:T(8,128)(2,1)} %copy-done.6, bf16[256,1024]{1,0:T(8,128)(2,1)} %collective-permute-done.46.b1, bf16[256,1024]{1,0:T(8,128)(2,1)} %get-tuple-element.499.b2, bf16[256,1024]{1,0:T(8,128)(2,1)} %get-tuple-element.500.b3, ...), custom_call_target="tpu_custom_call" | custom-call | flops 1000 | bytes 1000 | tf_op jit(solution)/shard_map/pallas_call | solution.py:611
  96.3 3.4 %all-gather.2.cloned.1.call-done.gu_w = bf16[1024,1152]{1,0:T(8,128)(2,1)} async-done(((bf16[256,1152]{1,0:T(8,128)(2,1)}), bf16[1024,1152]{1,0:T(8,128)(2,1)}) %all-gather.2.cloned.1.call-update) | async-done | bytes 2359312 | tf_op jit(solution)/shard_map/all_gather | solution.py:709
  101.4 14.5 %shard_map.261 = (bf16[512,1024]{1,0:T(8,128)(2,1)}, bf16[512,1024]{1,0:T(8,128)(2,1)}, bf16[1024,1792]{1,0:T(8,128)(2,1)}, bf16[1024,640]{1,0:T(8,128)(2,1)}) custom-call(s32[5]{0:T(128)S(1)} %stack.93.index, bf16[512,1024]{1,0:T(8,128)(2,1)} %get-tuple-element.497.x_low, bf16[512,1024]{1,0:T(8,128)(2,1)} %get-tuple-element.498.x_high, ...), custom_call_target="tpu_custom_call" | custom-call | flops 1000 | bytes 1000 | tf_op jit(solution)/shard_map/pallas_call | solution.py:611
  117.8 68.0 %conditional.12 = (bf16[512,1024]{1,0:T(8,128)(2,1)}, bf16[512,1024]{1,0:T(8,128)(2,1)}, bf16[1024,384]{1,0:T(8,128)(2,1)}, f32[8,1024]{1,0:T(8,128)S(1)}, f32[8...) conditional(s32[]{:T(128)} %bitcast.30, () %tuple.93, ...), branch_computations={%region_8.9_spmd, %region_9.10_spmd} | conditional | flops 4464448 | bytes 45621996 | solution.py:88
  127.1 3.6 %branch_1_fun.25 = (bf16[512,1024]{1,0:T(8,128)(2,1)S(1)}, bf16[512,1024]{1,0:T(8,128)(2,1)S(1)}) custom-call(s32[5]{0:T(128)S(1)} %get-tuple-element.209.index, bf16[1024,640]{1,0:T(8,128)(2,1)} %get-tuple-element.212.activated, bf16[1024,640]{1,0:T(8,128)(2,1)} %get-tuple-element.213.down_w), custom_call_target="tpu_custom_call" | custom-call | flops 1000 | bytes 1000 | tf_op jit(solution)/shard_map/cond/branch_1_fun/pallas_call | solution.py:611
  133.4 6.4 %collective-permute-done.26.from_x = bf16[256,512]{1,0:T(8,128)(2,1)S(1)} collective-permute-done((bf16[256,512]{1,0:T(8,128)(2,1)S(1)}, bf16[256,512]{1,0:T(8,128)(2,1)S(1)}, u32[]{:S(2)}, u32[]{:S(2)}) %collective-permute-start.26) | collective-permute-done | bytes 262176 | tf_op jit(solution)/shard_map/cond/branch_1_fun/ppermute | solution.py:17
  156.3 4.1 %collective-permute-done.32 = bf16[2,128,512]{2,1,0:T(8,128)(2,1)S(1)} collective-permute-done((bf16[2,128,512]{2,1,0:T(8,128)(2,1)S(1)}, bf16[2,128,512]{2,1,0:T(8,128)(2,1)S(1)}, u32[]{:S(2)}, u32[]{:S(2)}) %collective-permute-start.32) | collective-permute-done | bytes 262176 | tf_op jit(solution)/shard_map/cond/branch_1_fun/ppermute | solution.py:17
  166.7 11.1 %branch_1_fun.29 = (bf16[512,1024]{1,0:T(8,128)(2,1)}, bf16[512,1024]{1,0:T(8,128)(2,1)}, bf16[1024,256]{1,0:T(8,128)(2,1)S(1)}, f32[8,128]{1,0:T(8,128)S(1)}) custom-call(s32[5]{0:T(128)S(1)} %get-tuple-element.209.index, bf16[512,1024]{1,0:T(8,128)(2,1)S(1)} %bitcast.48, bf16[512,1024]{1,0:T(8,128)(2,1)S(1)} %collective-permute-done.35.a_high, ...), custom_call_target="tpu_custom_call" | custom-call | flops 1000 | bytes 1000 | tf_op jit(solution)/shard_map/cond/branch_1_fun/pallas_call | solution.py:611
  182.0 3.6 %branch_1_fun.32 = (bf16[1024,384]{1,0:T(8,128)(2,1)}, f32[8,1024]{1,0:T(8,128)S(1)}) custom-call(s32[5]{0:T(128)S(1)} %get-tuple-element.209.index, bf16[1024,1024]{1,0:T(8,128)(2,1)S(1)} %get-tuple-element.252.unit, bf16[1024,256]{1,0:T(8,128)(2,1)S(1)} %get-tuple-element.269.back, bf16[512,1024]{1,0:T(8,128)(2,1)S(1)} %bitcast.49, ...), custom_call_target="tpu_custom_call" | custom-call | flops 1000 | bytes 1000 | tf_op jit(solution)/shard_map/cond/branch_1_fun/pallas_call | solution.py:611
  185.9 20.1 %conditional.13 = (f32[128,512]{1,0:T(8,128)S(1)}, bf16[128,512]{1,0:T(8,128)(2,1)}, f32[128,512]{1,0:T(8,128)S(1)}, bf16[128,512]{1,0:T(8,128)(2,1)}, f32[24,12...) conditional(s32[]{:T(128)} %bitcast.30, () %tuple.92, (bf16[512,1024]{1,0:T(8,128)(2,1)}, s32[5]{0:T(128)S(1)}, ...), branch_computations={%region_10.11_spmd, %region_11.12_spmd} | conditional | flops 13216 | bytes 7602448 | solution.py:88
  194.1 5.2 %collective-permute-done.9 = f32[24,128]{1,0:T(8,128)S(1)} collective-permute-done((f32[24,128]{1,0:T(8,128)S(1)}, f32[24,128]{1,0:T(8,128)S(1)}, u32[]{:S(2)}, u32[]{:S(2)}) %collective-permute-start.9) | collective-permute-done | bytes 12320 | tf_op jit(solution)/shard_map/cond/branch_1_fun/ppermute | solution.py:22
  206.7 17.1 %conditional.14 = (bf16[256,1024]{1,0:T(8,128)(2,1)}, bf16[256,1024]{1,0:T(8,128)(2,1)}, bf16[256,1024]{1,0:T(8,128)(2,1)}, f32[24,128]{1,0:T(8,128)S(1)}) conditional(s32[]{:T(128)} %bitcast.30, () %tuple.91, (f32[128,512]{1,0:T(8,128)S(1)}, bf16[128,512]{1,0:T(8,128)(2,1)}, f32[128,512]{1,0:T(8,128)S(1)}, bf16[128,512]{1,0:T(8,128)(2,1)}, ...), branch_computations={%region_13.14_spmd, %region_14.15_spmd} | conditional | flops 7144 | bytes 4367528 | solution.py:88
  219.4 4.4 %collective-permute-done.13 = bf16[256,1024]{1,0:T(8,128)(2,1)} collective-permute-done((bf16[256,1024]{1,0:T(8,128)(2,1)}, bf16[256,1024]{1,0:T(8,128)(2,1)}, u32[]{:S(2)}, u32[]{:S(2)}) %collective-permute-start.13) | collective-permute-done | bytes 524320 | tf_op jit(solution)/shard_map/cond/branch_1_fun/ppermute | solution.py:17
  228.0 4.0 %conditional.15 = (bf16[256,1024]{1,0:T(8,128)(2,1)}, f32[256,1152]{1,0:T(8,128)}, f32[256,1152]{1,0:T(8,128)}, f32[1152,256]{1,0:T(8,128)}, f32[256]{0:T(256)},...) conditional(s32[]{:T(128)} %bitcast.30, () %tuple.113, (bf16[256,1024]{1,0:T(8,128)(2,1)}, ...), branch_computations={%region_16.17_spmd, %region_17.18_spmd} | conditional | flops 2000 | bytes 4065914 | solution.py:88
  232.0 3.4 %shard_map.262 = (f32[512,1024]{1,0:T(8,128)}, bf16[512,1024]{1,0:T(8,128)(2,1)}) custom-call(s32[5]{0:T(128)S(1)} %stack.93.index, bf16[256,1024]{1,0:T(8,128)(2,1)} %get-tuple-element.552.own, bf16[256,1024]{1,0:T(8,128)(2,1)} %get-tuple-element.553.from_y, bf16[256,1024]{1,0:T(8,128)(2,1)} %get-tuple-element.554.from_core, ...), custom_call_target="tpu_custom_call" | custom-call | flops 1000 | bytes 1000 | tf_op jit(solution)/shard_map/pallas_call | solution.py:611
  (206 shorter events, 124.1 us)
Async XLA Ops:
  7.2 92.6 %all-gather.2.cloned.1.call-start = ((), (), s32[]{:S(2)}) async-start(), calls=%async_computation.2 | async-start | bytes 2949120 | tf_op jit(solution)/shard_map/all_gather | solution.py:709
  10.8 24.2 %collective-permute-start.43 = (bf16[256,1024]{1,0:T(8,128)(2,1)S(1)}, bf16[256,1024]{1,0:T(8,128)(2,1)}, u32[]{:S(2)}, u32[]{:S(2)}) collective-permute-start(bf16[256,1024]{1,0:T(8,128)(2,1)S(1)} %get-tuple-element.467), channel_id=1, source_target_pairs={{0,4},{4,0},{1,5},{5,1},{2,6},{6,2},{3,7},{7,3},{8,12},{12,8},{9,1... | collective-permute-start | bytes 1572872 | tf_op jit(solution)/shard_map/ppermute | solution.py:17
  13.8 14.0 %collective-permute-start.42 = (bf16[272,384]{1,0:T(8,128)(2,1)S(1)}, bf16[272,384]{1,0:T(8,128)(2,1)S(1)}, u32[]{:S(2)}, u32[]{:S(2)}) collective-permute-start(bf16[272,384]{1,0:T(8,128)(2,1)S(1)} %get-tuple-element.475), channel_id=1, source_target_pairs={{0,24},{8,16},{16,8},{24,0},{1,25},{9,17},{17,9},{25,1},{2,26},{10... | collective-permute-start | bytes 626696 | tf_op jit(solution)/shard_map/ppermute | solution.py:72
  17.4 17.6 %collective-permute-start.41 = (bf16[272,384]{1,0:T(8,128)(2,1)S(1)}, bf16[272,384]{1,0:T(8,128)(2,1)}, u32[]{:S(2)}, u32[]{:S(2)}) collective-permute-start(bf16[272,384]{1,0:T(8,128)(2,1)S(1)} %get-tuple-element.475), channel_id=1, source_target_pairs={{0,16},{8,24},{16,0},{24,8},{1,17},{9,25},{17,1},{25,9},{2,18},{10... | collective-permute-start | bytes 626696 | tf_op jit(solution)/shard_map/ppermute | solution.py:72
  17.4 17.6 %collective-permute-start.40 = (bf16[272,384]{1,0:T(8,128)(2,1)S(1)}, bf16[272,384]{1,0:T(8,128)(2,1)}, u32[]{:S(2)}, u32[]{:S(2)}) collective-permute-start(bf16[272,384]{1,0:T(8,128)(2,1)S(1)} %get-tuple-element.475), channel_id=1, source_target_pairs={{0,8},{8,0},{16,24},{24,16},{1,9},{9,1},{17,25},{25,17},{2,10},{10... | collective-permute-start | bytes 626696 | tf_op jit(solution)/shard_map/ppermute | solution.py:72
  35.0 170.9 %reduce-scatter.3.cloned.1.call-start = ((), (), s32[]{:S(2)}) async-start(), calls=%async_computation.3 | async-start | bytes 4587520 | tf_op jit(solution)/shard_map/reduce_scatter | solution.py:771
  35.2 12.6 %collective-permute-start.45 = (bf16[256,640]{1,0:T(8,128)(2,1)S(1)}, bf16[256,640]{1,0:T(8,128)(2,1)S(1)}, u32[]{:S(2)}, u32[]{:S(2)}) collective-permute-start(bf16[256,640]{1,0:T(8,128)(2,1)S(1)} %get-tuple-element.502.rest_0_), channel_id=1, source_target_pairs={{0,8},{8,16},{16,24},{24,0},{1,9},{9,17},{17,25},{25,1},{2,10},{10... | collective-permute-start | bytes 983048 | tf_op jit(solution)/shard_map/ppermute | solution.py:79
  35.2 31.6 %collective-permute-start.46 = (bf16[256,1024]{1,0:T(8,128)(2,1)S(1)}, bf16[256,1024]{1,0:T(8,128)(2,1)}, u32[]{:S(2)}, u32[]{:S(2)}) collective-permute-start(bf16[256,1024]{1,0:T(8,128)(2,1)S(1)} %get-tuple-element.486.b0), channel_id=1, source_target_pairs={{0,4},{4,0},{1,5},{5,1},{2,6},{6,2},{3,7},{7,3},{8,12},{12,8},{9,1... | collective-permute-start | bytes 1572872 | tf_op jit(solution)/shard_map/ppermute | solution.py:17
  47.8 19.0 %collective-permute-start.47 = (bf16[256,640]{1,0:T(8,128)(2,1)S(1)}, bf16[256,640]{1,0:T(8,128)(2,1)S(1)}, u32[]{:S(2)}, u32[]{:S(2)}) collective-permute-start(bf16[256,640]{1,0:T(8,128)(2,1)S(1)} %collective-permute-done.45.rest_1_), channel_id=1, source_target_pairs={{0,8},{8,16},{16,24},{24,0},{1,9},{9,17},{17,25},{25,1},{2,10},{10... | collective-permute-start | bytes 983048 | tf_op jit(solution)/shard_map/ppermute | solution.py:79
  50.7 8.4 %collective-permute-start.1 = (bf16[256,512]{1,0:T(8,128)(2,1)S(1)}, bf16[256,512]{1,0:T(8,128)(2,1)S(1)}, u32[]{:S(2)}, u32[]{:S(2)}) collective-permute-start(bf16[256,512]{1,0:T(8,128)(2,1)S(1)} %get-tuple-element.194), channel_id=1, source_target_pairs={{0,4},{4,0},{1,5},{5,1},{2,6},{6,2},{3,7},{7,3},{8,12},{12,8},{9,1... | collective-permute-start | bytes 786440 | tf_op jit(solution)/shard_map/cond/branch_1_fun/ppermute | solution.py:17
  50.8 8.4 %collective-permute-start.2 = (bf16[256,512]{1,0:T(8,128)(2,1)S(1)}, bf16[256,512]{1,0:T(8,128)(2,1)S(1)}, u32[]{:S(2)}, u32[]{:S(2)}) collective-permute-start(bf16[256,512]{1,0:T(8,128)(2,1)S(1)} %get-tuple-element.196), channel_id=1, source_target_pairs={{0,2},{2,0},{1,3},{3,1},{4,6},{6,4},{5,7},{7,5},{8,10},{10,8},{9,1... | collective-permute-start | bytes 786440 | tf_op jit(solution)/shard_map/cond/branch_1_fun/ppermute | solution.py:17
  66.9 24.2 %collective-permute-start.48 = (bf16[256,640]{1,0:T(8,128)(2,1)S(1)}, bf16[256,640]{1,0:T(8,128)(2,1)S(1)}, u32[]{:S(2)}, u32[]{:S(2)}) collective-permute-start(bf16[256,640]{1,0:T(8,128)(2,1)S(1)} %collective-permute-done.47.rest_2_), channel_id=1, source_target_pairs={{0,8},{8,16},{16,24},{24,0},{1,9},{9,17},{17,25},{25,1},{2,10},{10... | collective-permute-start | bytes 983048 | tf_op jit(solution)/shard_map/ppermute | solution.py:79
  116.0 107.9 %reduce-scatter.5.cloned.1.call-start = ((), (), s32[]{:S(2)}) async-start(), calls=%async_computation.4 | async-start | bytes 983040 | tf_op jit(solution)/shard_map/reduce_scatter | solution.py:819
  130.7 9.2 %collective-permute-start.28 = (bf16[512,1024]{1,0:T(8,128)(2,1)S(1)}, bf16[512,1024]{1,0:T(8,128)(2,1)S(1)}, u32[]{:S(2)}, u32[]{:S(2)}) collective-permute-start(bf16[512,1024]{1,0:T(8,128)(2,1)S(1)} %get-tuple-element.221), channel_id=1, source_target_pairs={{0,1},{1,0},{2,3},{3,2},{4,5},{5,4},{6,7},{7,6},{8,9},{9,8},{10,11... | collective-permute-start | bytes 3145736 | tf_op jit(solution)/shard_map/cond/branch_1_fun/ppermute | solution.py:17
  131.4 8.4 %collective-permute-start.26 = (bf16[256,512]{1,0:T(8,128)(2,1)S(1)}, bf16[256,512]{1,0:T(8,128)(2,1)S(1)}, u32[]{:S(2)}, u32[]{:S(2)}) collective-permute-start(bf16[256,512]{1,0:T(8,128)(2,1)S(1)} %get-tuple-element.218), channel_id=1, source_target_pairs={{0,4},{4,0},{1,5},{5,1},{2,6},{6,2},{3,7},{7,3},{8,12},{12,8},{9,1... | collective-permute-start | bytes 786440 | tf_op jit(solution)/shard_map/cond/branch_1_fun/ppermute | solution.py:17
  131.9 8.0 %collective-permute-start.27 = (bf16[256,512]{1,0:T(8,128)(2,1)S(1)}, bf16[256,512]{1,0:T(8,128)(2,1)S(1)}, u32[]{:S(2)}, u32[]{:S(2)}) collective-permute-start(bf16[256,512]{1,0:T(8,128)(2,1)S(1)} %get-tuple-element.220), channel_id=1, source_target_pairs={{0,2},{2,0},{1,3},{3,1},{4,6},{6,4},{5,7},{7,5},{8,10},{10,8},{9,1... | collective-permute-start | bytes 786440 | tf_op jit(solution)/shard_map/cond/branch_1_fun/ppermute | solution.py:17
  165.8 12.0 %collective-permute-start.36 = (bf16[256,512]{1,0:T(8,128)(2,1)S(1)}, bf16[256,512]{1,0:T(8,128)(2,1)S(1)}, u32[]{:S(2)}, u32[]{:S(2)}) collective-permute-start(bf16[256,512]{1,0:T(8,128)(2,1)S(1)} %get-tuple-element.257), channel_id=1, source_target_pairs={{0,4},{4,0},{1,5},{5,1},{2,6},{6,2},{3,7},{7,3},{8,12},{12,8},{9,1... | collective-permute-start | bytes 786440 | tf_op jit(solution)/shard_map/cond/branch_1_fun/ppermute | solution.py:17
  165.9 11.9 %collective-permute-start.37 = (bf16[256,512]{1,0:T(8,128)(2,1)S(1)}, bf16[256,512]{1,0:T(8,128)(2,1)S(1)}, u32[]{:S(2)}, u32[]{:S(2)}) collective-permute-start(bf16[256,512]{1,0:T(8,128)(2,1)S(1)} %get-tuple-element.259), channel_id=1, source_target_pairs={{0,2},{2,0},{1,3},{3,1},{4,6},{6,4},{5,7},{7,5},{8,10},{10,8},{9,1... | collective-permute-start | bytes 786440 | tf_op jit(solution)/shard_map/cond/branch_1_fun/ppermute | solution.py:17
  190.3 9.0 %collective-permute-start.6 = (bf16[256,512]{1,0:T(8,128)(2,1)S(1)}, bf16[256,512]{1,0:T(8,128)(2,1)S(1)}, u32[]{:S(2)}, u32[]{:S(2)}) collective-permute-start(bf16[256,512]{1,0:T(8,128)(2,1)S(1)} %get-tuple-element.301), channel_id=1, source_target_pairs={{0,4},{4,0},{1,5},{5,1},{2,6},{6,2},{3,7},{7,3},{8,12},{12,8},{9,1... | collective-permute-start | bytes 786440 | tf_op jit(solution)/shard_map/cond/branch_1_fun/ppermute | solution.py:17
  191.8 8.4 %collective-permute-start.7 = (bf16[256,512]{1,0:T(8,128)(2,1)S(1)}, bf16[256,512]{1,0:T(8,128)(2,1)S(1)}, u32[]{:S(2)}, u32[]{:S(2)}) collective-permute-start(bf16[256,512]{1,0:T(8,128)(2,1)S(1)} %get-tuple-element.303), channel_id=1, source_target_pairs={{0,2},{2,0},{1,3},{3,1},{4,6},{6,4},{5,7},{7,5},{8,10},{10,8},{9,1... | collective-permute-start | bytes 786440 | tf_op jit(solution)/shard_map/cond/branch_1_fun/ppermute | solution.py:17
  206.0 20.9 %collective-permute-start.49 = (bf16[256,1792]{1,0:T(8,128)(2,1)}, bf16[256,1792]{1,0:T(8,128)(2,1)S(1)}, u32[]{:S(2)}, u32[]{:S(2)}) collective-permute-start(bf16[256,1792]{1,0:T(8,128)(2,1)} %reduce-scatter.3.cloned.1.call-done), channel_id=1, source_target_pairs={{0,4},{4,0},{1,5},{5,1},{2,6},{6,2},{3,7},{7,3},{8,12},{12,8},{9,1... | collective-permute-start | bytes 2752520 | tf_op jit(solution)/shard_map/ppermute | solution.py:17
  209.2 10.2 %collective-permute-start.14 = (bf16[256,1024]{1,0:T(8,128)(2,1)}, bf16[256,1024]{1,0:T(8,128)(2,1)}, u32[]{:S(2)}, u32[]{:S(2)}) collective-permute-start(bf16[256,1024]{1,0:T(8,128)(2,1)} %branch_1_fun.37), channel_id=1, source_target_pairs={{0,1},{1,0},{2,3},{3,2},{4,5},{5,4},{6,7},{7,6},{8,9},{9,8},{10,11... | collective-permute-start | bytes 1572872 | tf_op jit(solution)/shard_map/cond/branch_1_fun/ppermute | solution.py:17
  209.2 14.7 %collective-permute-start.13 = (bf16[256,1024]{1,0:T(8,128)(2,1)}, bf16[256,1024]{1,0:T(8,128)(2,1)}, u32[]{:S(2)}, u32[]{:S(2)}) collective-permute-start(bf16[256,1024]{1,0:T(8,128)(2,1)} %branch_1_fun.37), channel_id=1, source_target_pairs={{0,2},{2,0},{1,3},{3,1},{4,6},{6,4},{5,7},{7,5},{8,10},{10,8},{9,1... | collective-permute-start | bytes 1572872 | tf_op jit(solution)/shard_map/cond/branch_1_fun/ppermute | solution.py:17
  226.8 8.6 %collective-permute-start.50 = (bf16[256,384]{1,0:T(8,128)(2,1)}, bf16[256,384]{1,0:T(8,128)(2,1)S(1)}, u32[]{:S(2)}, u32[]{:S(2)}) collective-permute-start(bf16[256,384]{1,0:T(8,128)(2,1)} %reduce-scatter.5.cloned.1.call-done.mine), channel_id=1, source_target_pairs={{0,4},{4,0},{1,5},{5,1},{2,6},{6,2},{3,7},{7,3},{8,12},{12,8},{9,1... | collective-permute-start | bytes 589832 | tf_op jit(solution)/shard_map/ppermute | solution.py:17
  (60 other events, 351.6 us)
Sparse Core Ops, SparseCore 0:
  35.2 64.5 all-gather.1
  116.1 69.7 reduce-scatter.2
  188.2 23.6 reduce-scatter.4
where the time goes:
time: 248 us; the launch traced here: 244 us
  waiting for transfers between devices  89 us (36%)
  Pallas kernels  71.2 us (29%)
  starting transfers between devices  48.4 us (20%)
  between operations  14.8 us (6%)
  loops' own time  9.91 us (4%)
  local copies, waits for them, and re-layouts  7.15 us (3%)
  other arithmetic  3.35 us (1%)
    pallas_call x25, Pallas kernels, call(): pl.pallas_call(kernel, out_shape=[jax.ShapeDtypeStruct(shape, kind) for s...  71.2 us
    ppermute x40, waiting for transfers between devices, swap(): return lax.ppermute(value, axis, [(0, 1), (1, 0)])  64.2 us
    ppermute x40, starting transfers between devices, swap(): return lax.ppermute(value, axis, [(0, 1), (1, 0)])  33.9 us
    ppermute x5, waiting for transfers between devices, hop(): return lax.ppermute(value, axis, [(i, i ^ step) for i in range(size)])  13.1 us
    another operation x8, loops' own time, region(): lax.cond(flag, work, lambda *_: jax.tree.map(lambda x: jnp.zeros(x.shape,...  9.91 us
    ppermute x3, waiting for transfers between devices, direct(): lax.ppermute(piece, 'fsdp', [(i, i ^ step) for i in range(size)])  7.13 us
    ppermute x5, starting transfers between devices, hop(): return lax.ppermute(value, axis, [(i, i ^ step) for i in range(size)])  6.61 us
    unnamed x36, local copies, waits for them, and re-layouts  5.2 us
  transfers between devices with their start and end apart: 54, of which 33 were waited for; matrix products, arithmetic and copies ran while one was open for 2% of the time, Pallas kernels for 21%

commit v1 on v0

--- a/solution.py
+++ b/solution.py
@@ -287,33 +287,40 @@
     main = gate_up.shape[1] // 2 // 128 * 128
     both = 2 * main
     wide = both + 128
-    low = lanes((four, 128)) < HD
-    row = lax.broadcasted_iota(jnp.int32, (four, 1), 0)
+    low = lanes((pair, 128)) < HD
+    row = lax.broadcasted_iota(jnp.int32, (pair, 1), 0)
     bs = (b0, b1, b2, b3)
     for kk, (x, to) in enumerate(((x_low, second_low), (x_high, second_high))):
-        here = slice(kk * four, (kk + 1) * four)
-        start = own ^ (kk + jnp.where(row >= pair, 4, 0) + jnp.where(row % pair >= block, 2, 0))
-        ok = start * block + row % block < length
-        gu = nn(x[...], gu_w[...])
-        back = back_all[here, :]
-        tail = gu[:, both:]
-        gate = jnp.concatenate([gu[:, :main], tail], 1)
-        upper = jnp.concatenate([gu[:, main:both], pltpu.roll(tail, HD, 1)], 1)
-        sigmoid = 1.0 / (1.0 + jnp.exp(-gate))
-        silu = gate * sigmoid
-        act = jnp.where(ok, silu * upper, 0.0)
-        gate_back = back * upper * (sigmoid + silu * (1.0 - sigmoid))
-        upper_back = back * silu
-        activated[here, :main] = act[:, :main].astype(BF16)
-        activated[here, main:] = jnp.where(low, act[:, main:], 0.0).astype(BF16)
-        mix = jnp.where(low, gate_back[:, main:], pltpu.roll(upper_back[:, main:], HD, 1))
-        gate_up[here, :main] = gate_back[:, :main].astype(BF16)
-        gate_up[here, main:both] = upper_back[:, :main].astype(BF16)
-        gate_up[here, both:] = mix.astype(BF16)
-        to[...] = nt(gate_up[here, :], gu_w[...]).astype(BF16)
-    step = width // 2
-    for row in range(0, width, step):
-        here = slice(row, row + step)
+
+        @pl.loop(0, 2)
+        def _(xx, kk=kk, x=x, to=to):
+            some = pl.ds(pl.multiple_of(xx * pair, pair), pair)
+            here = pl.ds(pl.multiple_of(kk * four + xx * pair, pair), pair)
+            start = own ^ (kk + 4 * xx + jnp.where(row >= block, 2, 0))
+            ok = start * block + row % block < length
+            gu = nn(x[some, :], gu_w[...])
+            back = back_all[here, :]
+            tail = gu[:, both:]
+            gate = jnp.concatenate([gu[:, :main], tail], 1)
+            upper = jnp.concatenate([gu[:, main:both], pltpu.roll(tail, HD, 1)], 1)
+            sigmoid = 1.0 / (1.0 + jnp.exp(-gate))
+            silu = gate * sigmoid
+            act = jnp.where(ok, silu * upper, 0.0)
+            gate_back = back * upper * (sigmoid + silu * (1.0 - sigmoid))
+            upper_back = back * silu
+            activated[here, :main] = act[:, :main].astype(BF16)
+            activated[here, main:] = jnp.where(low, act[:, main:], 0.0).astype(BF16)
+            mix = jnp.where(low, gate_back[:, main:], pltpu.roll(upper_back[:, main:], HD, 1))
+            gate_up[here, :main] = gate_back[:, :main].astype(BF16)
+            gate_up[here, main:both] = upper_back[:, :main].astype(BF16)
+            gate_up[here, both:] = mix.astype(BF16)
+            to[some, :] = nt(gate_up[here, :], gu_w[...]).astype(BF16)
+
+    step = 256
+
+    @pl.loop(0, width // step)
+    def _(at):
+        here = pl.ds(pl.multiple_of(at * step, step), step)
         out = tn(x_low[:, here], gate_up[:four, :]) + tn(x_high[:, here], gate_up[four:, :])
         grad[here, :wide] = out.astype(BF16)
         out = tn(b0[:, here], activated[:pair, :])
@@ -324,8 +331,13 @@
 
 def down_product(index, activated, down_w, branch_low, branch_high):
     four = branch_low.shape[0]
-    branch_low[...] = nt(activated[:four, :], down_w[...]).astype(BF16)
-    branch_high[...] = nt(activated[four:, :], down_w[...]).astype(BF16)
+    for at, branch in ((0, branch_low), (four, branch_high)):
+
+        @pl.loop(0, 2)
+        def _(xx, at=at, branch=branch):
+            here = pl.ds(pl.multiple_of(at + xx * (four // 2), four // 2), four // 2)
+            some = pl.ds(pl.multiple_of(xx * (four // 2), four // 2), four // 2)
+            branch[some, :] = nt(activated[here, :], down_w[...]).astype(BF16)
 
 
 def split_sum(near, far, left_low, right_low, left, right):

time: 248 us -> 236 us (0.952); the launches traced: 244 us -> 236 us
  loops' own time: 9.91 us -> 0.34 us
    another operation x8, loops' own time: 9.91 us -> 0.34 us  [region(): lax.cond(flag, work, lambda *_: jax.tree.map(lambda x: jnp.zeros(x.shape,...]
  transfers between devices with their start and end apart: 54 -> 54, of which waited for: 33 -> 33; matrix products, arithmetic and copies ran while one was open for 2% -> 2% of each run, Pallas kernels for 21% -> 22%
where the time goes in v1:
time: 236 us
  waiting for transfers between devices  89.5 us (38%)
  Pallas kernels  73 us (31%)
  starting transfers between devices  47.7 us (20%)
  between operations  14.6 us (6%)
  local copies, waits for them, and re-layouts  7.15 us (3%)
  other arithmetic  3.35 us (1%)
    pallas_call x25, Pallas kernels, call(): pl.pallas_call(kernel, out_shape=[jax.ShapeDtypeStruct(shape, kind) for s...  73 us
    ppermute x40, waiting for transfers between devices, swap(): return lax.ppermute(value, axis, [(0, 1), (1, 0)])  64.2 us
    ppermute x40, starting transfers between devices, swap(): return lax.ppermute(value, axis, [(0, 1), (1, 0)])  33.4 us
    ppermute x5, waiting for transfers between devices, hop(): return lax.ppermute(value, axis, [(i, i ^ step) for i in range(size)])  13.4 us
    ppermute x3, waiting for transfers between devices, direct(): lax.ppermute(piece, 'fsdp', [(i, i ^ step) for i in range(size)])  7.13 us
    ppermute x5, starting transfers between devices, hop(): return lax.ppermute(value, axis, [(i, i ^ step) for i in range(size)])  6.36 us
    unnamed x36, local copies, waits for them, and re-layouts  5.2 us
  transfers between devices with their start and end apart: 54, of which 33 were waited for; matrix products, arithmetic and copies ran while one was open for 2% of the time, Pallas kernels for 22%

profile of v1, /device:TPU:0, one launch (start us, length us, event | category | flops | bytes accessed | tf_op | source)
XLA Modules:
  0.0 235.7 jit_solution(15972787351737903802)
XLA Ops:
  13.8 3.6 %collective-permute-start.42 = (bf16[272,384]{1,0:T(8,128)(2,1)S(1)}, bf16[272,384]{1,0:T(8,128)(2,1)S(1)}, u32[]{:S(2)}, u32[]{:S(2)}) collective-permute-start(bf16[272,384]{1,0:T(8,128)(2,1)S(1)} %get-tuple-element.475), channel_id=1, source_target_pairs={{0,24},{8,16},{16,8},{24,0},{1,25},{9,17},{17,9},{25,1},{2,26},{10... | collective-permute-start | bytes 626696 | tf_op jit(solution)/shard_map/ppermute | solution.py:72
  18.2 9.6 %conditional.8 = (bf16[256,1152]{1,0:T(8,128)(2,1)S(1)}, bf16[256,640]{1,0:T(8,128)(2,1)S(1)}, f32[1024,128]{1,0:T(8,128)S(1)}, f32[1024,128]{1,0:T(8,128)S(1)},...) conditional(s32[]{:T(128)} %bitcast.30, () %tuple.97, (s32[5]{0:T(128)S(1)}, ...), branch_computations={%region_0.0_spmd, %region_1.2_spmd} | conditional | flops 267808 | bytes 3014720 | solution.py:88
  27.9 7.1 %collective-permute-done.41 = bf16[272,384]{1,0:T(8,128)(2,1)} collective-permute-done((bf16[272,384]{1,0:T(8,128)(2,1)S(1)}, bf16[272,384]{1,0:T(8,128)(2,1)}, u32[]{:S(2)}, u32[]{:S(2)}) %collective-permute-start.41) | collective-permute-done | bytes 208928 | tf_op jit(solution)/shard_map/ppermute | solution.py:72
  37.3 9.5 %conditional.9 = (bf16[512,1024]{1,0:T(8,128)(2,1)S(1)}, bf16[512,1024]{1,0:T(8,128)(2,1)S(1)}, f32[8,1024]{1,0:T(8,128)S(1)}, bf16[1024,1024]{1,0:T(8,128)(2,1)...) conditional(s32[]{:T(128)} %bitcast.30, () %tuple.96, ...), branch_computations={%region_2.3_spmd, %region_3.4_spmd} | conditional | flops 8000001024 | bytes 8159360 | solution.py:88
  38.2 8.6 %branch_1_fun.21 = (bf16[1024,384]{1,0:T(8,128)(2,1)}, f32[8,1024]{1,0:T(8,128)S(1)}, bf16[512,1024]{1,0:T(8,128)(2,1)S(1)}, bf16[512,1024]{1,0:T(8,128)(2,1)S(1...) custom-call(s32[5]{0:T(128)S(1)} %get-tuple-element.166.index, ...), custom_call_target="tpu_custom_call" | custom-call | flops 8000001024 | bytes 1000 | tf_op jit(solution)/shard_map/cond/branch_1_fun/pallas_call | solution.py:623
  47.8 19.0 %conditional.10 = ((f32[128,1024]{1,0:T(8,128)}, f32[128,128]{1,0:T(8,128)}, bf16[128,512]{1,0:T(8,128)(2,1)S(1)}, bf16[128,512]{1,0:T(8,128)(2,1)S(1)})) conditional(s32[]{:T(128)} %bitcast.30, () %tuple.95, (bf16[512,1024]{1,0:T(8,128)(2,1)S(1)}, bf16[512,1024]{1,0:T(8,128)(2,1)S(1)}, bf16[256,1024]{1,0:T(8,128)(2,1)S(1)}, ...), branch_computations={%region_4.5_spmd, %region_5.6_spmd} | conditional | flops 3000 | bytes 7343240 | solution.py:88
  52.5 6.7 %collective-permute-done.1.from_x = bf16[256,512]{1,0:T(8,128)(2,1)S(1)} collective-permute-done((bf16[256,512]{1,0:T(8,128)(2,1)S(1)}, bf16[256,512]{1,0:T(8,128)(2,1)S(1)}, u32[]{:S(2)}, u32[]{:S(2)}) %collective-permute-start.1) | collective-permute-done | bytes 262176 | tf_op jit(solution)/shard_map/cond/branch_1_fun/ppermute | solution.py:17
  70.2 20.6 %conditional.11 = (bf16[512,1024]{1,0:T(8,128)(2,1)}, bf16[512,1024]{1,0:T(8,128)(2,1)}, bf16[256,1024]{1,0:T(8,128)(2,1)}) conditional(s32[]{:T(128)} %bitcast.30, () %tuple.94, (bf16[128,512]{1,0:T(8,128)(2,1)S(1)}, bf16[256,1024]{1,0:T(8,128)(2,1)}, bf16[128,512]{1,0:T(8,128)(2,1)S(1)}) %tuple.104), branch_computations={%region_6.7_spmd, %region_7.8_spmd} | conditional | flops 4456448 | bytes 13107464 | solution.py:88
  79.6 5.8 %collective-permute-done.22 = bf16[2,128,512]{2,1,0:T(8,128)(2,1)S(1)} collective-permute-done((bf16[2,128,512]{2,1,0:T(8,128)(2,1)S(1)}, bf16[2,128,512]{2,1,0:T(8,128)(2,1)S(1)}, u32[]{:S(2)}, u32[]{:S(2)}) %collective-permute-start.22) | collective-permute-done | bytes 262176 | tf_op jit(solution)/shard_map/cond/branch_1_fun/ppermute | solution.py:17
  92.5 3.5 %shard_map.260 = (bf16[1024,640]{1,0:T(8,128)(2,1)}, f32[1024,640]{1,0:T(8,128)S(1)}) custom-call(s32[5]{0:T(128)S(1)} %stack.93.index, bf16[256,1024]{1,0:T(8,128)(2,1)} %copy-done.6, bf16[256,1024]{1,0:T(8,128)(2,1)} %collective-permute-done.46.b1, bf16[256,1024]{1,0:T(8,128)(2,1)} %get-tuple-element.499.b2, bf16[256,1024]{1,0:T(8,128)(2,1)} %get-tuple-element.500.b3, ...), custom_call_target="tpu_custom_call" | custom-call | flops 1000 | bytes 1000 | tf_op jit(solution)/shard_map/pallas_call | solution.py:623
  96.0 3.7 %all-gather.2.cloned.1.call-done.gu_w = bf16[1024,1152]{1,0:T(8,128)(2,1)} async-done(((bf16[256,1152]{1,0:T(8,128)(2,1)}), bf16[1024,1152]{1,0:T(8,128)(2,1)}) %all-gather.2.cloned.1.call-update) | async-done | bytes 2359312 | tf_op jit(solution)/shard_map/all_gather | solution.py:721
  101.4 15.7 %shard_map.261 = (bf16[512,1024]{1,0:T(8,128)(2,1)}, bf16[512,1024]{1,0:T(8,128)(2,1)}, bf16[1024,1792]{1,0:T(8,128)(2,1)}, bf16[1024,640]{1,0:T(8,128)(2,1)}) custom-call(s32[5]{0:T(128)S(1)} %stack.93.index, bf16[512,1024]{1,0:T(8,128)(2,1)} %get-tuple-element.497.x_low, bf16[512,1024]{1,0:T(8,128)(2,1)} %get-tuple-element.498.x_high, ...), custom_call_target="tpu_custom_call" | custom-call | flops 1000 | bytes 1000 | tf_op jit(solution)/shard_map/pallas_call | solution.py:623
  119.0 59.2 %conditional.12 = (bf16[512,1024]{1,0:T(8,128)(2,1)}, bf16[512,1024]{1,0:T(8,128)(2,1)}, bf16[1024,384]{1,0:T(8,128)(2,1)}, f32[8,1024]{1,0:T(8,128)S(1)}, f32[8...) conditional(s32[]{:T(128)} %bitcast.30, () %tuple.93, ...), branch_computations={%region_8.9_spmd, %region_9.10_spmd} | conditional | flops 4464448 | bytes 45621996 | solution.py:88
  119.1 4.2 %branch_1_fun.25 = (bf16[512,1024]{1,0:T(8,128)(2,1)S(1)}, bf16[512,1024]{1,0:T(8,128)(2,1)S(1)}) custom-call(s32[5]{0:T(128)S(1)} %get-tuple-element.209.index, bf16[1024,640]{1,0:T(8,128)(2,1)} %get-tuple-element.212.activated, bf16[1024,640]{1,0:T(8,128)(2,1)} %get-tuple-element.213.down_w), custom_call_target="tpu_custom_call" | custom-call | flops 1000 | bytes 1000 | tf_op jit(solution)/shard_map/cond/branch_1_fun/pallas_call | solution.py:623
  126.0 6.4 %collective-permute-done.26.from_x = bf16[256,512]{1,0:T(8,128)(2,1)S(1)} collective-permute-done((bf16[256,512]{1,0:T(8,128)(2,1)S(1)}, bf16[256,512]{1,0:T(8,128)(2,1)S(1)}, u32[]{:S(2)}, u32[]{:S(2)}) %collective-permute-start.26) | collective-permute-done | bytes 262176 | tf_op jit(solution)/shard_map/cond/branch_1_fun/ppermute | solution.py:17
  148.9 4.1 %collective-permute-done.32 = bf16[2,128,512]{2,1,0:T(8,128)(2,1)S(1)} collective-permute-done((bf16[2,128,512]{2,1,0:T(8,128)(2,1)S(1)}, bf16[2,128,512]{2,1,0:T(8,128)(2,1)S(1)}, u32[]{:S(2)}, u32[]{:S(2)}) %collective-permute-start.32) | collective-permute-done | bytes 262176 | tf_op jit(solution)/shard_map/cond/branch_1_fun/ppermute | solution.py:17
  159.3 11.1 %branch_1_fun.29 = (bf16[512,1024]{1,0:T(8,128)(2,1)}, bf16[512,1024]{1,0:T(8,128)(2,1)}, bf16[1024,256]{1,0:T(8,128)(2,1)S(1)}, f32[8,128]{1,0:T(8,128)S(1)}) custom-call(s32[5]{0:T(128)S(1)} %get-tuple-element.209.index, bf16[512,1024]{1,0:T(8,128)(2,1)S(1)} %bitcast.48, bf16[512,1024]{1,0:T(8,128)(2,1)S(1)} %collective-permute-done.35.a_high, ...), custom_call_target="tpu_custom_call" | custom-call | flops 1000 | bytes 1000 | tf_op jit(solution)/shard_map/cond/branch_1_fun/pallas_call | solution.py:623
  174.6 3.6 %branch_1_fun.32 = (bf16[1024,384]{1,0:T(8,128)(2,1)}, f32[8,1024]{1,0:T(8,128)S(1)}) custom-call(s32[5]{0:T(128)S(1)} %get-tuple-element.209.index, bf16[1024,1024]{1,0:T(8,128)(2,1)S(1)} %get-tuple-element.252.unit, bf16[1024,256]{1,0:T(8,128)(2,1)S(1)} %get-tuple-element.269.back, bf16[512,1024]{1,0:T(8,128)(2,1)S(1)} %bitcast.49, ...), custom_call_target="tpu_custom_call" | custom-call | flops 1000 | bytes 1000 | tf_op jit(solution)/shard_map/cond/branch_1_fun/pallas_call | solution.py:623
  178.3 20.1 %conditional.13 = (f32[128,512]{1,0:T(8,128)S(1)}, bf16[128,512]{1,0:T(8,128)(2,1)}, f32[128,512]{1,0:T(8,128)S(1)}, bf16[128,512]{1,0:T(8,128)(2,1)}, f32[24,12...) conditional(s32[]{:T(128)} %bitcast.30, () %tuple.92, (bf16[512,1024]{1,0:T(8,128)(2,1)}, s32[5]{0:T(128)S(1)}, ...), branch_computations={%region_10.11_spmd, %region_11.12_spmd} | conditional | flops 13216 | bytes 7602448 | solution.py:88
  186.5 5.2 %collective-permute-done.9 = f32[24,128]{1,0:T(8,128)S(1)} collective-permute-done((f32[24,128]{1,0:T(8,128)S(1)}, f32[24,128]{1,0:T(8,128)S(1)}, u32[]{:S(2)}, u32[]{:S(2)}) %collective-permute-start.9) | collective-permute-done | bytes 12320 | tf_op jit(solution)/shard_map/cond/branch_1_fun/ppermute | solution.py:22
  199.2 17.1 %conditional.14 = (bf16[256,1024]{1,0:T(8,128)(2,1)}, bf16[256,1024]{1,0:T(8,128)(2,1)}, bf16[256,1024]{1,0:T(8,128)(2,1)}, f32[24,128]{1,0:T(8,128)S(1)}) conditional(s32[]{:T(128)} %bitcast.30, () %tuple.91, (f32[128,512]{1,0:T(8,128)S(1)}, bf16[128,512]{1,0:T(8,128)(2,1)}, f32[128,512]{1,0:T(8,128)S(1)}, bf16[128,512]{1,0:T(8,128)(2,1)}, ...), branch_computations={%region_13.14_spmd, %region_14.15_spmd} | conditional | flops 7144 | bytes 4367528 | solution.py:88
  212.0 4.4 %collective-permute-done.13 = bf16[256,1024]{1,0:T(8,128)(2,1)} collective-permute-done((bf16[256,1024]{1,0:T(8,128)(2,1)}, bf16[256,1024]{1,0:T(8,128)(2,1)}, u32[]{:S(2)}, u32[]{:S(2)}) %collective-permute-start.13) | collective-permute-done | bytes 524320 | tf_op jit(solution)/shard_map/cond/branch_1_fun/ppermute | solution.py:17
  220.1 4.0 %conditional.15 = (bf16[256,1024]{1,0:T(8,128)(2,1)}, f32[256,1152]{1,0:T(8,128)}, f32[256,1152]{1,0:T(8,128)}, f32[1152,256]{1,0:T(8,128)}, f32[256]{0:T(256)},...) conditional(s32[]{:T(128)} %bitcast.30, () %tuple.113, (bf16[256,1024]{1,0:T(8,128)(2,1)}, ...), branch_computations={%region_16.17_spmd, %region_17.18_spmd} | conditional | flops 2000 | bytes 4065914 | solution.py:88
  224.2 3.4 %shard_map.262 = (f32[512,1024]{1,0:T(8,128)}, bf16[512,1024]{1,0:T(8,128)(2,1)}) custom-call(s32[5]{0:T(128)S(1)} %stack.93.index, bf16[256,1024]{1,0:T(8,128)(2,1)} %get-tuple-element.552.own, bf16[256,1024]{1,0:T(8,128)(2,1)} %get-tuple-element.553.from_y, bf16[256,1024]{1,0:T(8,128)(2,1)} %get-tuple-element.554.from_core, ...), custom_call_target="tpu_custom_call" | custom-call | flops 1000 | bytes 1000 | tf_op jit(solution)/shard_map/pallas_call | solution.py:623
  (206 shorter events, 123.7 us)
Async XLA Ops:
  7.2 92.6 %all-gather.2.cloned.1.call-start = ((), (), s32[]{:S(2)}) async-start(), calls=%async_computation.2 | async-start | bytes 2949120 | tf_op jit(solution)/shard_map/all_gather | solution.py:721
  10.8 24.2 %collective-permute-start.43 = (bf16[256,1024]{1,0:T(8,128)(2,1)S(1)}, bf16[256,1024]{1,0:T(8,128)(2,1)}, u32[]{:S(2)}, u32[]{:S(2)}) collective-permute-start(bf16[256,1024]{1,0:T(8,128)(2,1)S(1)} %get-tuple-element.467), channel_id=1, source_target_pairs={{0,4},{4,0},{1,5},{5,1},{2,6},{6,2},{3,7},{7,3},{8,12},{12,8},{9,1... | collective-permute-start | bytes 1572872 | tf_op jit(solution)/shard_map/ppermute | solution.py:17
  13.8 14.0 %collective-permute-start.42 = (bf16[272,384]{1,0:T(8,128)(2,1)S(1)}, bf16[272,384]{1,0:T(8,128)(2,1)S(1)}, u32[]{:S(2)}, u32[]{:S(2)}) collective-permute-start(bf16[272,384]{1,0:T(8,128)(2,1)S(1)} %get-tuple-element.475), channel_id=1, source_target_pairs={{0,24},{8,16},{16,8},{24,0},{1,25},{9,17},{17,9},{25,1},{2,26},{10... | collective-permute-start | bytes 626696 | tf_op jit(solution)/shard_map/ppermute | solution.py:72
  17.4 17.6 %collective-permute-start.41 = (bf16[272,384]{1,0:T(8,128)(2,1)S(1)}, bf16[272,384]{1,0:T(8,128)(2,1)}, u32[]{:S(2)}, u32[]{:S(2)}) collective-permute-start(bf16[272,384]{1,0:T(8,128)(2,1)S(1)} %get-tuple-element.475), channel_id=1, source_target_pairs={{0,16},{8,24},{16,0},{24,8},{1,17},{9,25},{17,1},{25,9},{2,18},{10... | collective-permute-start | bytes 626696 | tf_op jit(solution)/shard_map/ppermute | solution.py:72
  17.4 17.6 %collective-permute-start.40 = (bf16[272,384]{1,0:T(8,128)(2,1)S(1)}, bf16[272,384]{1,0:T(8,128)(2,1)}, u32[]{:S(2)}, u32[]{:S(2)}) collective-permute-start(bf16[272,384]{1,0:T(8,128)(2,1)S(1)} %get-tuple-element.475), channel_id=1, source_target_pairs={{0,8},{8,0},{16,24},{24,16},{1,9},{9,1},{17,25},{25,17},{2,10},{10... | collective-permute-start | bytes 626696 | tf_op jit(solution)/shard_map/ppermute | solution.py:72
  35.0 163.4 %reduce-scatter.3.cloned.1.call-start = ((), (), s32[]{:S(2)}) async-start(), calls=%async_computation.3 | async-start | bytes 4587520 | tf_op jit(solution)/shard_map/reduce_scatter | solution.py:783
  35.2 12.6 %collective-permute-start.45 = (bf16[256,640]{1,0:T(8,128)(2,1)S(1)}, bf16[256,640]{1,0:T(8,128)(2,1)S(1)}, u32[]{:S(2)}, u32[]{:S(2)}) collective-permute-start(bf16[256,640]{1,0:T(8,128)(2,1)S(1)} %get-tuple-element.502.rest_0_), channel_id=1, source_target_pairs={{0,8},{8,16},{16,24},{24,0},{1,9},{9,17},{17,25},{25,1},{2,10},{10... | collective-permute-start | bytes 983048 | tf_op jit(solution)/shard_map/ppermute | solution.py:79
  35.2 31.6 %collective-permute-start.46 = (bf16[256,1024]{1,0:T(8,128)(2,1)S(1)}, bf16[256,1024]{1,0:T(8,128)(2,1)}, u32[]{:S(2)}, u32[]{:S(2)}) collective-permute-start(bf16[256,1024]{1,0:T(8,128)(2,1)S(1)} %get-tuple-element.486.b0), channel_id=1, source_target_pairs={{0,4},{4,0},{1,5},{5,1},{2,6},{6,2},{3,7},{7,3},{8,12},{12,8},{9,1... | collective-permute-start | bytes 1572872 | tf_op jit(solution)/shard_map/ppermute | solution.py:17
  47.8 19.0 %collective-permute-start.47 = (bf16[256,640]{1,0:T(8,128)(2,1)S(1)}, bf16[256,640]{1,0:T(8,128)(2,1)S(1)}, u32[]{:S(2)}, u32[]{:S(2)}) collective-permute-start(bf16[256,640]{1,0:T(8,128)(2,1)S(1)} %collective-permute-done.45.rest_1_), channel_id=1, source_target_pairs={{0,8},{8,16},{16,24},{24,0},{1,9},{9,17},{17,25},{25,1},{2,10},{10... | collective-permute-start | bytes 983048 | tf_op jit(solution)/shard_map/ppermute | solution.py:79
  50.7 8.4 %collective-permute-start.1 = (bf16[256,512]{1,0:T(8,128)(2,1)S(1)}, bf16[256,512]{1,0:T(8,128)(2,1)S(1)}, u32[]{:S(2)}, u32[]{:S(2)}) collective-permute-start(bf16[256,512]{1,0:T(8,128)(2,1)S(1)} %get-tuple-element.194), channel_id=1, source_target_pairs={{0,4},{4,0},{1,5},{5,1},{2,6},{6,2},{3,7},{7,3},{8,12},{12,8},{9,1... | collective-permute-start | bytes 786440 | tf_op jit(solution)/shard_map/cond/branch_1_fun/ppermute | solution.py:17
  50.8 8.4 %collective-permute-start.2 = (bf16[256,512]{1,0:T(8,128)(2,1)S(1)}, bf16[256,512]{1,0:T(8,128)(2,1)S(1)}, u32[]{:S(2)}, u32[]{:S(2)}) collective-permute-start(bf16[256,512]{1,0:T(8,128)(2,1)S(1)} %get-tuple-element.196), channel_id=1, source_target_pairs={{0,2},{2,0},{1,3},{3,1},{4,6},{6,4},{5,7},{7,5},{8,10},{10,8},{9,1... | collective-permute-start | bytes 786440 | tf_op jit(solution)/shard_map/cond/branch_1_fun/ppermute | solution.py:17
  66.9 24.0 %collective-permute-start.48 = (bf16[256,640]{1,0:T(8,128)(2,1)S(1)}, bf16[256,640]{1,0:T(8,128)(2,1)S(1)}, u32[]{:S(2)}, u32[]{:S(2)}) collective-permute-start(bf16[256,640]{1,0:T(8,128)(2,1)S(1)} %collective-permute-done.47.rest_2_), channel_id=1, source_target_pairs={{0,8},{8,16},{16,24},{24,0},{1,9},{9,17},{17,25},{25,1},{2,10},{10... | collective-permute-start | bytes 983048 | tf_op jit(solution)/shard_map/ppermute | solution.py:79
  117.2 99.1 %reduce-scatter.5.cloned.1.call-start = ((), (), s32[]{:S(2)}) async-start(), calls=%async_computation.4 | async-start | bytes 983040 | tf_op jit(solution)/shard_map/reduce_scatter | solution.py:831
  123.3 9.2 %collective-permute-start.28 = (bf16[512,1024]{1,0:T(8,128)(2,1)S(1)}, bf16[512,1024]{1,0:T(8,128)(2,1)S(1)}, u32[]{:S(2)}, u32[]{:S(2)}) collective-permute-start(bf16[512,1024]{1,0:T(8,128)(2,1)S(1)} %get-tuple-element.221), channel_id=1, source_target_pairs={{0,1},{1,0},{2,3},{3,2},{4,5},{5,4},{6,7},{7,6},{8,9},{9,8},{10,11... | collective-permute-start | bytes 3145736 | tf_op jit(solution)/shard_map/cond/branch_1_fun/ppermute | solution.py:17
  124.0 8.4 %collective-permute-start.26 = (bf16[256,512]{1,0:T(8,128)(2,1)S(1)}, bf16[256,512]{1,0:T(8,128)(2,1)S(1)}, u32[]{:S(2)}, u32[]{:S(2)}) collective-permute-start(bf16[256,512]{1,0:T(8,128)(2,1)S(1)} %get-tuple-element.218), channel_id=1, source_target_pairs={{0,4},{4,0},{1,5},{5,1},{2,6},{6,2},{3,7},{7,3},{8,12},{12,8},{9,1... | collective-permute-start | bytes 786440 | tf_op jit(solution)/shard_map/cond/branch_1_fun/ppermute | solution.py:17
  124.5 8.0 %collective-permute-start.27 = (bf16[256,512]{1,0:T(8,128)(2,1)S(1)}, bf16[256,512]{1,0:T(8,128)(2,1)S(1)}, u32[]{:S(2)}, u32[]{:S(2)}) collective-permute-start(bf16[256,512]{1,0:T(8,128)(2,1)S(1)} %get-tuple-element.220), channel_id=1, source_target_pairs={{0,2},{2,0},{1,3},{3,1},{4,6},{6,4},{5,7},{7,5},{8,10},{10,8},{9,1... | collective-permute-start | bytes 786440 | tf_op jit(solution)/shard_map/cond/branch_1_fun/ppermute | solution.py:17
  158.4 12.0 %collective-permute-start.36 = (bf16[256,512]{1,0:T(8,128)(2,1)S(1)}, bf16[256,512]{1,0:T(8,128)(2,1)S(1)}, u32[]{:S(2)}, u32[]{:S(2)}) collective-permute-start(bf16[256,512]{1,0:T(8,128)(2,1)S(1)} %get-tuple-element.257), channel_id=1, source_target_pairs={{0,4},{4,0},{1,5},{5,1},{2,6},{6,2},{3,7},{7,3},{8,12},{12,8},{9,1... | collective-permute-start | bytes 786440 | tf_op jit(solution)/shard_map/cond/branch_1_fun/ppermute | solution.py:17
  158.5 11.9 %collective-permute-start.37 = (bf16[256,512]{1,0:T(8,128)(2,1)S(1)}, bf16[256,512]{1,0:T(8,128)(2,1)S(1)}, u32[]{:S(2)}, u32[]{:S(2)}) collective-permute-start(bf16[256,512]{1,0:T(8,128)(2,1)S(1)} %get-tuple-element.259), channel_id=1, source_target_pairs={{0,2},{2,0},{1,3},{3,1},{4,6},{6,4},{5,7},{7,5},{8,10},{10,8},{9,1... | collective-permute-start | bytes 786440 | tf_op jit(solution)/shard_map/cond/branch_1_fun/ppermute | solution.py:17
  182.8 9.0 %collective-permute-start.6 = (bf16[256,512]{1,0:T(8,128)(2,1)S(1)}, bf16[256,512]{1,0:T(8,128)(2,1)S(1)}, u32[]{:S(2)}, u32[]{:S(2)}) collective-permute-start(bf16[256,512]{1,0:T(8,128)(2,1)S(1)} %get-tuple-element.301), channel_id=1, source_target_pairs={{0,4},{4,0},{1,5},{5,1},{2,6},{6,2},{3,7},{7,3},{8,12},{12,8},{9,1... | collective-permute-start | bytes 786440 | tf_op jit(solution)/shard_map/cond/branch_1_fun/ppermute | solution.py:17
  184.3 8.4 %collective-permute-start.7 = (bf16[256,512]{1,0:T(8,128)(2,1)S(1)}, bf16[256,512]{1,0:T(8,128)(2,1)S(1)}, u32[]{:S(2)}, u32[]{:S(2)}) collective-permute-start(bf16[256,512]{1,0:T(8,128)(2,1)S(1)} %get-tuple-element.303), channel_id=1, source_target_pairs={{0,2},{2,0},{1,3},{3,1},{4,6},{6,4},{5,7},{7,5},{8,10},{10,8},{9,1... | collective-permute-start | bytes 786440 | tf_op jit(solution)/shard_map/cond/branch_1_fun/ppermute | solution.py:17
  198.4 20.7 %collective-permute-start.49 = (bf16[256,1792]{1,0:T(8,128)(2,1)}, bf16[256,1792]{1,0:T(8,128)(2,1)S(1)}, u32[]{:S(2)}, u32[]{:S(2)}) collective-permute-start(bf16[256,1792]{1,0:T(8,128)(2,1)} %reduce-scatter.3.cloned.1.call-done), channel_id=1, source_target_pairs={{0,4},{4,0},{1,5},{5,1},{2,6},{6,2},{3,7},{7,3},{8,12},{12,8},{9,1... | collective-permute-start | bytes 2752520 | tf_op jit(solution)/shard_map/ppermute | solution.py:17
  201.7 10.3 %collective-permute-start.14 = (bf16[256,1024]{1,0:T(8,128)(2,1)}, bf16[256,1024]{1,0:T(8,128)(2,1)}, u32[]{:S(2)}, u32[]{:S(2)}) collective-permute-start(bf16[256,1024]{1,0:T(8,128)(2,1)} %branch_1_fun.37), channel_id=1, source_target_pairs={{0,1},{1,0},{2,3},{3,2},{4,5},{5,4},{6,7},{7,6},{8,9},{9,8},{10,11... | collective-permute-start | bytes 1572872 | tf_op jit(solution)/shard_map/cond/branch_1_fun/ppermute | solution.py:17
  201.7 14.7 %collective-permute-start.13 = (bf16[256,1024]{1,0:T(8,128)(2,1)}, bf16[256,1024]{1,0:T(8,128)(2,1)}, u32[]{:S(2)}, u32[]{:S(2)}) collective-permute-start(bf16[256,1024]{1,0:T(8,128)(2,1)} %branch_1_fun.37), channel_id=1, source_target_pairs={{0,2},{2,0},{1,3},{3,1},{4,6},{6,4},{5,7},{7,5},{8,10},{10,8},{9,1... | collective-permute-start | bytes 1572872 | tf_op jit(solution)/shard_map/cond/branch_1_fun/ppermute | solution.py:17
  219.2 8.4 %collective-permute-start.50 = (bf16[256,384]{1,0:T(8,128)(2,1)}, bf16[256,384]{1,0:T(8,128)(2,1)S(1)}, u32[]{:S(2)}, u32[]{:S(2)}) collective-permute-start(bf16[256,384]{1,0:T(8,128)(2,1)} %reduce-scatter.5.cloned.1.call-done.mine), channel_id=1, source_target_pairs={{0,4},{4,0},{1,5},{5,1},{2,6},{6,2},{3,7},{7,3},{8,12},{12,8},{9,1... | collective-permute-start | bytes 589832 | tf_op jit(solution)/shard_map/ppermute | solution.py:17
  (60 other events, 352.5 us)
Sparse Core Ops, SparseCore 0:
  35.2 64.5 all-gather.1
  117.3 69.7 reduce-scatter.2
  189.4 23.9 reduce-scatter.4

commit v2 on v1

--- a/solution.py
+++ b/solution.py
@@ -411,14 +411,13 @@
     output[...] = ((middle[...] + total) * validity(index, middle.shape[0])).astype(BF16)
 
 
-def to_input_grad(left, from_y, right, from_x, middle_grad, hidden, gains, output, out):
-    block = middle_grad.shape[0]
+def to_input_grad(left, from_y, right, from_x, middle_grad, hidden, gains, out):
+    block = out.shape[0]
     x = hidden[:block, :].astype(F32)
     r = inverse_of(x)
     u = x * r
     c = joined(left, from_y, right, from_x) * gains[0:1, :]
-    out[:block, :] = (middle_grad[...] + r * (c - u * jnp.mean(c * u, axis=-1, keepdims=True))).astype(BF16)
-    out[block:, :] = output[...]
+    out[...] = (middle_grad[...] + r * (c - u * jnp.mean(c * u, axis=-1, keepdims=True))).astype(BF16)
 
 
 def small_sums(index, hidden, middle, branch, second, inverse, attention_sums, head_sums, out):
@@ -598,12 +597,11 @@
     stats[...] = jnp.sqrt(line / (count * index[4].astype(F32)))[0, :4]
 
 
-def unpack_rows(index, own, from_y, from_core, from_both, rows, block_rows):
-    block = own.shape[0] // 2
+def unpack_rows(index, own, from_y, from_core, from_both, rows):
+    block = own.shape[0]
     for at, part in enumerate((own, from_y, from_core, from_both)):
         to = pl.multiple_of(((index[0] ^ (2 * (at % 2) + at // 2)) & 3) * block, block)
-        rows[pl.ds(to, block), :] = part[:block, :].astype(F32)
-        block_rows[pl.ds(to, block), :] = part[block:, :]
+        rows[pl.ds(to, block), :] = part[...].astype(rows.dtype)
 
 
 def call(kernel, outs, args, scratch=(), limit=48, fetched=0, cost=0):
@@ -685,7 +683,6 @@
         limit=60,
         fetched=6,
     )
-    hidden_other = swap(hidden_near, "ctx")
     if near_shards():
         attn_parts = direct([attn_own] * size)
     else:
@@ -693,7 +690,8 @@
         gains = attn_parts[:, rows : rows + 8, :rows].astype(F32).transpose(1, 0, 2).reshape(8, -1)
         attn_parts = [attn_parts[:, :rows].reshape(-1, wide + lane), gains]
 
-    def prepare(positions, gate_weight, up_weight, down_weight, cotangent):
+    def prepare(hidden_near, positions, gate_weight, up_weight, down_weight, cotangent):
+        hidden_other = swap(hidden_near, "ctx")
         gu_own, down_own, *cotangent_rel = call(
             pack_feed_forward,
             [((rows, 2 * hidden), BF16), ((rows, main + lane), BF16)] + [((local // 2, width), BF16)] * 2,
@@ -712,12 +710,13 @@
         angles = places.astype(F32)[:, None] * jnp.tile(freqs, 4)[None, :]
         cosine = jnp.cos(angles)
         sine = jnp.sin(angles) * jnp.where(jnp.arange(lane) % HD < HD // 2, -1.0, 1.0)[None, :]
-        return gu_own, down_own, cosine, sine, *cotangent_rel
-
-    gu_own, down_own, cosine, sine, cotangent_near, cotangent_far = region(
-        flag, prepare, positions, gate_weight, up_weight, down_weight, cotangent
-    )
-    attn_parts, gu_own, hidden_other, cotangent_near = together(attn_parts, gu_own, hidden_other, cotangent_near)
+        hidden_other, gu_own, cosine, sine = together(hidden_other, gu_own, cosine, sine)
+        return hidden_other, gu_own, down_own, cosine, sine, *cotangent_rel
+
+    hidden_other, gu_own, down_own, cosine, sine, cotangent_near, cotangent_far = region(
+        flag, prepare, hidden_near, positions, gate_weight, up_weight, down_weight, cotangent
+    )
+    attn_parts, gu_own, cotangent_near = together(attn_parts, gu_own, cotangent_near)
     gu_full = lax.all_gather(gu_own, "fsdp", axis=0, tiled=True)
     down_parts = [down_own]
     if near_shards():
@@ -783,10 +782,11 @@
     ff_share = lax.psum_scatter(ff_grad, "fsdp", scatter_dimension=0, tiled=True)
 
     def turn(near, far, middle, inverse_two, cotangent_near, gains, activated, down_full, unit, mixed_rel, kept):
-        far, branch_parts = together(
-            swap(far, "core"), call(down_product, [((every // 2, width), BF16)] * 2, (index, activated, down_full))
-        )
-        terms, branch_far = together(scatter_start(near, far), swap(branch_parts[1], "core"))
+        terms, branch_parts = together(
+            scatter_start(near, swap(far, "core")),
+            call(down_product, [((every // 2, width), BF16)] * 2, (index, activated, down_full)),
+        )
+        branch_far = swap(branch_parts[1], "core")
         second, middle_grad, left, right = call(
             to_middle_grad,
             [whole, whole, quarter, quarter],
@@ -831,19 +831,16 @@
     attn_share = lax.psum_scatter(attn_grad, "fsdp", scatter_dimension=0, tiled=True)
 
     def sum_first(near, far, branch, middle, hidden_near, second, inverse, attention_sums, head_sums):
-        far = swap(far, "core")
+        terms = scatter_start(near, swap(far, "core"))
         branch, output = call(to_output, [whole, ((block, width), BF16)], (index, *branch, middle))
         (small,) = call(
             small_sums,
             [((24, lane), F32)],
             (index, hidden_near, middle, branch, second, inverse, attention_sums, head_sums),
         )
-        far, small = together(far, small)
-        terms = scatter_start(near, far)
         small = small + hop(small, "core")
-        terms, more = together(terms, hop(small, "ctx"))
-        small = small + more
-        terms, more = together(scatter_next(*terms), hop(small, "y"))
+        terms, small = together(terms, small)
+        terms, more = together(scatter_next(*terms), hop(small, "ctx"))
         return terms, small + more, output
 
     pieces, small, output = region(
@@ -864,22 +861,27 @@
 
     def finish(pieces, middle_grad, hidden_near, gains, output, small):
         (own_rows,) = call(
-            to_input_grad, [((2 * block, width), BF16)], (*pieces, middle_grad, hidden_near, gains, output)
-        )
+            to_input_grad, [((block, width), BF16)], (*pieces, middle_grad, hidden_near, gains)
+        )
+        own_rows, small = together(own_rows, small + hop(small, "y"))
         rows_y, rows_core = swap(own_rows, "y"), swap(own_rows, "core")
-        step = 1
+        output_y = swap(output, "y")
+        rows_y, rows_core, output_y, small = together(rows_y, rows_core, output_y, small + hop(small, "fsdp"))
+        (input_rows,) = call(
+            unpack_rows, [((local, width), F32)], (index, own_rows, rows_y, rows_core, swap(rows_y, "core"))
+        )
+        step = 2
         while step < size:
             small = small + hop(small, "fsdp", step)
             step *= 2
-        rows_y, rows_core, small = together(rows_y, rows_core, small)
-        return own_rows, rows_y, rows_core, small
-
-    *three, small = region(flag, finish, pieces, middle_grad, hidden_near, gains, output, small)
-    three, attn_share, ff_other = together(three, attn_share, ff_other)
+        return together(input_rows, output_y, small)
+
+    input_rows, output_y, small = region(flag, finish, pieces, middle_grad, hidden_near, gains, output, small)
+    output_y, attn_share, ff_other = together(output_y, attn_share, ff_other)
     attn_other = swap(attn_share, "ctx")
 
-    def unpack(index, three, ff_share, ff_other, small):
-        last = swap(three[1], "core")
+    def unpack(index, output, output_y, ff_share, ff_other, small):
+        output_core, last = swap(output, "core"), swap(output_y, "core")
         ff_grads = call(
             unpack_feed_forward,
             [((rows, 2 * hidden), F32)] * 2 + [((2 * hidden, rows), F32)],
@@ -888,13 +890,14 @@
         results = call(
             small_results, [((rows,), F32)] * 2 + [((HD,), F32)] * 2 + [((4,), F32)], (index, small)
         )
-        return together(last, ff_grads, results)
-
-    last, ff_grads, results = region(flag, unpack, index, three, ff_share, ff_other, small)
-    input_rows, block_rows = call(
-        unpack_rows, [((local, width), F32), ((local, width), BF16)], (index, *three, last)
-    )
-    attn_other, input_rows = together(attn_other, input_rows)
+        output_core, last, ff_grads, results = together(output_core, last, ff_grads, results)
+        (block_rows,) = call(
+            unpack_rows, [((local, width), BF16)], (index, output, output_y, output_core, last)
+        )
+        return block_rows, ff_grads, results
+
+    block_rows, ff_grads, results = region(flag, unpack, index, output, output_y, ff_share, ff_other, small)
+    attn_other, block_rows = together(attn_other, block_rows)
     attn_grads = call(
         unpack_attention,
         [((rows, 2 * lane), F32)] + [((rows, lane), F32)] * 2 + [((2 * lane, rows), F32)],

time: 236 us -> 234 us (level)
  waiting for transfers between devices: 89.5 us -> 83.9 us
  starting transfers between devices: 47.7 us -> 51.5 us
    ppermute x3, waiting for transfers between devices: 7.13 us -> 1.91 us  [direct(): lax.ppermute(piece, 'fsdp', [(i, i ^ step) for i in range(size)])]
    ppermute x40 -> x43, waiting for transfers between devices: 64.2 us -> 67.7 us  [swap(): return lax.ppermute(value, axis, [(0, 1), (1, 0)])]
    ppermute x5, waiting for transfers between devices: 13.4 us -> 10.2 us  [hop(): return lax.ppermute(value, axis, [(i, i ^ step) for i in range(size)])]
    ppermute x40 -> x43, starting transfers between devices: 33.4 us -> 35.6 us  [swap(): return lax.ppermute(value, axis, [(0, 1), (1, 0)])]
    pallas_call x25 -> x26, Pallas kernels: 73 us -> 71.8 us  [call(): pl.pallas_call(kernel, out_shape=[jax.ShapeDtypeStruct(shape, kind) for s...]
    unnamed x36 -> x38, local copies, waits for them, and re-layouts: 5.2 us -> 5.53 us
  transfers between devices with their start and end apart: 54 -> 57, of which waited for: 33 -> 35; matrix products, arithmetic and copies ran while one was open for 2% -> 2% of each run, Pallas kernels for 22% -> 22%
where the time goes in v2:
time: 234 us; the launch traced here: 233 us
  waiting for transfers between devices  83.9 us (36%)
  Pallas kernels  71.8 us (31%)
  starting transfers between devices  51.5 us (22%)
  between operations  14.6 us (6%)
  local copies, waits for them, and re-layouts  7.48 us (3%)
  other arithmetic  3.35 us (1%)
    pallas_call x26, Pallas kernels, call(): pl.pallas_call(kernel, out_shape=[jax.ShapeDtypeStruct(shape, kind) for s...  71.8 us
    ppermute x43, waiting for transfers between devices, swap(): return lax.ppermute(value, axis, [(0, 1), (1, 0)])  67.7 us
    ppermute x43, starting transfers between devices, swap(): return lax.ppermute(value, axis, [(0, 1), (1, 0)])  35.6 us
    ppermute x5, waiting for transfers between devices, hop(): return lax.ppermute(value, axis, [(i, i ^ step) for i in range(size)])  10.2 us
    ppermute x5, starting transfers between devices, hop(): return lax.ppermute(value, axis, [(i, i ^ step) for i in range(size)])  5.87 us
    ppermute x3, starting transfers between devices, direct(): lax.ppermute(piece, 'fsdp', [(i, i ^ step) for i in range(size)])  5.76 us
    unnamed x38, local copies, waits for them, and re-layouts  5.53 us
  transfers between devices with their start and end apart: 57, of which 35 were waited for; matrix products, arithmetic and copies ran while one was open for 2% of the time, Pallas kernels for 22%

profile of v2, /device:TPU:0, one launch (start us, length us, event | category | flops | bytes accessed | tf_op | source)
XLA Modules:
  0.0 233.0 jit_solution(5671497918123799209)
XLA Ops:
  10.8 5.1 %collective-permute-start.47 = (bf16[272,384]{1,0:T(8,128)(2,1)S(1)}, bf16[272,384]{1,0:T(8,128)(2,1)S(1)}, u32[]{:S(2)}, u32[]{:S(2)}) collective-permute-start(bf16[272,384]{1,0:T(8,128)(2,1)S(1)} %get-tuple-element.499), channel_id=1, source_target_pairs={{0,24},{8,16},{16,8},{24,0},{1,25},{9,17},{17,9},{25,1},{2,26},{10... | collective-permute-start | bytes 626696 | tf_op jit(solution)/shard_map/ppermute | solution.py:72
  16.6 15.3 %conditional.8 = (bf16[256,1024]{1,0:T(8,128)(2,1)}, bf16[256,1152]{1,0:T(8,128)(2,1)S(1)}, bf16[256,640]{1,0:T(8,128)(2,1)S(1)}, f32[1024,128]{1,0:T(8,128)S(1)...) conditional(s32[]{:T(128)} %bitcast.28, () %tuple.101, ...), branch_computations={%region_0.0_spmd, %region_1.2_spmd} | conditional | flops 267808 | bytes 3539018 | solution.py:88
  24.6 7.2 %collective-permute-done.21 = bf16[256,1024]{1,0:T(8,128)(2,1)} collective-permute-done((bf16[256,1024]{1,0:T(8,128)(2,1)S(1)}, bf16[256,1024]{1,0:T(8,128)(2,1)}, u32[]{:S(2)}, u32[]{:S(2)}) %collective-permute-start.21) | collective-permute-done | bytes 524320 | tf_op jit(solution)/shard_map/cond/branch_1_fun/ppermute | solution.py:17
  36.1 9.5 %conditional.9 = (bf16[512,1024]{1,0:T(8,128)(2,1)S(1)}, bf16[512,1024]{1,0:T(8,128)(2,1)S(1)}, f32[8,1024]{1,0:T(8,128)S(1)}, bf16[1024,1024]{1,0:T(8,128)(2,1)...) conditional(s32[]{:T(128)} %bitcast.28, () %tuple.100, ...), branch_computations={%region_2.3_spmd, %region_3.4_spmd} | conditional | flops 8000001024 | bytes 8159360 | solution.py:88
  37.0 8.6 %branch_1_fun.23 = (bf16[1024,384]{1,0:T(8,128)(2,1)}, f32[8,1024]{1,0:T(8,128)S(1)}, bf16[512,1024]{1,0:T(8,128)(2,1)S(1)}, bf16[512,1024]{1,0:T(8,128)(2,1)S(1...) custom-call(s32[5]{0:T(128)S(1)} %get-tuple-element.181.index, ...), custom_call_target="tpu_custom_call" | custom-call | flops 8000001024 | bytes 1000 | tf_op jit(solution)/shard_map/cond/branch_1_fun/pallas_call | solution.py:621
  46.0 20.1 %conditional.10 = ((f32[128,1024]{1,0:T(8,128)}, f32[128,128]{1,0:T(8,128)}, bf16[128,512]{1,0:T(8,128)(2,1)S(1)}, bf16[128,512]{1,0:T(8,128)(2,1)S(1)})) conditional(s32[]{:T(128)} %bitcast.28, () %tuple.99, (bf16[512,1024]{1,0:T(8,128)(2,1)S(1)}, bf16[512,1024]{1,0:T(8,128)(2,1)S(1)}, bf16[256,1024]{1,0:T(8,128)(2,1)S(1)}, ...), branch_computations={%region_4.5_spmd, %region_5.6_spmd} | conditional | flops 3000 | bytes 7343240 | solution.py:88
  52.0 5.3 %collective-permute-done.1.from_x = bf16[256,512]{1,0:T(8,128)(2,1)S(1)} collective-permute-done((bf16[256,512]{1,0:T(8,128)(2,1)S(1)}, bf16[256,512]{1,0:T(8,128)(2,1)S(1)}, u32[]{:S(2)}, u32[]{:S(2)}) %collective-permute-start.1) | collective-permute-done | bytes 262176 | tf_op jit(solution)/shard_map/cond/branch_1_fun/ppermute | solution.py:17
  66.1 3.9 %collective-permute-start.51 = (bf16[256,640]{1,0:T(8,128)(2,1)S(1)}, bf16[256,640]{1,0:T(8,128)(2,1)S(1)}, u32[]{:S(2)}, u32[]{:S(2)}) collective-permute-start(bf16[256,640]{1,0:T(8,128)(2,1)S(1)} %collective-permute-done.50.rest_2_), channel_id=1, source_target_pairs={{0,8},{8,16},{16,24},{24,0},{1,9},{9,17},{17,25},{25,1},{2,10},{10... | collective-permute-start | bytes 983048 | tf_op jit(solution)/shard_map/ppermute | solution.py:79
  70.0 19.7 %conditional.11 = (bf16[512,1024]{1,0:T(8,128)(2,1)}, bf16[512,1024]{1,0:T(8,128)(2,1)}, bf16[256,1024]{1,0:T(8,128)(2,1)}) conditional(s32[]{:T(128)} %bitcast.28, () %tuple.98, (bf16[128,512]{1,0:T(8,128)(2,1)S(1)}, bf16[256,1024]{1,0:T(8,128)(2,1)}, bf16[128,512]{1,0:T(8,128)(2,1)S(1)}) %tuple.108), branch_computations={%region_6.7_spmd, %region_7.8_spmd} | conditional | flops 4456448 | bytes 13107464 | solution.py:88
  72.2 3.6 %collective-permute-done.24 = bf16[128,512]{1,0:T(8,128)(2,1)S(1)} collective-permute-done((bf16[128,512]{1,0:T(8,128)(2,1)S(1)}, bf16[128,512]{1,0:T(8,128)(2,1)S(1)}, u32[]{:S(2)}, u32[]{:S(2)}) %collective-permute-start.24) | collective-permute-done | bytes 131104 | tf_op jit(solution)/shard_map/cond/branch_1_fun/ppermute | solution.py:17
  79.5 4.7 %collective-permute-done.26 = bf16[2,128,512]{2,1,0:T(8,128)(2,1)S(1)} collective-permute-done((bf16[2,128,512]{2,1,0:T(8,128)(2,1)S(1)}, bf16[2,128,512]{2,1,0:T(8,128)(2,1)S(1)}, u32[]{:S(2)}, u32[]{:S(2)}) %collective-permute-start.26) | collective-permute-done | bytes 262176 | tf_op jit(solution)/shard_map/cond/branch_1_fun/ppermute | solution.py:17
  94.9 3.6 %all-gather.2.cloned.1.call-done.gu_w = bf16[1024,1152]{1,0:T(8,128)(2,1)} async-done(((bf16[256,1152]{1,0:T(8,128)(2,1)}), bf16[1024,1152]{1,0:T(8,128)(2,1)}) %all-gather.2.cloned.1.call-update) | async-done | bytes 2359312 | tf_op jit(solution)/shard_map/all_gather | solution.py:720
  100.2 15.7 %shard_map.261 = (bf16[512,1024]{1,0:T(8,128)(2,1)}, bf16[512,1024]{1,0:T(8,128)(2,1)}, bf16[1024,1792]{1,0:T(8,128)(2,1)}, bf16[1024,640]{1,0:T(8,128)(2,1)}) custom-call(s32[5]{0:T(128)S(1)} %stack.93.index, bf16[512,1024]{1,0:T(8,128)(2,1)} %get-tuple-element.521.x_low, bf16[512,1024]{1,0:T(8,128)(2,1)} %get-tuple-element.522.x_high, ...), custom_call_target="tpu_custom_call" | custom-call | flops 1000 | bytes 1000 | tf_op jit(solution)/shard_map/pallas_call | solution.py:621
  117.8 59.2 %conditional.12 = (bf16[512,1024]{1,0:T(8,128)(2,1)}, bf16[512,1024]{1,0:T(8,128)(2,1)}, bf16[1024,384]{1,0:T(8,128)(2,1)}, f32[8,1024]{1,0:T(8,128)S(1)}, f32[8...) conditional(s32[]{:T(128)} %bitcast.28, () %tuple.97, ...), branch_computations={%region_8.9_spmd, %region_9.10_spmd} | conditional | flops 4464448 | bytes 46670572 | solution.py:88
  125.1 3.7 %branch_1_fun.28 = (bf16[512,1024]{1,0:T(8,128)(2,1)S(1)}, bf16[512,1024]{1,0:T(8,128)(2,1)S(1)}) custom-call(s32[5]{0:T(128)S(1)} %get-tuple-element.224.index, bf16[1024,640]{1,0:T(8,128)(2,1)} %get-tuple-element.231.activated, bf16[1024,640]{1,0:T(8,128)(2,1)S(1)} %copy-done.19), custom_call_target="tpu_custom_call" | custom-call | flops 1000 | bytes 1000 | tf_op jit(solution)/shard_map/cond/branch_1_fun/pallas_call | solution.py:621
  141.1 3.9 %collective-permute-done.34 = bf16[128,512]{1,0:T(8,128)(2,1)S(1)} collective-permute-done((bf16[128,512]{1,0:T(8,128)(2,1)S(1)}, bf16[128,512]{1,0:T(8,128)(2,1)S(1)}, u32[]{:S(2)}, u32[]{:S(2)}) %collective-permute-start.34) | collective-permute-done | bytes 131104 | tf_op jit(solution)/shard_map/cond/branch_1_fun/ppermute | solution.py:17
  158.6 10.9 %branch_1_fun.31 = (bf16[512,1024]{1,0:T(8,128)(2,1)}, bf16[512,1024]{1,0:T(8,128)(2,1)}, bf16[1024,256]{1,0:T(8,128)(2,1)S(1)}, f32[8,128]{1,0:T(8,128)}) custom-call(s32[5]{0:T(128)S(1)} %get-tuple-element.224.index, bf16[512,1024]{1,0:T(8,128)(2,1)S(1)} %bitcast.48, bf16[512,1024]{1,0:T(8,128)(2,1)S(1)} %collective-permute-done.38.a_high, ...), custom_call_target="tpu_custom_call" | custom-call | flops 1000 | bytes 1000 | tf_op jit(solution)/shard_map/cond/branch_1_fun/pallas_call | solution.py:621
  172.0 3.7 %branch_1_fun.34 = (bf16[1024,384]{1,0:T(8,128)(2,1)}, f32[8,1024]{1,0:T(8,128)S(1)}) custom-call(s32[5]{0:T(128)S(1)} %get-tuple-element.224.index, bf16[1024,1024]{1,0:T(8,128)(2,1)S(1)} %get-tuple-element.265.unit, bf16[1024,256]{1,0:T(8,128)(2,1)S(1)} %get-tuple-element.282.back, bf16[512,1024]{1,0:T(8,128)(2,1)S(1)} %bitcast.49, ...), custom_call_target="tpu_custom_call" | custom-call | flops 1000 | bytes 1000 | tf_op jit(solution)/shard_map/cond/branch_1_fun/pallas_call | solution.py:621
  177.1 18.9 %conditional.13 = (f32[128,512]{1,0:T(8,128)S(1)}, bf16[128,512]{1,0:T(8,128)(2,1)}, f32[128,512]{1,0:T(8,128)S(1)}, bf16[128,512]{1,0:T(8,128)(2,1)}, f32[24,12...) conditional(s32[]{:T(128)} %bitcast.28, () %tuple.96, (bf16[512,1024]{1,0:T(8,128)(2,1)}, ...), branch_computations={%region_10.11_spmd, %region_11.12_spmd} | conditional | flops 10144 | bytes 9613572 | solution.py:88
  197.5 19.5 %conditional.14 = (bf16[128,1024]{1,0:T(8,128)(2,1)}, f32[24,128]{1,0:T(8,128)S(1)}, f32[1,512,1024]{2,1,0:T(8,128)S(1)}) conditional(s32[]{:T(128)} %bitcast.28, () %tuple.95, (f32[128,512]{1,0:T(8,128)S(1)}, bf16[128,512]{1,0:T(8,128)(2,1)}, f32[128,512]{1,0:T(8,128)S(1)}, bf16[128,512]{1,0:T(8,128)(2,1)}, f32[128,1024]{1,0:T(8,128)}, ...), branch_computations={%region_13.14_spmd, %region_14.15_spmd} | conditional | flops 11216 | bytes 4454656 | solution.py:88
  202.9 4.0 %collective-permute-done.16 = f32[24,128]{1,0:T(8,128)S(1)} collective-permute-done((f32[24,128]{1,0:T(8,128)S(1)}, f32[24,128]{1,0:T(8,128)S(1)}, u32[]{:S(2)}, u32[]{:S(2)}) %collective-permute-start.16) | collective-permute-done | bytes 12320 | tf_op jit(solution)/shard_map/cond/branch_1_fun/ppermute | solution.py:22
  206.9 4.1 %collective-permute-done.13.from_y = bf16[128,1024]{1,0:T(8,128)(2,1)S(1)} collective-permute-done((bf16[128,1024]{1,0:T(8,128)(2,1)S(1)}, bf16[128,1024]{1,0:T(8,128)(2,1)S(1)}, u32[]{:S(2)}, u32[]{:S(2)}) %collective-permute-start.13) | collective-permute-done | bytes 262176 | tf_op jit(solution)/shard_map/cond/branch_1_fun/ppermute | solution.py:17
  218.3 6.5 %conditional.15 = (bf16[512,1024]{1,0:T(8,128)(2,1)S(1)}, f32[256,1152]{1,0:T(8,128)}, f32[256,1152]{1,0:T(8,128)}, f32[1152,256]{1,0:T(8,128)}, f32[256]{0:T(25...) conditional(s32[]{:T(128)} %bitcast.28, () %tuple.117, (bf16[128,1024]{1,0:T(8,128)(2,1)S(1)}, ...), branch_computations={%region_16.17_spmd, %region_17.18_spmd} | conditional | flops 3000 | bytes 4590202 | solution.py:88
  220.1 3.7 %branch_1_fun.41 = (f32[256,1152]{1,0:T(8,128)}, f32[256,1152]{1,0:T(8,128)}, f32[1152,256]{1,0:T(8,128)}) custom-call(s32[5]{0:T(128)S(1)} %get-tuple-element.350.index, bf16[256,1792]{1,0:T(8,128)(2,1)} %get-tuple-element.353.mine, bf16[256,1792]{1,0:T(8,128)(2,1)} %get-tuple-element.354.other), custom_call_target="tpu_custom_call" | custom-call | flops 1000 | bytes 1000 | tf_op jit(solution)/shard_map/cond/branch_1_fun/pallas_call | solution.py:621
  (217 shorter events, 126.2 us)
Async XLA Ops:
  7.2 91.3 %all-gather.2.cloned.1.call-start = ((), (), s32[]{:S(2)}) async-start(), calls=%async_computation.2 | async-start | bytes 2949120 | tf_op jit(solution)/shard_map/all_gather | solution.py:720
  10.8 21.1 %collective-permute-start.47 = (bf16[272,384]{1,0:T(8,128)(2,1)S(1)}, bf16[272,384]{1,0:T(8,128)(2,1)S(1)}, u32[]{:S(2)}, u32[]{:S(2)}) collective-permute-start(bf16[272,384]{1,0:T(8,128)(2,1)S(1)} %get-tuple-element.499), channel_id=1, source_target_pairs={{0,24},{8,16},{16,8},{24,0},{1,25},{9,17},{17,9},{25,1},{2,26},{10... | collective-permute-start | bytes 626696 | tf_op jit(solution)/shard_map/ppermute | solution.py:72
  15.9 17.9 %collective-permute-start.46 = (bf16[272,384]{1,0:T(8,128)(2,1)S(1)}, bf16[272,384]{1,0:T(8,128)(2,1)}, u32[]{:S(2)}, u32[]{:S(2)}) collective-permute-start(bf16[272,384]{1,0:T(8,128)(2,1)S(1)} %get-tuple-element.499), channel_id=1, source_target_pairs={{0,16},{8,24},{16,0},{24,8},{1,17},{9,25},{17,1},{25,9},{2,18},{10... | collective-permute-start | bytes 626696 | tf_op jit(solution)/shard_map/ppermute | solution.py:72
  15.9 17.9 %collective-permute-start.45 = (bf16[272,384]{1,0:T(8,128)(2,1)S(1)}, bf16[272,384]{1,0:T(8,128)(2,1)}, u32[]{:S(2)}, u32[]{:S(2)}) collective-permute-start(bf16[272,384]{1,0:T(8,128)(2,1)S(1)} %get-tuple-element.499), channel_id=1, source_target_pairs={{0,8},{8,0},{16,24},{24,16},{1,9},{9,1},{17,25},{25,17},{2,10},{10... | collective-permute-start | bytes 626696 | tf_op jit(solution)/shard_map/ppermute | solution.py:72
  19.0 12.8 %collective-permute-start.21 = (bf16[256,1024]{1,0:T(8,128)(2,1)S(1)}, bf16[256,1024]{1,0:T(8,128)(2,1)}, u32[]{:S(2)}, u32[]{:S(2)}) collective-permute-start(bf16[256,1024]{1,0:T(8,128)(2,1)S(1)} %get-tuple-element.164), channel_id=1, source_target_pairs={{0,4},{4,0},{1,5},{5,1},{2,6},{6,2},{3,7},{7,3},{8,12},{12,8},{9,1... | collective-permute-start | bytes 1572872 | tf_op jit(solution)/shard_map/cond/branch_1_fun/ppermute | solution.py:17
  33.8 162.2 %reduce-scatter.3.cloned.1.call-start = ((), (), s32[]{:S(2)}) async-start(), calls=%async_computation.3 | async-start | bytes 4587520 | tf_op jit(solution)/shard_map/reduce_scatter | solution.py:782
  34.0 12.0 %collective-permute-start.48 = (bf16[256,640]{1,0:T(8,128)(2,1)S(1)}, bf16[256,640]{1,0:T(8,128)(2,1)S(1)}, u32[]{:S(2)}, u32[]{:S(2)}) collective-permute-start(bf16[256,640]{1,0:T(8,128)(2,1)S(1)} %get-tuple-element.526.rest_0_), channel_id=1, source_target_pairs={{0,8},{8,16},{16,24},{24,0},{1,9},{9,17},{17,25},{25,1},{2,10},{10... | collective-permute-start | bytes 983048 | tf_op jit(solution)/shard_map/ppermute | solution.py:79
  34.3 31.8 %collective-permute-start.49 = (bf16[256,1024]{1,0:T(8,128)(2,1)S(1)}, bf16[256,1024]{1,0:T(8,128)(2,1)}, u32[]{:S(2)}, u32[]{:S(2)}) collective-permute-start(bf16[256,1024]{1,0:T(8,128)(2,1)S(1)} %get-tuple-element.510.b0), channel_id=1, source_target_pairs={{0,4},{4,0},{1,5},{5,1},{2,6},{6,2},{3,7},{7,3},{8,12},{12,8},{9,1... | collective-permute-start | bytes 1572872 | tf_op jit(solution)/shard_map/ppermute | solution.py:17
  46.0 20.1 %collective-permute-start.50 = (bf16[256,640]{1,0:T(8,128)(2,1)S(1)}, bf16[256,640]{1,0:T(8,128)(2,1)S(1)}, u32[]{:S(2)}, u32[]{:S(2)}) collective-permute-start(bf16[256,640]{1,0:T(8,128)(2,1)S(1)} %collective-permute-done.48.rest_1_), channel_id=1, source_target_pairs={{0,8},{8,16},{16,24},{24,0},{1,9},{9,17},{17,25},{25,1},{2,10},{10... | collective-permute-start | bytes 983048 | tf_op jit(solution)/shard_map/ppermute | solution.py:79
  48.9 8.4 %collective-permute-start.1 = (bf16[256,512]{1,0:T(8,128)(2,1)S(1)}, bf16[256,512]{1,0:T(8,128)(2,1)S(1)}, u32[]{:S(2)}, u32[]{:S(2)}) collective-permute-start(bf16[256,512]{1,0:T(8,128)(2,1)S(1)} %get-tuple-element.209), channel_id=1, source_target_pairs={{0,4},{4,0},{1,5},{5,1},{2,6},{6,2},{3,7},{7,3},{8,12},{12,8},{9,1... | collective-permute-start | bytes 786440 | tf_op jit(solution)/shard_map/cond/branch_1_fun/ppermute | solution.py:17
  50.4 8.1 %collective-permute-start.2 = (bf16[256,512]{1,0:T(8,128)(2,1)S(1)}, bf16[256,512]{1,0:T(8,128)(2,1)S(1)}, u32[]{:S(2)}, u32[]{:S(2)}) collective-permute-start(bf16[256,512]{1,0:T(8,128)(2,1)S(1)} %get-tuple-element.211), channel_id=1, source_target_pairs={{0,2},{2,0},{1,3},{3,1},{4,6},{6,4},{5,7},{7,5},{8,10},{10,8},{9,1... | collective-permute-start | bytes 786440 | tf_op jit(solution)/shard_map/cond/branch_1_fun/ppermute | solution.py:17
  66.1 23.6 %collective-permute-start.51 = (bf16[256,640]{1,0:T(8,128)(2,1)S(1)}, bf16[256,640]{1,0:T(8,128)(2,1)S(1)}, u32[]{:S(2)}, u32[]{:S(2)}) collective-permute-start(bf16[256,640]{1,0:T(8,128)(2,1)S(1)} %collective-permute-done.50.rest_2_), channel_id=1, source_target_pairs={{0,8},{8,16},{16,24},{24,0},{1,9},{9,17},{17,25},{25,1},{2,10},{10... | collective-permute-start | bytes 983048 | tf_op jit(solution)/shard_map/ppermute | solution.py:79
  76.4 7.8 %collective-permute-start.26 = (bf16[2,128,512]{2,1,0:T(8,128)(2,1)S(1)}, bf16[2,128,512]{2,1,0:T(8,128)(2,1)S(1)}, u32[]{:S(2)}, u32[]{:S(2)}) collective-permute-start(bf16[2,128,512]{2,1,0:T(8,128)(2,1)S(1)} %get-tuple-element.611), channel_id=1, source_target_pairs={{0,2},{2,0},{1,3},{3,1},{4,6},{6,4},{5,7},{7,5},{8,10},{10,8},{9,1... | collective-permute-start | bytes 786440 | tf_op jit(solution)/shard_map/cond/branch_1_fun/ppermute | solution.py:17
  116.0 101.1 %reduce-scatter.5.cloned.1.call-start = ((), (), s32[]{:S(2)}) async-start(), calls=%async_computation.4 | async-start | bytes 983040 | tf_op jit(solution)/shard_map/reduce_scatter | solution.py:831
  122.1 8.4 %collective-permute-start.30 = (bf16[256,512]{1,0:T(8,128)(2,1)S(1)}, bf16[256,512]{1,0:T(8,128)(2,1)S(1)}, u32[]{:S(2)}, u32[]{:S(2)}) collective-permute-start(bf16[256,512]{1,0:T(8,128)(2,1)S(1)} %get-tuple-element.228), channel_id=1, source_target_pairs={{0,4},{4,0},{1,5},{5,1},{2,6},{6,2},{3,7},{7,3},{8,12},{12,8},{9,1... | collective-permute-start | bytes 786440 | tf_op jit(solution)/shard_map/cond/branch_1_fun/ppermute | solution.py:17
  123.6 8.1 %collective-permute-start.31 = (bf16[256,512]{1,0:T(8,128)(2,1)S(1)}, bf16[256,512]{1,0:T(8,128)(2,1)S(1)}, u32[]{:S(2)}, u32[]{:S(2)}) collective-permute-start(bf16[256,512]{1,0:T(8,128)(2,1)S(1)} %get-tuple-element.230), channel_id=1, source_target_pairs={{0,2},{2,0},{1,3},{3,1},{4,6},{6,4},{5,7},{7,5},{8,10},{10,8},{9,1... | collective-permute-start | bytes 786440 | tf_op jit(solution)/shard_map/cond/branch_1_fun/ppermute | solution.py:17
  156.0 13.6 %collective-permute-start.40 = (bf16[256,512]{1,0:T(8,128)(2,1)S(1)}, bf16[256,512]{1,0:T(8,128)(2,1)S(1)}, u32[]{:S(2)}, u32[]{:S(2)}) collective-permute-start(bf16[256,512]{1,0:T(8,128)(2,1)S(1)} %get-tuple-element.270), channel_id=1, source_target_pairs={{0,4},{4,0},{1,5},{5,1},{2,6},{6,2},{3,7},{7,3},{8,12},{12,8},{9,1... | collective-permute-start | bytes 786440 | tf_op jit(solution)/shard_map/cond/branch_1_fun/ppermute | solution.py:17
  158.1 11.5 %collective-permute-start.41 = (bf16[256,512]{1,0:T(8,128)(2,1)S(1)}, bf16[256,512]{1,0:T(8,128)(2,1)S(1)}, u32[]{:S(2)}, u32[]{:S(2)}) collective-permute-start(bf16[256,512]{1,0:T(8,128)(2,1)S(1)} %get-tuple-element.272), channel_id=1, source_target_pairs={{0,2},{2,0},{1,3},{3,1},{4,6},{6,4},{5,7},{7,5},{8,10},{10,8},{9,1... | collective-permute-start | bytes 786440 | tf_op jit(solution)/shard_map/cond/branch_1_fun/ppermute | solution.py:17
  181.5 8.4 %collective-permute-start.6 = (bf16[256,512]{1,0:T(8,128)(2,1)S(1)}, bf16[256,512]{1,0:T(8,128)(2,1)S(1)}, u32[]{:S(2)}, u32[]{:S(2)}) collective-permute-start(bf16[256,512]{1,0:T(8,128)(2,1)S(1)} %get-tuple-element.301), channel_id=1, source_target_pairs={{0,4},{4,0},{1,5},{5,1},{2,6},{6,2},{3,7},{7,3},{8,12},{12,8},{9,1... | collective-permute-start | bytes 786440 | tf_op jit(solution)/shard_map/cond/branch_1_fun/ppermute | solution.py:17
  182.2 8.1 %collective-permute-start.7 = (bf16[256,512]{1,0:T(8,128)(2,1)S(1)}, bf16[256,512]{1,0:T(8,128)(2,1)S(1)}, u32[]{:S(2)}, u32[]{:S(2)}) collective-permute-start(bf16[256,512]{1,0:T(8,128)(2,1)S(1)} %get-tuple-element.303), channel_id=1, source_target_pairs={{0,2},{2,0},{1,3},{3,1},{4,6},{6,4},{5,7},{7,5},{8,10},{10,8},{9,1... | collective-permute-start | bytes 786440 | tf_op jit(solution)/shard_map/cond/branch_1_fun/ppermute | solution.py:17
  196.0 21.0 %collective-permute-start.52 = (bf16[256,1792]{1,0:T(8,128)(2,1)}, bf16[256,1792]{1,0:T(8,128)(2,1)}, u32[]{:S(2)}, u32[]{:S(2)}) collective-permute-start(bf16[256,1792]{1,0:T(8,128)(2,1)} %reduce-scatter.3.cloned.1.call-done), channel_id=1, source_target_pairs={{0,4},{4,0},{1,5},{5,1},{2,6},{6,2},{3,7},{7,3},{8,12},{12,8},{9,1... | collective-permute-start | bytes 2752520 | tf_op jit(solution)/shard_map/ppermute | solution.py:17
  199.0 7.9 %collective-permute-start.15 = (bf16[128,1024]{1,0:T(8,128)(2,1)S(1)}, bf16[128,1024]{1,0:T(8,128)(2,1)}, u32[]{:S(2)}, u32[]{:S(2)}) collective-permute-start(bf16[128,1024]{1,0:T(8,128)(2,1)S(1)} %get-tuple-element.341), channel_id=1, source_target_pairs={{0,2},{2,0},{1,3},{3,1},{4,6},{6,4},{5,7},{7,5},{8,10},{10,8},{9,1... | collective-permute-start | bytes 786440 | tf_op jit(solution)/shard_map/cond/branch_1_fun/ppermute | solution.py:17
  201.4 9.6 %collective-permute-start.13 = (bf16[128,1024]{1,0:T(8,128)(2,1)S(1)}, bf16[128,1024]{1,0:T(8,128)(2,1)S(1)}, u32[]{:S(2)}, u32[]{:S(2)}) collective-permute-start(bf16[128,1024]{1,0:T(8,128)(2,1)S(1)} %branch_1_fun.39.own), channel_id=1, source_target_pairs={{0,2},{2,0},{1,3},{3,1},{4,6},{6,4},{5,7},{7,5},{8,10},{10,8},{9,1... | collective-permute-start | bytes 786440 | tf_op jit(solution)/shard_map/cond/branch_1_fun/ppermute | solution.py:17
  217.1 7.8 %collective-permute-start.53 = (bf16[256,384]{1,0:T(8,128)(2,1)}, bf16[256,384]{1,0:T(8,128)(2,1)S(1)}, u32[]{:S(2)}, u32[]{:S(2)}) collective-permute-start(bf16[256,384]{1,0:T(8,128)(2,1)} %reduce-scatter.5.cloned.1.call-done.mine), channel_id=1, source_target_pairs={{0,4},{4,0},{1,5},{5,1},{2,6},{6,2},{3,7},{7,3},{8,12},{12,8},{9,1... | collective-permute-start | bytes 589832 | tf_op jit(solution)/shard_map/ppermute | solution.py:17
  (65 other events, 338.8 us)
Sparse Core Ops, SparseCore 0:
  33.9 64.5 all-gather.1
  116.1 69.7 reduce-scatter.2
  188.2 23.9 reduce-scatter.4

commit v3 on v2

--- a/solution.py
+++ b/solution.py
@@ -84,8 +84,18 @@
 
 
 def region(flag, work, *args):
-    shapes = jax.eval_shape(work, *args)
-    return lax.cond(flag, work, lambda *_: jax.tree.map(lambda x: jnp.zeros(x.shape, x.dtype), shapes), *args)
+    leaves, tree = jax.tree.flatten(jax.eval_shape(work, *args))
+
+    def otherwise(*_):
+        hbm = pl.BlockSpec(memory_space=pl.ANY)
+        outs = pl.pallas_call(
+            lambda *refs: None,
+            out_shape=[jax.ShapeDtypeStruct(leaf.shape, leaf.dtype) for leaf in leaves],
+            out_specs=[hbm] * len(leaves),
+        )()
+        return jax.tree.unflatten(tree, outs)
+
+    return lax.cond(flag, work, otherwise, *args)
 
 
 def lanes(shape):
@@ -287,35 +297,30 @@
     main = gate_up.shape[1] // 2 // 128 * 128
     both = 2 * main
     wide = both + 128
-    low = lanes((pair, 128)) < HD
-    row = lax.broadcasted_iota(jnp.int32, (pair, 1), 0)
+    low = lanes((four, 128)) < HD
+    row = lax.broadcasted_iota(jnp.int32, (four, 1), 0)
     bs = (b0, b1, b2, b3)
     for kk, (x, to) in enumerate(((x_low, second_low), (x_high, second_high))):
-
-        @pl.loop(0, 2)
-        def _(xx, kk=kk, x=x, to=to):
-            some = pl.ds(pl.multiple_of(xx * pair, pair), pair)
-            here = pl.ds(pl.multiple_of(kk * four + xx * pair, pair), pair)
-            start = own ^ (kk + 4 * xx + jnp.where(row >= block, 2, 0))
-            ok = start * block + row % block < length
-            gu = nn(x[some, :], gu_w[...])
-            back = back_all[here, :]
-            tail = gu[:, both:]
-            gate = jnp.concatenate([gu[:, :main], tail], 1)
-            upper = jnp.concatenate([gu[:, main:both], pltpu.roll(tail, HD, 1)], 1)
-            sigmoid = 1.0 / (1.0 + jnp.exp(-gate))
-            silu = gate * sigmoid
-            act = jnp.where(ok, silu * upper, 0.0)
-            gate_back = back * upper * (sigmoid + silu * (1.0 - sigmoid))
-            upper_back = back * silu
-            activated[here, :main] = act[:, :main].astype(BF16)
-            activated[here, main:] = jnp.where(low, act[:, main:], 0.0).astype(BF16)
-            mix = jnp.where(low, gate_back[:, main:], pltpu.roll(upper_back[:, main:], HD, 1))
-            gate_up[here, :main] = gate_back[:, :main].astype(BF16)
-            gate_up[here, main:both] = upper_back[:, :main].astype(BF16)
-            gate_up[here, both:] = mix.astype(BF16)
-            to[some, :] = nt(gate_up[here, :], gu_w[...]).astype(BF16)
-
+        here = slice(kk * four, (kk + 1) * four)
+        start = own ^ (kk + jnp.where(row >= pair, 4, 0) + jnp.where(row % pair >= block, 2, 0))
+        ok = start * block + row % block < length
+        gu = nn(x[...], gu_w[...])
+        back = back_all[here, :]
+        tail = gu[:, both:]
+        gate = jnp.concatenate([gu[:, :main], tail], 1)
+        upper = jnp.concatenate([gu[:, main:both], pltpu.roll(tail, HD, 1)], 1)
+        sigmoid = 1.0 / (1.0 + jnp.exp(-gate))
+        silu = gate * sigmoid
+        act = jnp.where(ok, silu * upper, 0.0)
+        gate_back = back * upper * (sigmoid + silu * (1.0 - sigmoid))
+        upper_back = back * silu
+        activated[here, :main] = act[:, :main].astype(BF16)
+        activated[here, main:] = jnp.where(low, act[:, main:], 0.0).astype(BF16)
+        mix = jnp.where(low, gate_back[:, main:], pltpu.roll(upper_back[:, main:], HD, 1))
+        gate_up[here, :main] = gate_back[:, :main].astype(BF16)
+        gate_up[here, main:both] = upper_back[:, :main].astype(BF16)
+        gate_up[here, both:] = mix.astype(BF16)
+        to[...] = nt(gate_up[here, :], gu_w[...]).astype(BF16)
     step = 256
 
     @pl.loop(0, width // step)

time: 234 us -> 233 us (level)
    unnamed x38 -> x40, local copies, waits for them, and re-layouts: 5.53 us -> 5.79 us
where the time goes in v3:
time: 233 us; the launch traced here: 232 us
  waiting for transfers between devices  82.1 us (35%)
  Pallas kernels  70.7 us (30%)
  starting transfers between devices  52.2 us (22%)
  between operations  14.6 us (6%)
  local copies, waits for them, and re-layouts  7.64 us (3%)
  other arithmetic  4.56 us (2%)
    pallas_call x26, Pallas kernels, call(): pl.pallas_call(kernel, out_shape=[jax.ShapeDtypeStruct(shape, kind) for s...  70.7 us
    ppermute x43, waiting for transfers between devices, swap(): return lax.ppermute(value, axis, [(0, 1), (1, 0)])  68.2 us
    ppermute x43, starting transfers between devices, swap(): return lax.ppermute(value, axis, [(0, 1), (1, 0)])  34.7 us
    ppermute x5, waiting for transfers between devices, hop(): return lax.ppermute(value, axis, [(i, i ^ step) for i in range(size)])  9.43 us
    ppermute x5, starting transfers between devices, hop(): return lax.ppermute(value, axis, [(i, i ^ step) for i in range(size)])  6.5 us
    unnamed x40, local copies, waits for them, and re-layouts  5.79 us
    ppermute x3, starting transfers between devices, direct(): lax.ppermute(piece, 'fsdp', [(i, i ^ step) for i in range(size)])  5.76 us
    ppermute x3, starting transfers between devices, onward(): lax.ppermute(value, 'fsdp', [(i, (i + 1) % size) for i in range(size)])  5.12 us
  transfers between devices with their start and end apart: 57, of which 35 were waited for; matrix products, arithmetic and copies ran while one was open for 2% of the time, Pallas kernels for 22%

profile of v3, /device:TPU:0, one launch (start us, length us, event | category | flops | bytes accessed | tf_op | source)
XLA Modules:
  0.0 232.0 jit_solution(9545413262257764452)
XLA Ops:
  10.0 5.1 %collective-permute-start.47 = (bf16[272,384]{1,0:T(8,128)(2,1)S(1)}, bf16[272,384]{1,0:T(8,128)(2,1)S(1)}, u32[]{:S(2)}, u32[]{:S(2)}) collective-permute-start(bf16[272,384]{1,0:T(8,128)(2,1)S(1)} %get-tuple-element.505), channel_id=1, source_target_pairs={{0,24},{8,16},{16,8},{24,0},{1,25},{9,17},{17,9},{25,1},{2,26},{10... | collective-permute-start | bytes 626696 | tf_op jit(solution)/shard_map/ppermute | solution.py:72
  15.8 15.3 %conditional.8 = ((bf16[256,1024]{1,0:T(8,128)(2,1)}, bf16[256,1152]{1,0:T(8,128)(2,1)}, bf16[256,640]{1,0:T(8,128)(2,1)S(1)}, f32[1024,128]{1,0:T(8,128)}, f32[...) conditional(s32[]{:T(128)} %bitcast.29, () %tuple.94, ...), branch_computations={%region_0.0_spmd, %region_1.2_spmd} | conditional | flops 267808 | bytes 3195552 | solution.py:98
  25.2 5.8 %collective-permute-done.21 = bf16[256,1024]{1,0:T(8,128)(2,1)} collective-permute-done((bf16[256,1024]{1,0:T(8,128)(2,1)S(1)}, bf16[256,1024]{1,0:T(8,128)(2,1)}, u32[]{:S(2)}, u32[]{:S(2)}) %collective-permute-start.21) | collective-permute-done | bytes 524320 | tf_op jit(solution)/shard_map/cond/branch_1_fun/ppermute | solution.py:17
  35.8 9.9 %conditional.9 = ((bf16[512,1024]{1,0:T(8,128)(2,1)S(1)}, bf16[512,1024]{1,0:T(8,128)(2,1)}, f32[8,1024]{1,0:T(8,128)S(1)}, bf16[1024,1024]{1,0:T(8,128)(2,1)}, ...) conditional(s32[]{:T(128)} %bitcast.29, () %tuple.93, ...), branch_computations={%region_2.3_spmd, %region_3.4_spmd} | conditional | flops 8000001024 | bytes 2098284 | solution.py:98
  36.6 9.1 %branch_1_fun.23 = (bf16[1024,384]{1,0:T(8,128)(2,1)}, f32[8,1024]{1,0:T(8,128)S(1)}, bf16[512,1024]{1,0:T(8,128)(2,1)S(1)}, bf16[512,1024]{1,0:T(8,128)(2,1)}, ...) custom-call(s32[5]{0:T(128)S(1)} %get-tuple-element.184.index, ...), custom_call_target="tpu_custom_call" | custom-call | flops 8000001024 | bytes 1000 | tf_op jit(solution)/shard_map/cond/branch_1_fun/pallas_call | solution.py:626
  45.9 20.3 %conditional.10 = ((f32[128,1024]{1,0:T(8,128)}, f32[128,128]{1,0:T(8,128)S(1)}, bf16[128,512]{1,0:T(8,128)(2,1)S(1)}, bf16[128,512]{1,0:T(8,128)(2,1)S(1)})) conditional(s32[]{:T(128)} %bitcast.29, () %tuple.92, (bf16[512,1024]{1,0:T(8,128)(2,1)}, bf16[512,1024]{1,0:T(8,128)(2,1)S(1)}, bf16[256,1024]{1,0:T(8,128)(2,1)S(1)}, ...), branch_computations={%region_4.5_spmd, %region_5.6_spmd} | conditional | flops 3000 | bytes 7343240 | solution.py:98
  52.1 5.3 %collective-permute-done.1.from_x = bf16[256,512]{1,0:T(8,128)(2,1)S(1)} collective-permute-done((bf16[256,512]{1,0:T(8,128)(2,1)S(1)}, bf16[256,512]{1,0:T(8,128)(2,1)S(1)}, u32[]{:S(2)}, u32[]{:S(2)}) %collective-permute-start.1) | collective-permute-done | bytes 262176 | tf_op jit(solution)/shard_map/cond/branch_1_fun/ppermute | solution.py:17
  66.2 5.1 %collective-permute-start.51 = (bf16[256,640]{1,0:T(8,128)(2,1)S(1)}, bf16[256,640]{1,0:T(8,128)(2,1)S(1)}, u32[]{:S(2)}, u32[]{:S(2)}) collective-permute-start(bf16[256,640]{1,0:T(8,128)(2,1)S(1)} %collective-permute-done.50.rest_2_), channel_id=1, source_target_pairs={{0,8},{8,16},{16,24},{24,0},{1,9},{9,17},{17,25},{25,1},{2,10},{10... | collective-permute-start | bytes 983048 | tf_op jit(solution)/shard_map/ppermute | solution.py:79
  71.3 19.2 %conditional.11 = ((bf16[512,1024]{1,0:T(8,128)(2,1)}, bf16[512,1024]{1,0:T(8,128)(2,1)}, bf16[256,1024]{1,0:T(8,128)(2,1)})) conditional(s32[]{:T(128)} %bitcast.29, () %tuple.91, (bf16[128,512]{1,0:T(8,128)(2,1)S(1)}, bf16[256,1024]{1,0:T(8,128)(2,1)}, bf16[128,512]{1,0:T(8,128)(2,1)S(1)}) %tuple.101), branch_computations={%region_6.7_spmd, %region_7.8_spmd} | conditional | flops 4456448 | bytes 13107472 | solution.py:98
  72.5 4.7 %collective-permute-done.24 = bf16[128,512]{1,0:T(8,128)(2,1)S(1)} collective-permute-done((bf16[128,512]{1,0:T(8,128)(2,1)S(1)}, bf16[128,512]{1,0:T(8,128)(2,1)S(1)}, u32[]{:S(2)}, u32[]{:S(2)}) %collective-permute-start.24) | collective-permute-done | bytes 131104 | tf_op jit(solution)/shard_map/cond/branch_1_fun/ppermute | solution.py:17
  80.4 5.0 %collective-permute-done.26 = bf16[2,128,512]{2,1,0:T(8,128)(2,1)S(1)} collective-permute-done((bf16[2,128,512]{2,1,0:T(8,128)(2,1)S(1)}, bf16[2,128,512]{2,1,0:T(8,128)(2,1)S(1)}, u32[]{:S(2)}, u32[]{:S(2)}) %collective-permute-start.26) | collective-permute-done | bytes 262176 | tf_op jit(solution)/shard_map/cond/branch_1_fun/ppermute | solution.py:17
  92.2 3.5 %shard_map.260 = (bf16[1024,640]{1,0:T(8,128)(2,1)}, f32[1024,640]{1,0:T(8,128)S(1)}) custom-call(s32[5]{0:T(128)S(1)} %stack.93.index, bf16[256,1024]{1,0:T(8,128)(2,1)} %copy-done.7, bf16[256,1024]{1,0:T(8,128)(2,1)} %collective-permute-done.49.b1, bf16[256,1024]{1,0:T(8,128)(2,1)} %get-tuple-element.529.b2, bf16[256,1024]{1,0:T(8,128)(2,1)} %get-tuple-element.530.b3, ...), custom_call_target="tpu_custom_call" | custom-call | flops 1000 | bytes 1000 | tf_op jit(solution)/shard_map/pallas_call | solution.py:626
  99.9 15.3 %shard_map.261 = (bf16[512,1024]{1,0:T(8,128)(2,1)}, bf16[512,1024]{1,0:T(8,128)(2,1)}, bf16[1024,1792]{1,0:T(8,128)(2,1)}, bf16[1024,640]{1,0:T(8,128)(2,1)}) custom-call(s32[5]{0:T(128)S(1)} %stack.93.index, bf16[512,1024]{1,0:T(8,128)(2,1)} %get-tuple-element.527.x_low, bf16[512,1024]{1,0:T(8,128)(2,1)} %get-tuple-element.528.x_high, ...), custom_call_target="tpu_custom_call" | custom-call | flops 1000 | bytes 1000 | tf_op jit(solution)/shard_map/pallas_call | solution.py:626
  117.0 58.4 %conditional.12 = ((bf16[512,1024]{1,0:T(8,128)(2,1)}, bf16[512,1024]{1,0:T(8,128)(2,1)}, bf16[1024,384]{1,0:T(8,128)(2,1)}, f32[8,1024]{1,0:T(8,128)S(1)}, f32[...) conditional(s32[]{:T(128)} %bitcast.29, () %tuple.90, ...), branch_computations={%region_8.9_spmd, %region_9.10_spmd} | conditional | flops 4464448 | bytes 54010640 | solution.py:98
  123.2 4.1 %branch_1_fun.28 = (bf16[512,1024]{1,0:T(8,128)(2,1)S(1)}, bf16[512,1024]{1,0:T(8,128)(2,1)S(1)}) custom-call(s32[5]{0:T(128)S(1)} %get-tuple-element.227.index, bf16[1024,640]{1,0:T(8,128)(2,1)} %get-tuple-element.234.activated, bf16[1024,640]{1,0:T(8,128)(2,1)S(1)} %copy-done.11), custom_call_target="tpu_custom_call" | custom-call | flops 1000 | bytes 1000 | tf_op jit(solution)/shard_map/cond/branch_1_fun/pallas_call | solution.py:626
  139.0 4.0 %collective-permute-done.34 = bf16[128,512]{1,0:T(8,128)(2,1)S(1)} collective-permute-done((bf16[128,512]{1,0:T(8,128)(2,1)S(1)}, bf16[128,512]{1,0:T(8,128)(2,1)S(1)}, u32[]{:S(2)}, u32[]{:S(2)}) %collective-permute-start.34) | collective-permute-done | bytes 131104 | tf_op jit(solution)/shard_map/cond/branch_1_fun/ppermute | solution.py:17
  156.6 11.3 %branch_1_fun.31 = (bf16[512,1024]{1,0:T(8,128)(2,1)}, bf16[512,1024]{1,0:T(8,128)(2,1)}, bf16[1024,256]{1,0:T(8,128)(2,1)S(1)}, f32[8,128]{1,0:T(8,128)S(1)}) custom-call(s32[5]{0:T(128)S(1)} %get-tuple-element.227.index, bf16[512,1024]{1,0:T(8,128)(2,1)S(1)} %bitcast.49, bf16[512,1024]{1,0:T(8,128)(2,1)S(1)} %collective-permute-done.38.a_high, ...), custom_call_target="tpu_custom_call" | custom-call | flops 1000 | bytes 1000 | tf_op jit(solution)/shard_map/cond/branch_1_fun/pallas_call | solution.py:626
  175.4 19.5 %conditional.13 = ((f32[128,512]{1,0:T(8,128)S(1)}, bf16[128,512]{1,0:T(8,128)(2,1)}, f32[128,512]{1,0:T(8,128)}, bf16[128,512]{1,0:T(8,128)(2,1)}, f32[24,128]{...) conditional(s32[]{:T(128)} %bitcast.29, () %tuple.89, (bf16[512,1024]{1,0:T(8,128)(2,1)}, ...), branch_computations={%region_10.11_spmd, %region_11.12_spmd} | conditional | flops 10144 | bytes 7516400 | solution.py:98
  184.2 4.1 %collective-permute-done.6.from_x = bf16[256,512]{1,0:T(8,128)(2,1)S(1)} collective-permute-done((bf16[256,512]{1,0:T(8,128)(2,1)S(1)}, bf16[256,512]{1,0:T(8,128)(2,1)S(1)}, u32[]{:S(2)}, u32[]{:S(2)}) %collective-permute-start.6) | collective-permute-done | bytes 262176 | tf_op jit(solution)/shard_map/cond/branch_1_fun/ppermute | solution.py:17
  191.6 3.3 %collective-permute-done.11 = f32[24,128]{1,0:T(8,128)S(1)} collective-permute-done((f32[24,128]{1,0:T(8,128)S(1)}, f32[24,128]{1,0:T(8,128)S(1)}, u32[]{:S(2)}, u32[]{:S(2)}) %collective-permute-start.11) | collective-permute-done | bytes 12320 | tf_op jit(solution)/shard_map/cond/branch_1_fun/ppermute | solution.py:22
  196.5 20.6 %conditional.14 = (bf16[128,1024]{1,0:T(8,128)(2,1)}, f32[24,128]{1,0:T(8,128)S(1)}, f32[1,512,1024]{2,1,0:T(8,128)}) conditional(s32[]{:T(128)} %bitcast.29, () %tuple.88, (f32[128,512]{1,0:T(8,128)S(1)}, bf16[128,512]{1,0:T(8,128)(2,1)}, f32[128,512]{1,0:T(8,128)}, bf16[128,512]{1,0:T(8,128)(2,1)}, f32[128,1024]{1,0:T(8,128)}, ...), branch_computations={%region_13.14_spmd, %region_14.15_spmd} | conditional | flops 11216 | bytes 4454656 | solution.py:98
  205.9 4.2 %collective-permute-done.13.from_y = bf16[128,1024]{1,0:T(8,128)(2,1)S(1)} collective-permute-done((bf16[128,1024]{1,0:T(8,128)(2,1)S(1)}, bf16[128,1024]{1,0:T(8,128)(2,1)S(1)}, u32[]{:S(2)}, u32[]{:S(2)}) %collective-permute-start.13) | collective-permute-done | bytes 262176 | tf_op jit(solution)/shard_map/cond/branch_1_fun/ppermute | solution.py:17
  210.0 3.4 %collective-permute-start.18 = (f32[24,128]{1,0:T(8,128)S(1)}, f32[24,128]{1,0:T(8,128)S(1)}, u32[]{:S(2)}, u32[]{:S(2)}) collective-permute-start(f32[24,128]{1,0:T(8,128)S(1)} %add.55), channel_id=1, source_target_pairs={{0,16},{8,24},{16,0},{24,8},{1,17},{9,25},{17,1},{25,9},{2,18},{10... | collective-permute-start | bytes 36872 | tf_op jit(solution)/shard_map/cond/branch_1_fun/ppermute | solution.py:22
  218.0 5.6 %conditional.15 = ((bf16[512,1024]{1,0:T(8,128)(2,1)S(1)}, f32[256,1152]{1,0:T(8,128)}, f32[256,1152]{1,0:T(8,128)}, f32[1152,256]{1,0:T(8,128)}, f32[256]{0:T(2...) conditional(s32[]{:T(128)} %bitcast.29, () %tuple.110, (bf16[128,1024]{1,0:T(8,128)(2,1)S(1)}, ...), branch_computations={%region_16.17_spmd, %region_17.18_spmd} | conditional | flops 3000 | bytes 2100312 | solution.py:98
  (215 shorter events, 123.8 us)
Async XLA Ops:
  7.2 91.1 %all-gather.2.cloned.1.call-start = ((), (), s32[]{:S(2)}) async-start(), calls=%async_computation.2 | async-start | bytes 2949120 | tf_op jit(solution)/shard_map/all_gather | solution.py:725
  10.0 21.0 %collective-permute-start.47 = (bf16[272,384]{1,0:T(8,128)(2,1)S(1)}, bf16[272,384]{1,0:T(8,128)(2,1)S(1)}, u32[]{:S(2)}, u32[]{:S(2)}) collective-permute-start(bf16[272,384]{1,0:T(8,128)(2,1)S(1)} %get-tuple-element.505), channel_id=1, source_target_pairs={{0,24},{8,16},{16,8},{24,0},{1,25},{9,17},{17,9},{25,1},{2,26},{10... | collective-permute-start | bytes 626696 | tf_op jit(solution)/shard_map/ppermute | solution.py:72
  15.2 17.7 %collective-permute-start.46 = (bf16[272,384]{1,0:T(8,128)(2,1)S(1)}, bf16[272,384]{1,0:T(8,128)(2,1)S(1)}, u32[]{:S(2)}, u32[]{:S(2)}) collective-permute-start(bf16[272,384]{1,0:T(8,128)(2,1)S(1)} %get-tuple-element.505), channel_id=1, source_target_pairs={{0,16},{8,24},{16,0},{24,8},{1,17},{9,25},{17,1},{25,9},{2,18},{10... | collective-permute-start | bytes 626696 | tf_op jit(solution)/shard_map/ppermute | solution.py:72
  15.2 17.7 %collective-permute-start.45 = (bf16[272,384]{1,0:T(8,128)(2,1)S(1)}, bf16[272,384]{1,0:T(8,128)(2,1)S(1)}, u32[]{:S(2)}, u32[]{:S(2)}) collective-permute-start(bf16[272,384]{1,0:T(8,128)(2,1)S(1)} %get-tuple-element.505), channel_id=1, source_target_pairs={{0,8},{8,0},{16,24},{24,16},{1,9},{9,1},{17,25},{25,17},{2,10},{10... | collective-permute-start | bytes 626696 | tf_op jit(solution)/shard_map/ppermute | solution.py:72
  18.3 12.8 %collective-permute-start.21 = (bf16[256,1024]{1,0:T(8,128)(2,1)S(1)}, bf16[256,1024]{1,0:T(8,128)(2,1)}, u32[]{:S(2)}, u32[]{:S(2)}) collective-permute-start(bf16[256,1024]{1,0:T(8,128)(2,1)S(1)} %get-tuple-element.167), channel_id=1, source_target_pairs={{0,4},{4,0},{1,5},{5,1},{2,6},{6,2},{3,7},{7,3},{8,12},{12,8},{9,1... | collective-permute-start | bytes 1572872 | tf_op jit(solution)/shard_map/cond/branch_1_fun/ppermute | solution.py:17
  33.0 162.1 %reduce-scatter.3.cloned.1.call-start = ((), (), s32[]{:S(2)}) async-start(), calls=%async_computation.3 | async-start | bytes 4587520 | tf_op jit(solution)/shard_map/reduce_scatter | solution.py:787
  33.7 12.1 %collective-permute-start.48 = (bf16[256,640]{1,0:T(8,128)(2,1)S(1)}, bf16[256,640]{1,0:T(8,128)(2,1)S(1)}, u32[]{:S(2)}, u32[]{:S(2)}) collective-permute-start(bf16[256,640]{1,0:T(8,128)(2,1)S(1)} %get-tuple-element.532.rest_0_), channel_id=1, source_target_pairs={{0,8},{8,16},{16,24},{24,0},{1,9},{9,17},{17,25},{25,1},{2,10},{10... | collective-permute-start | bytes 983048 | tf_op jit(solution)/shard_map/ppermute | solution.py:79
  33.7 32.5 %collective-permute-start.49 = (bf16[256,1024]{1,0:T(8,128)(2,1)S(1)}, bf16[256,1024]{1,0:T(8,128)(2,1)}, u32[]{:S(2)}, u32[]{:S(2)}) collective-permute-start(bf16[256,1024]{1,0:T(8,128)(2,1)S(1)} %get-tuple-element.516.b0), channel_id=1, source_target_pairs={{0,4},{4,0},{1,5},{5,1},{2,6},{6,2},{3,7},{7,3},{8,12},{12,8},{9,1... | collective-permute-start | bytes 1572872 | tf_op jit(solution)/shard_map/ppermute | solution.py:17
  45.8 20.4 %collective-permute-start.50 = (bf16[256,640]{1,0:T(8,128)(2,1)S(1)}, bf16[256,640]{1,0:T(8,128)(2,1)S(1)}, u32[]{:S(2)}, u32[]{:S(2)}) collective-permute-start(bf16[256,640]{1,0:T(8,128)(2,1)S(1)} %collective-permute-done.48.rest_1_), channel_id=1, source_target_pairs={{0,8},{8,16},{16,24},{24,0},{1,9},{9,17},{17,25},{25,1},{2,10},{10... | collective-permute-start | bytes 983048 | tf_op jit(solution)/shard_map/ppermute | solution.py:79
  49.0 8.4 %collective-permute-start.1 = (bf16[256,512]{1,0:T(8,128)(2,1)S(1)}, bf16[256,512]{1,0:T(8,128)(2,1)S(1)}, u32[]{:S(2)}, u32[]{:S(2)}) collective-permute-start(bf16[256,512]{1,0:T(8,128)(2,1)S(1)} %get-tuple-element.212), channel_id=1, source_target_pairs={{0,4},{4,0},{1,5},{5,1},{2,6},{6,2},{3,7},{7,3},{8,12},{12,8},{9,1... | collective-permute-start | bytes 786440 | tf_op jit(solution)/shard_map/cond/branch_1_fun/ppermute | solution.py:17
  50.6 8.1 %collective-permute-start.2 = (bf16[256,512]{1,0:T(8,128)(2,1)S(1)}, bf16[256,512]{1,0:T(8,128)(2,1)S(1)}, u32[]{:S(2)}, u32[]{:S(2)}) collective-permute-start(bf16[256,512]{1,0:T(8,128)(2,1)S(1)} %get-tuple-element.214), channel_id=1, source_target_pairs={{0,2},{2,0},{1,3},{3,1},{4,6},{6,4},{5,7},{7,5},{8,10},{10,8},{9,1... | collective-permute-start | bytes 786440 | tf_op jit(solution)/shard_map/cond/branch_1_fun/ppermute | solution.py:17
  66.2 24.3 %collective-permute-start.51 = (bf16[256,640]{1,0:T(8,128)(2,1)S(1)}, bf16[256,640]{1,0:T(8,128)(2,1)S(1)}, u32[]{:S(2)}, u32[]{:S(2)}) collective-permute-start(bf16[256,640]{1,0:T(8,128)(2,1)S(1)} %collective-permute-done.50.rest_2_), channel_id=1, source_target_pairs={{0,8},{8,16},{16,24},{24,0},{1,9},{9,17},{17,25},{25,1},{2,10},{10... | collective-permute-start | bytes 983048 | tf_op jit(solution)/shard_map/ppermute | solution.py:79
  77.2 8.1 %collective-permute-start.26 = (bf16[2,128,512]{2,1,0:T(8,128)(2,1)S(1)}, bf16[2,128,512]{2,1,0:T(8,128)(2,1)S(1)}, u32[]{:S(2)}, u32[]{:S(2)}) collective-permute-start(bf16[2,128,512]{2,1,0:T(8,128)(2,1)S(1)} %get-tuple-element.617), channel_id=1, source_target_pairs={{0,2},{2,0},{1,3},{3,1},{4,6},{6,4},{5,7},{7,5},{8,10},{10,8},{9,1... | collective-permute-start | bytes 786440 | tf_op jit(solution)/shard_map/cond/branch_1_fun/ppermute | solution.py:17
  78.6 7.8 %collective-permute-start.27 = (bf16[2,128,512]{2,1,0:T(8,128)(2,1)S(1)}, bf16[2,128,512]{2,1,0:T(8,128)(2,1)S(1)}, u32[]{:S(2)}, u32[]{:S(2)}) collective-permute-start(bf16[2,128,512]{2,1,0:T(8,128)(2,1)S(1)} %get-tuple-element.619), channel_id=1, source_target_pairs={{0,4},{4,0},{1,5},{5,1},{2,6},{6,2},{3,7},{7,3},{8,12},{12,8},{9,1... | collective-permute-start | bytes 786440 | tf_op jit(solution)/shard_map/cond/branch_1_fun/ppermute | solution.py:17
  115.3 101.8 %reduce-scatter.5.cloned.1.call-start = ((), (), s32[]{:S(2)}) async-start(), calls=%async_computation.4 | async-start | bytes 983040 | tf_op jit(solution)/shard_map/reduce_scatter | solution.py:836
  120.1 8.4 %collective-permute-start.30 = (bf16[256,512]{1,0:T(8,128)(2,1)S(1)}, bf16[256,512]{1,0:T(8,128)(2,1)S(1)}, u32[]{:S(2)}, u32[]{:S(2)}) collective-permute-start(bf16[256,512]{1,0:T(8,128)(2,1)S(1)} %get-tuple-element.231), channel_id=1, source_target_pairs={{0,4},{4,0},{1,5},{5,1},{2,6},{6,2},{3,7},{7,3},{8,12},{12,8},{9,1... | collective-permute-start | bytes 786440 | tf_op jit(solution)/shard_map/cond/branch_1_fun/ppermute | solution.py:17
  121.7 8.1 %collective-permute-start.31 = (bf16[256,512]{1,0:T(8,128)(2,1)S(1)}, bf16[256,512]{1,0:T(8,128)(2,1)S(1)}, u32[]{:S(2)}, u32[]{:S(2)}) collective-permute-start(bf16[256,512]{1,0:T(8,128)(2,1)S(1)} %get-tuple-element.233), channel_id=1, source_target_pairs={{0,2},{2,0},{1,3},{3,1},{4,6},{6,4},{5,7},{7,5},{8,10},{10,8},{9,1... | collective-permute-start | bytes 786440 | tf_op jit(solution)/shard_map/cond/branch_1_fun/ppermute | solution.py:17
  154.0 13.9 %collective-permute-start.40 = (bf16[256,512]{1,0:T(8,128)(2,1)S(1)}, bf16[256,512]{1,0:T(8,128)(2,1)S(1)}, u32[]{:S(2)}, u32[]{:S(2)}) collective-permute-start(bf16[256,512]{1,0:T(8,128)(2,1)S(1)} %get-tuple-element.273), channel_id=1, source_target_pairs={{0,4},{4,0},{1,5},{5,1},{2,6},{6,2},{3,7},{7,3},{8,12},{12,8},{9,1... | collective-permute-start | bytes 786440 | tf_op jit(solution)/shard_map/cond/branch_1_fun/ppermute | solution.py:17
  156.1 11.8 %collective-permute-start.41 = (bf16[256,512]{1,0:T(8,128)(2,1)S(1)}, bf16[256,512]{1,0:T(8,128)(2,1)S(1)}, u32[]{:S(2)}, u32[]{:S(2)}) collective-permute-start(bf16[256,512]{1,0:T(8,128)(2,1)S(1)} %get-tuple-element.275), channel_id=1, source_target_pairs={{0,2},{2,0},{1,3},{3,1},{4,6},{6,4},{5,7},{7,5},{8,10},{10,8},{9,1... | collective-permute-start | bytes 786440 | tf_op jit(solution)/shard_map/cond/branch_1_fun/ppermute | solution.py:17
  179.9 8.4 %collective-permute-start.6 = (bf16[256,512]{1,0:T(8,128)(2,1)S(1)}, bf16[256,512]{1,0:T(8,128)(2,1)S(1)}, u32[]{:S(2)}, u32[]{:S(2)}) collective-permute-start(bf16[256,512]{1,0:T(8,128)(2,1)S(1)} %get-tuple-element.304), channel_id=1, source_target_pairs={{0,4},{4,0},{1,5},{5,1},{2,6},{6,2},{3,7},{7,3},{8,12},{12,8},{9,1... | collective-permute-start | bytes 786440 | tf_op jit(solution)/shard_map/cond/branch_1_fun/ppermute | solution.py:17
  180.2 8.2 %collective-permute-start.7 = (bf16[256,512]{1,0:T(8,128)(2,1)S(1)}, bf16[256,512]{1,0:T(8,128)(2,1)S(1)}, u32[]{:S(2)}, u32[]{:S(2)}) collective-permute-start(bf16[256,512]{1,0:T(8,128)(2,1)S(1)} %get-tuple-element.306), channel_id=1, source_target_pairs={{0,2},{2,0},{1,3},{3,1},{4,6},{6,4},{5,7},{7,5},{8,10},{10,8},{9,1... | collective-permute-start | bytes 786440 | tf_op jit(solution)/shard_map/cond/branch_1_fun/ppermute | solution.py:17
  195.0 22.1 %collective-permute-start.52 = (bf16[256,1792]{1,0:T(8,128)(2,1)}, bf16[256,1792]{1,0:T(8,128)(2,1)S(1)}, u32[]{:S(2)}, u32[]{:S(2)}) collective-permute-start(bf16[256,1792]{1,0:T(8,128)(2,1)} %reduce-scatter.3.cloned.1.call-done), channel_id=1, source_target_pairs={{0,4},{4,0},{1,5},{5,1},{2,6},{6,2},{3,7},{7,3},{8,12},{12,8},{9,1... | collective-permute-start | bytes 2752520 | tf_op jit(solution)/shard_map/ppermute | solution.py:17
  198.1 7.8 %collective-permute-start.15 = (bf16[128,1024]{1,0:T(8,128)(2,1)S(1)}, bf16[128,1024]{1,0:T(8,128)(2,1)}, u32[]{:S(2)}, u32[]{:S(2)}) collective-permute-start(bf16[128,1024]{1,0:T(8,128)(2,1)S(1)} %get-tuple-element.347), channel_id=1, source_target_pairs={{0,2},{2,0},{1,3},{3,1},{4,6},{6,4},{5,7},{7,5},{8,10},{10,8},{9,1... | collective-permute-start | bytes 786440 | tf_op jit(solution)/shard_map/cond/branch_1_fun/ppermute | solution.py:17
  200.4 9.7 %collective-permute-start.13 = (bf16[128,1024]{1,0:T(8,128)(2,1)S(1)}, bf16[128,1024]{1,0:T(8,128)(2,1)S(1)}, u32[]{:S(2)}, u32[]{:S(2)}) collective-permute-start(bf16[128,1024]{1,0:T(8,128)(2,1)S(1)} %branch_1_fun.39.own), channel_id=1, source_target_pairs={{0,2},{2,0},{1,3},{3,1},{4,6},{6,4},{5,7},{7,5},{8,10},{10,8},{9,1... | collective-permute-start | bytes 786440 | tf_op jit(solution)/shard_map/cond/branch_1_fun/ppermute | solution.py:17
  (64 other events, 435.3 us)
Sparse Core Ops, SparseCore 0:
  33.1 65.1 all-gather.1
  115.4 71.1 reduce-scatter.2
  188.9 23.9 reduce-scatter.4

commit v4 on v3

--- a/solution.py
+++ b/solution.py
@@ -871,37 +871,36 @@
         own_rows, small = together(own_rows, small + hop(small, "y"))
         rows_y, rows_core = swap(own_rows, "y"), swap(own_rows, "core")
         output_y = swap(output, "y")
-        rows_y, rows_core, output_y, small = together(rows_y, rows_core, output_y, small + hop(small, "fsdp"))
-        (input_rows,) = call(
-            unpack_rows, [((local, width), F32)], (index, own_rows, rows_y, rows_core, swap(rows_y, "core"))
-        )
-        step = 2
+        step = 1
         while step < size:
             small = small + hop(small, "fsdp", step)
             step *= 2
-        return together(input_rows, output_y, small)
-
-    input_rows, output_y, small = region(flag, finish, pieces, middle_grad, hidden_near, gains, output, small)
+        rows_y, rows_core, output_y, small = together(rows_y, rows_core, output_y, small)
+        results = call(
+            small_results, [((rows,), F32)] * 2 + [((HD,), F32)] * 2 + [((4,), F32)], (index, small)
+        )
+        last, results = together(swap(rows_y, "core"), results)
+        (input_rows,) = call(unpack_rows, [((local, width), F32)], (index, own_rows, rows_y, rows_core, last))
+        return input_rows, output_y, results
+
+    input_rows, output_y, results = region(flag, finish, pieces, middle_grad, hidden_near, gains, output, small)
     output_y, attn_share, ff_other = together(output_y, attn_share, ff_other)
     attn_other = swap(attn_share, "ctx")
 
-    def unpack(index, output, output_y, ff_share, ff_other, small):
+    def unpack(index, output, output_y, ff_share, ff_other):
         output_core, last = swap(output, "core"), swap(output_y, "core")
         ff_grads = call(
             unpack_feed_forward,
             [((rows, 2 * hidden), F32)] * 2 + [((2 * hidden, rows), F32)],
             (index, ff_share, ff_other),
         )
-        results = call(
-            small_results, [((rows,), F32)] * 2 + [((HD,), F32)] * 2 + [((4,), F32)], (index, small)
-        )
-        output_core, last, ff_grads, results = together(output_core, last, ff_grads, results)
+        output_core, last, ff_grads = together(output_core, last, ff_grads)
         (block_rows,) = call(
             unpack_rows, [((local, width), BF16)], (index, output, output_y, output_core, last)
         )
-        return block_rows, ff_grads, results
-
-    block_rows, ff_grads, results = region(flag, unpack, index, output, output_y, ff_share, ff_other, small)
+        return block_rows, ff_grads
+
+    block_rows, ff_grads = region(flag, unpack, index, output, output_y, ff_share, ff_other)
     attn_other, block_rows = together(attn_other, block_rows)
     attn_grads = call(
         unpack_attention,

time: 233 us -> 231 us (level)
  waiting for transfers between devices: 82.1 us -> 79.6 us
    ppermute x43, waiting for transfers between devices: 68.2 us -> 65.6 us  [swap(): return lax.ppermute(value, axis, [(0, 1), (1, 0)])]
  transfers between devices with their start and end apart: 57 -> 57, of which waited for: 35 -> 36; matrix products, arithmetic and copies ran while one was open for 2% -> 2% of each run, Pallas kernels for 22% -> 22%
where the time goes in v4:
time: 231 us; the launch traced here: 230 us
  waiting for transfers between devices  79.6 us (34%)
  Pallas kernels  70.6 us (31%)
  starting transfers between devices  52.9 us (23%)
  between operations  14.6 us (6%)
  local copies, waits for them, and re-layouts  7.64 us (3%)
  other arithmetic  4.56 us (2%)
    pallas_call x26, Pallas kernels, call(): pl.pallas_call(kernel, out_shape=[jax.ShapeDtypeStruct(shape, kind) for s...  70.6 us
    ppermute x43, waiting for transfers between devices, swap(): return lax.ppermute(value, axis, [(0, 1), (1, 0)])  65.6 us
    ppermute x43, starting transfers between devices, swap(): return lax.ppermute(value, axis, [(0, 1), (1, 0)])  35.2 us
    ppermute x5, waiting for transfers between devices, hop(): return lax.ppermute(value, axis, [(i, i ^ step) for i in range(size)])  9.53 us
    ppermute x5, starting transfers between devices, hop(): return lax.ppermute(value, axis, [(i, i ^ step) for i in range(size)])  6.69 us
    unnamed x40, local copies, waits for them, and re-layouts  5.79 us
    ppermute x3, starting transfers between devices, direct(): lax.ppermute(piece, 'fsdp', [(i, i ^ step) for i in range(size)])  5.76 us
    ppermute x3, starting transfers between devices, onward(): lax.ppermute(value, 'fsdp', [(i, (i + 1) % size) for i in range(size)])  5.11 us
  transfers between devices with their start and end apart: 57, of which 36 were waited for; matrix products, arithmetic and copies ran while one was open for 2% of the time, Pallas kernels for 22%

profile of v4, /device:TPU:0, one launch (start us, length us, event | category | flops | bytes accessed | tf_op | source)
XLA Modules:
  0.0 230.2 jit_solution(1829040129040553990)
XLA Ops:
  10.0 5.1 %collective-permute-start.47 = (bf16[272,384]{1,0:T(8,128)(2,1)S(1)}, bf16[272,384]{1,0:T(8,128)(2,1)S(1)}, u32[]{:S(2)}, u32[]{:S(2)}) collective-permute-start(bf16[272,384]{1,0:T(8,128)(2,1)S(1)} %get-tuple-element.504), channel_id=1, source_target_pairs={{0,24},{8,16},{16,8},{24,0},{1,25},{9,17},{17,9},{25,1},{2,26},{10... | collective-permute-start | bytes 626696 | tf_op jit(solution)/shard_map/ppermute | solution.py:72
  15.8 15.3 %conditional.8 = ((bf16[256,1024]{1,0:T(8,128)(2,1)}, bf16[256,1152]{1,0:T(8,128)(2,1)}, bf16[256,640]{1,0:T(8,128)(2,1)S(1)}, f32[1024,128]{1,0:T(8,128)}, f32[...) conditional(s32[]{:T(128)} %bitcast.29, () %tuple.94, ...), branch_computations={%region_0.0_spmd, %region_1.2_spmd} | conditional | flops 267808 | bytes 3195552 | solution.py:98
  18.7 3.3 %branch_1_fun.22 = (bf16[256,1152]{1,0:T(8,128)(2,1)}, bf16[256,640]{1,0:T(8,128)(2,1)S(1)}, bf16[256,1024]{1,0:T(8,128)(2,1)S(1)}, bf16[256,1024]{1,0:T(8,128)(2,1)}) custom-call(s32[5]{0:T(128)S(1)} %get-tuple-element.167.index, bf16[256,1152]{1,0:T(8,128)(2,1)} %get-tuple-element.603.rest_0_, bf16[256,1152]{1,0:T(8,128)(2,1)} %get-tuple-element.604.rest_1_, ...), custom_call_target="tpu_custom_call" | custom-call | flops 1000 | bytes 1000 | tf_op jit(solution)/shard_map/cond/branch_1_fun/pallas_call | solution.py:626
  25.2 5.8 %collective-permute-done.21 = bf16[256,1024]{1,0:T(8,128)(2,1)} collective-permute-done((bf16[256,1024]{1,0:T(8,128)(2,1)S(1)}, bf16[256,1024]{1,0:T(8,128)(2,1)}, u32[]{:S(2)}, u32[]{:S(2)}) %collective-permute-start.21) | collective-permute-done | bytes 524320 | tf_op jit(solution)/shard_map/cond/branch_1_fun/ppermute | solution.py:17
  35.8 9.9 %conditional.9 = ((bf16[512,1024]{1,0:T(8,128)(2,1)S(1)}, bf16[512,1024]{1,0:T(8,128)(2,1)}, f32[8,1024]{1,0:T(8,128)S(1)}, bf16[1024,1024]{1,0:T(8,128)(2,1)}, ...) conditional(s32[]{:T(128)} %bitcast.29, () %tuple.93, ...), branch_computations={%region_2.3_spmd, %region_3.4_spmd} | conditional | flops 8000001024 | bytes 2098284 | solution.py:98
  36.6 9.1 %branch_1_fun.23 = (bf16[1024,384]{1,0:T(8,128)(2,1)}, f32[8,1024]{1,0:T(8,128)S(1)}, bf16[512,1024]{1,0:T(8,128)(2,1)S(1)}, bf16[512,1024]{1,0:T(8,128)(2,1)}, ...) custom-call(s32[5]{0:T(128)S(1)} %get-tuple-element.183.index, ...), custom_call_target="tpu_custom_call" | custom-call | flops 8000001024 | bytes 1000 | tf_op jit(solution)/shard_map/cond/branch_1_fun/pallas_call | solution.py:626
  45.9 20.3 %conditional.10 = ((f32[128,1024]{1,0:T(8,128)}, f32[128,128]{1,0:T(8,128)S(1)}, bf16[128,512]{1,0:T(8,128)(2,1)S(1)}, bf16[128,512]{1,0:T(8,128)(2,1)S(1)})) conditional(s32[]{:T(128)} %bitcast.29, () %tuple.92, (bf16[512,1024]{1,0:T(8,128)(2,1)}, bf16[512,1024]{1,0:T(8,128)(2,1)S(1)}, bf16[256,1024]{1,0:T(8,128)(2,1)S(1)}, ...), branch_computations={%region_4.5_spmd, %region_5.6_spmd} | conditional | flops 3000 | bytes 7343240 | solution.py:98
  52.1 5.3 %collective-permute-done.1.from_x = bf16[256,512]{1,0:T(8,128)(2,1)S(1)} collective-permute-done((bf16[256,512]{1,0:T(8,128)(2,1)S(1)}, bf16[256,512]{1,0:T(8,128)(2,1)S(1)}, u32[]{:S(2)}, u32[]{:S(2)}) %collective-permute-start.1) | collective-permute-done | bytes 262176 | tf_op jit(solution)/shard_map/cond/branch_1_fun/ppermute | solution.py:17
  66.2 5.1 %collective-permute-start.51 = (bf16[256,640]{1,0:T(8,128)(2,1)S(1)}, bf16[256,640]{1,0:T(8,128)(2,1)S(1)}, u32[]{:S(2)}, u32[]{:S(2)}) collective-permute-start(bf16[256,640]{1,0:T(8,128)(2,1)S(1)} %collective-permute-done.50.rest_2_), channel_id=1, source_target_pairs={{0,8},{8,16},{16,24},{24,0},{1,9},{9,17},{17,25},{25,1},{2,10},{10... | collective-permute-start | bytes 983048 | tf_op jit(solution)/shard_map/ppermute | solution.py:79
  71.3 19.2 %conditional.11 = ((bf16[512,1024]{1,0:T(8,128)(2,1)}, bf16[512,1024]{1,0:T(8,128)(2,1)}, bf16[256,1024]{1,0:T(8,128)(2,1)})) conditional(s32[]{:T(128)} %bitcast.29, () %tuple.91, (bf16[128,512]{1,0:T(8,128)(2,1)S(1)}, bf16[256,1024]{1,0:T(8,128)(2,1)}, bf16[128,512]{1,0:T(8,128)(2,1)S(1)}) %tuple.101), branch_computations={%region_6.7_spmd, %region_7.8_spmd} | conditional | flops 4456448 | bytes 13107472 | solution.py:98
  72.5 4.7 %collective-permute-done.24 = bf16[128,512]{1,0:T(8,128)(2,1)S(1)} collective-permute-done((bf16[128,512]{1,0:T(8,128)(2,1)S(1)}, bf16[128,512]{1,0:T(8,128)(2,1)S(1)}, u32[]{:S(2)}, u32[]{:S(2)}) %collective-permute-start.24) | collective-permute-done | bytes 131104 | tf_op jit(solution)/shard_map/cond/branch_1_fun/ppermute | solution.py:17
  80.4 5.0 %collective-permute-done.26 = bf16[2,128,512]{2,1,0:T(8,128)(2,1)S(1)} collective-permute-done((bf16[2,128,512]{2,1,0:T(8,128)(2,1)S(1)}, bf16[2,128,512]{2,1,0:T(8,128)(2,1)S(1)}, u32[]{:S(2)}, u32[]{:S(2)}) %collective-permute-start.26) | collective-permute-done | bytes 262176 | tf_op jit(solution)/shard_map/cond/branch_1_fun/ppermute | solution.py:17
  92.2 3.5 %shard_map.260 = (bf16[1024,640]{1,0:T(8,128)(2,1)}, f32[1024,640]{1,0:T(8,128)S(1)}) custom-call(s32[5]{0:T(128)S(1)} %stack.93.index, bf16[256,1024]{1,0:T(8,128)(2,1)} %copy-done.7, bf16[256,1024]{1,0:T(8,128)(2,1)} %collective-permute-done.49.b1, bf16[256,1024]{1,0:T(8,128)(2,1)} %get-tuple-element.528.b2, bf16[256,1024]{1,0:T(8,128)(2,1)} %get-tuple-element.529.b3, ...), custom_call_target="tpu_custom_call" | custom-call | flops 1000 | bytes 1000 | tf_op jit(solution)/shard_map/pallas_call | solution.py:626
  99.9 15.3 %shard_map.261 = (bf16[512,1024]{1,0:T(8,128)(2,1)}, bf16[512,1024]{1,0:T(8,128)(2,1)}, bf16[1024,1792]{1,0:T(8,128)(2,1)}, bf16[1024,640]{1,0:T(8,128)(2,1)}) custom-call(s32[5]{0:T(128)S(1)} %stack.93.index, bf16[512,1024]{1,0:T(8,128)(2,1)} %get-tuple-element.526.x_low, bf16[512,1024]{1,0:T(8,128)(2,1)} %get-tuple-element.527.x_high, ...), custom_call_target="tpu_custom_call" | custom-call | flops 1000 | bytes 1000 | tf_op jit(solution)/shard_map/pallas_call | solution.py:626
  117.0 58.4 %conditional.12 = ((bf16[512,1024]{1,0:T(8,128)(2,1)}, bf16[512,1024]{1,0:T(8,128)(2,1)}, bf16[1024,384]{1,0:T(8,128)(2,1)}, f32[8,1024]{1,0:T(8,128)S(1)}, f32[...) conditional(s32[]{:T(128)} %bitcast.29, () %tuple.90, ...), branch_computations={%region_8.9_spmd, %region_9.10_spmd} | conditional | flops 4464448 | bytes 54010640 | solution.py:98
  123.2 4.1 %branch_1_fun.28 = (bf16[512,1024]{1,0:T(8,128)(2,1)S(1)}, bf16[512,1024]{1,0:T(8,128)(2,1)S(1)}) custom-call(s32[5]{0:T(128)S(1)} %get-tuple-element.226.index, bf16[1024,640]{1,0:T(8,128)(2,1)} %get-tuple-element.233.activated, bf16[1024,640]{1,0:T(8,128)(2,1)S(1)} %copy-done.11), custom_call_target="tpu_custom_call" | custom-call | flops 1000 | bytes 1000 | tf_op jit(solution)/shard_map/cond/branch_1_fun/pallas_call | solution.py:626
  139.0 4.0 %collective-permute-done.34 = bf16[128,512]{1,0:T(8,128)(2,1)S(1)} collective-permute-done((bf16[128,512]{1,0:T(8,128)(2,1)S(1)}, bf16[128,512]{1,0:T(8,128)(2,1)S(1)}, u32[]{:S(2)}, u32[]{:S(2)}) %collective-permute-start.34) | collective-permute-done | bytes 131104 | tf_op jit(solution)/shard_map/cond/branch_1_fun/ppermute | solution.py:17
  156.6 11.3 %branch_1_fun.31 = (bf16[512,1024]{1,0:T(8,128)(2,1)}, bf16[512,1024]{1,0:T(8,128)(2,1)}, bf16[1024,256]{1,0:T(8,128)(2,1)S(1)}, f32[8,128]{1,0:T(8,128)S(1)}) custom-call(s32[5]{0:T(128)S(1)} %get-tuple-element.226.index, bf16[512,1024]{1,0:T(8,128)(2,1)S(1)} %bitcast.49, bf16[512,1024]{1,0:T(8,128)(2,1)S(1)} %collective-permute-done.38.a_high, ...), custom_call_target="tpu_custom_call" | custom-call | flops 1000 | bytes 1000 | tf_op jit(solution)/shard_map/cond/branch_1_fun/pallas_call | solution.py:626
  175.4 19.5 %conditional.13 = ((f32[128,512]{1,0:T(8,128)S(1)}, bf16[128,512]{1,0:T(8,128)(2,1)}, f32[128,512]{1,0:T(8,128)}, bf16[128,512]{1,0:T(8,128)(2,1)}, f32[24,128]{...) conditional(s32[]{:T(128)} %bitcast.29, () %tuple.89, (bf16[512,1024]{1,0:T(8,128)(2,1)}, ...), branch_computations={%region_10.11_spmd, %region_11.12_spmd} | conditional | flops 10144 | bytes 7516400 | solution.py:98
  184.2 4.1 %collective-permute-done.6.from_x = bf16[256,512]{1,0:T(8,128)(2,1)S(1)} collective-permute-done((bf16[256,512]{1,0:T(8,128)(2,1)S(1)}, bf16[256,512]{1,0:T(8,128)(2,1)S(1)}, u32[]{:S(2)}, u32[]{:S(2)}) %collective-permute-start.6) | collective-permute-done | bytes 262176 | tf_op jit(solution)/shard_map/cond/branch_1_fun/ppermute | solution.py:17
  191.6 3.3 %collective-permute-done.11 = f32[24,128]{1,0:T(8,128)S(1)} collective-permute-done((f32[24,128]{1,0:T(8,128)S(1)}, f32[24,128]{1,0:T(8,128)S(1)}, u32[]{:S(2)}, u32[]{:S(2)}) %collective-permute-start.11) | collective-permute-done | bytes 12320 | tf_op jit(solution)/shard_map/cond/branch_1_fun/ppermute | solution.py:22
  196.5 18.3 %conditional.14 = (bf16[128,1024]{1,0:T(8,128)(2,1)}, f32[256]{0:T(256)}, f32[256]{0:T(256)}, f32[64]{0:T(128)}, f32[64]{0:T(128)}, /*index=5*/f32[4]{0:T(128)}, f32[1,512,1024]{2,1,0:T(8,128)}) conditional(s32[]{:T(128)} %bitcast.29, () %tuple.88, (f32[128,512]{1,0:T(8,128)S(1)}, bf16[128,512]{1,0:T(8,128)(2,1)}, f32[128,512]{1,0:T(8,128)}, ...), branch_computations={%region_13.14_spmd, %region_14.15_spmd} | conditional | flops 12216 | bytes 4455688 | solution.py:98
  205.8 3.6 %collective-permute-start.17 = (f32[24,128]{1,0:T(8,128)S(1)}, f32[24,128]{1,0:T(8,128)S(1)}, u32[]{:S(2)}, u32[]{:S(2)}) collective-permute-start(f32[24,128]{1,0:T(8,128)S(1)} %add.55), channel_id=1, source_target_pairs={{0,16},{8,24},{16,0},{24,8},{1,17},{9,25},{17,1},{25,9},{2,18},{10... | collective-permute-start | bytes 36872 | tf_op jit(solution)/shard_map/cond/branch_1_fun/ppermute | solution.py:22
  216.5 4.4 %conditional.15 = ((bf16[512,1024]{1,0:T(8,128)(2,1)S(1)}, f32[256,1152]{1,0:T(8,128)}, f32[256,1152]{1,0:T(8,128)}, f32[1152,256]{1,0:T(8,128)})) conditional(s32[]{:T(128)} %bitcast.29, () %tuple.110, (bf16[128,1024]{1,0:T(8,128)(2,1)S(1)}, bf16[128,1024]{1,0:T(8,128)(2,1)}, s32[5]{0:T(128)S(1)}, bf16[256,1792]{1,0:T(8,128)(2,1)S(1)}, ...), branch_computations={%region_16.17_spmd, %region_17.18_spmd} | conditional | flops 2000 | bytes 2099272 | solution.py:98
  (215 shorter events, 122.7 us)
Async XLA Ops:
  7.2 91.1 %all-gather.2.cloned.1.call-start = ((), (), s32[]{:S(2)}) async-start(), calls=%async_computation.2 | async-start | bytes 2949120 | tf_op jit(solution)/shard_map/all_gather | solution.py:725
  10.0 21.0 %collective-permute-start.47 = (bf16[272,384]{1,0:T(8,128)(2,1)S(1)}, bf16[272,384]{1,0:T(8,128)(2,1)S(1)}, u32[]{:S(2)}, u32[]{:S(2)}) collective-permute-start(bf16[272,384]{1,0:T(8,128)(2,1)S(1)} %get-tuple-element.504), channel_id=1, source_target_pairs={{0,24},{8,16},{16,8},{24,0},{1,25},{9,17},{17,9},{25,1},{2,26},{10... | collective-permute-start | bytes 626696 | tf_op jit(solution)/shard_map/ppermute | solution.py:72
  15.2 17.7 %collective-permute-start.46 = (bf16[272,384]{1,0:T(8,128)(2,1)S(1)}, bf16[272,384]{1,0:T(8,128)(2,1)S(1)}, u32[]{:S(2)}, u32[]{:S(2)}) collective-permute-start(bf16[272,384]{1,0:T(8,128)(2,1)S(1)} %get-tuple-element.504), channel_id=1, source_target_pairs={{0,16},{8,24},{16,0},{24,8},{1,17},{9,25},{17,1},{25,9},{2,18},{10... | collective-permute-start | bytes 626696 | tf_op jit(solution)/shard_map/ppermute | solution.py:72
  15.2 17.7 %collective-permute-start.45 = (bf16[272,384]{1,0:T(8,128)(2,1)S(1)}, bf16[272,384]{1,0:T(8,128)(2,1)S(1)}, u32[]{:S(2)}, u32[]{:S(2)}) collective-permute-start(bf16[272,384]{1,0:T(8,128)(2,1)S(1)} %get-tuple-element.504), channel_id=1, source_target_pairs={{0,8},{8,0},{16,24},{24,16},{1,9},{9,1},{17,25},{25,17},{2,10},{10... | collective-permute-start | bytes 626696 | tf_op jit(solution)/shard_map/ppermute | solution.py:72
  18.3 12.8 %collective-permute-start.21 = (bf16[256,1024]{1,0:T(8,128)(2,1)S(1)}, bf16[256,1024]{1,0:T(8,128)(2,1)}, u32[]{:S(2)}, u32[]{:S(2)}) collective-permute-start(bf16[256,1024]{1,0:T(8,128)(2,1)S(1)} %get-tuple-element.166), channel_id=1, source_target_pairs={{0,4},{4,0},{1,5},{5,1},{2,6},{6,2},{3,7},{7,3},{8,12},{12,8},{9,1... | collective-permute-start | bytes 1572872 | tf_op jit(solution)/shard_map/cond/branch_1_fun/ppermute | solution.py:17
  32.9 162.1 %reduce-scatter.3.cloned.1.call-start = ((), (), s32[]{:S(2)}) async-start(), calls=%async_computation.3 | async-start | bytes 4587520 | tf_op jit(solution)/shard_map/reduce_scatter | solution.py:787
  33.7 12.1 %collective-permute-start.48 = (bf16[256,640]{1,0:T(8,128)(2,1)S(1)}, bf16[256,640]{1,0:T(8,128)(2,1)S(1)}, u32[]{:S(2)}, u32[]{:S(2)}) collective-permute-start(bf16[256,640]{1,0:T(8,128)(2,1)S(1)} %get-tuple-element.531.rest_0_), channel_id=1, source_target_pairs={{0,8},{8,16},{16,24},{24,0},{1,9},{9,17},{17,25},{25,1},{2,10},{10... | collective-permute-start | bytes 983048 | tf_op jit(solution)/shard_map/ppermute | solution.py:79
  33.7 32.5 %collective-permute-start.49 = (bf16[256,1024]{1,0:T(8,128)(2,1)S(1)}, bf16[256,1024]{1,0:T(8,128)(2,1)}, u32[]{:S(2)}, u32[]{:S(2)}) collective-permute-start(bf16[256,1024]{1,0:T(8,128)(2,1)S(1)} %get-tuple-element.515.b0), channel_id=1, source_target_pairs={{0,4},{4,0},{1,5},{5,1},{2,6},{6,2},{3,7},{7,3},{8,12},{12,8},{9,1... | collective-permute-start | bytes 1572872 | tf_op jit(solution)/shard_map/ppermute | solution.py:17
  45.8 20.4 %collective-permute-start.50 = (bf16[256,640]{1,0:T(8,128)(2,1)S(1)}, bf16[256,640]{1,0:T(8,128)(2,1)S(1)}, u32[]{:S(2)}, u32[]{:S(2)}) collective-permute-start(bf16[256,640]{1,0:T(8,128)(2,1)S(1)} %collective-permute-done.48.rest_1_), channel_id=1, source_target_pairs={{0,8},{8,16},{16,24},{24,0},{1,9},{9,17},{17,25},{25,1},{2,10},{10... | collective-permute-start | bytes 983048 | tf_op jit(solution)/shard_map/ppermute | solution.py:79
  49.0 8.4 %collective-permute-start.1 = (bf16[256,512]{1,0:T(8,128)(2,1)S(1)}, bf16[256,512]{1,0:T(8,128)(2,1)S(1)}, u32[]{:S(2)}, u32[]{:S(2)}) collective-permute-start(bf16[256,512]{1,0:T(8,128)(2,1)S(1)} %get-tuple-element.211), channel_id=1, source_target_pairs={{0,4},{4,0},{1,5},{5,1},{2,6},{6,2},{3,7},{7,3},{8,12},{12,8},{9,1... | collective-permute-start | bytes 786440 | tf_op jit(solution)/shard_map/cond/branch_1_fun/ppermute | solution.py:17
  50.6 8.1 %collective-permute-start.2 = (bf16[256,512]{1,0:T(8,128)(2,1)S(1)}, bf16[256,512]{1,0:T(8,128)(2,1)S(1)}, u32[]{:S(2)}, u32[]{:S(2)}) collective-permute-start(bf16[256,512]{1,0:T(8,128)(2,1)S(1)} %get-tuple-element.213), channel_id=1, source_target_pairs={{0,2},{2,0},{1,3},{3,1},{4,6},{6,4},{5,7},{7,5},{8,10},{10,8},{9,1... | collective-permute-start | bytes 786440 | tf_op jit(solution)/shard_map/cond/branch_1_fun/ppermute | solution.py:17
  66.2 24.3 %collective-permute-start.51 = (bf16[256,640]{1,0:T(8,128)(2,1)S(1)}, bf16[256,640]{1,0:T(8,128)(2,1)S(1)}, u32[]{:S(2)}, u32[]{:S(2)}) collective-permute-start(bf16[256,640]{1,0:T(8,128)(2,1)S(1)} %collective-permute-done.50.rest_2_), channel_id=1, source_target_pairs={{0,8},{8,16},{16,24},{24,0},{1,9},{9,17},{17,25},{25,1},{2,10},{10... | collective-permute-start | bytes 983048 | tf_op jit(solution)/shard_map/ppermute | solution.py:79
  77.2 8.1 %collective-permute-start.26 = (bf16[2,128,512]{2,1,0:T(8,128)(2,1)S(1)}, bf16[2,128,512]{2,1,0:T(8,128)(2,1)S(1)}, u32[]{:S(2)}, u32[]{:S(2)}) collective-permute-start(bf16[2,128,512]{2,1,0:T(8,128)(2,1)S(1)} %get-tuple-element.615), channel_id=1, source_target_pairs={{0,2},{2,0},{1,3},{3,1},{4,6},{6,4},{5,7},{7,5},{8,10},{10,8},{9,1... | collective-permute-start | bytes 786440 | tf_op jit(solution)/shard_map/cond/branch_1_fun/ppermute | solution.py:17
  115.3 99.5 %reduce-scatter.5.cloned.1.call-start = ((), (), s32[]{:S(2)}) async-start(), calls=%async_computation.4 | async-start | bytes 983040 | tf_op jit(solution)/shard_map/reduce_scatter | solution.py:836
  120.1 8.4 %collective-permute-start.30 = (bf16[256,512]{1,0:T(8,128)(2,1)S(1)}, bf16[256,512]{1,0:T(8,128)(2,1)S(1)}, u32[]{:S(2)}, u32[]{:S(2)}) collective-permute-start(bf16[256,512]{1,0:T(8,128)(2,1)S(1)} %get-tuple-element.230), channel_id=1, source_target_pairs={{0,4},{4,0},{1,5},{5,1},{2,6},{6,2},{3,7},{7,3},{8,12},{12,8},{9,1... | collective-permute-start | bytes 786440 | tf_op jit(solution)/shard_map/cond/branch_1_fun/ppermute | solution.py:17
  121.7 8.1 %collective-permute-start.31 = (bf16[256,512]{1,0:T(8,128)(2,1)S(1)}, bf16[256,512]{1,0:T(8,128)(2,1)S(1)}, u32[]{:S(2)}, u32[]{:S(2)}) collective-permute-start(bf16[256,512]{1,0:T(8,128)(2,1)S(1)} %get-tuple-element.232), channel_id=1, source_target_pairs={{0,2},{2,0},{1,3},{3,1},{4,6},{6,4},{5,7},{7,5},{8,10},{10,8},{9,1... | collective-permute-start | bytes 786440 | tf_op jit(solution)/shard_map/cond/branch_1_fun/ppermute | solution.py:17
  154.0 13.9 %collective-permute-start.40 = (bf16[256,512]{1,0:T(8,128)(2,1)S(1)}, bf16[256,512]{1,0:T(8,128)(2,1)S(1)}, u32[]{:S(2)}, u32[]{:S(2)}) collective-permute-start(bf16[256,512]{1,0:T(8,128)(2,1)S(1)} %get-tuple-element.272), channel_id=1, source_target_pairs={{0,4},{4,0},{1,5},{5,1},{2,6},{6,2},{3,7},{7,3},{8,12},{12,8},{9,1... | collective-permute-start | bytes 786440 | tf_op jit(solution)/shard_map/cond/branch_1_fun/ppermute | solution.py:17
  156.1 11.8 %collective-permute-start.41 = (bf16[256,512]{1,0:T(8,128)(2,1)S(1)}, bf16[256,512]{1,0:T(8,128)(2,1)S(1)}, u32[]{:S(2)}, u32[]{:S(2)}) collective-permute-start(bf16[256,512]{1,0:T(8,128)(2,1)S(1)} %get-tuple-element.274), channel_id=1, source_target_pairs={{0,2},{2,0},{1,3},{3,1},{4,6},{6,4},{5,7},{7,5},{8,10},{10,8},{9,1... | collective-permute-start | bytes 786440 | tf_op jit(solution)/shard_map/cond/branch_1_fun/ppermute | solution.py:17
  179.9 8.4 %collective-permute-start.6 = (bf16[256,512]{1,0:T(8,128)(2,1)S(1)}, bf16[256,512]{1,0:T(8,128)(2,1)S(1)}, u32[]{:S(2)}, u32[]{:S(2)}) collective-permute-start(bf16[256,512]{1,0:T(8,128)(2,1)S(1)} %get-tuple-element.303), channel_id=1, source_target_pairs={{0,4},{4,0},{1,5},{5,1},{2,6},{6,2},{3,7},{7,3},{8,12},{12,8},{9,1... | collective-permute-start | bytes 786440 | tf_op jit(solution)/shard_map/cond/branch_1_fun/ppermute | solution.py:17
  180.2 8.2 %collective-permute-start.7 = (bf16[256,512]{1,0:T(8,128)(2,1)S(1)}, bf16[256,512]{1,0:T(8,128)(2,1)S(1)}, u32[]{:S(2)}, u32[]{:S(2)}) collective-permute-start(bf16[256,512]{1,0:T(8,128)(2,1)S(1)} %get-tuple-element.305), channel_id=1, source_target_pairs={{0,2},{2,0},{1,3},{3,1},{4,6},{6,4},{5,7},{7,5},{8,10},{10,8},{9,1... | collective-permute-start | bytes 786440 | tf_op jit(solution)/shard_map/cond/branch_1_fun/ppermute | solution.py:17
  195.0 20.1 %collective-permute-start.52 = (bf16[256,1792]{1,0:T(8,128)(2,1)}, bf16[256,1792]{1,0:T(8,128)(2,1)S(1)}, u32[]{:S(2)}, u32[]{:S(2)}) collective-permute-start(bf16[256,1792]{1,0:T(8,128)(2,1)} %reduce-scatter.3.cloned.1.call-done), channel_id=1, source_target_pairs={{0,4},{4,0},{1,5},{5,1},{2,6},{6,2},{3,7},{7,3},{8,12},{12,8},{9,1... | collective-permute-start | bytes 2752520 | tf_op jit(solution)/shard_map/ppermute | solution.py:17
  198.1 13.1 %collective-permute-start.15 = (bf16[128,1024]{1,0:T(8,128)(2,1)S(1)}, bf16[128,1024]{1,0:T(8,128)(2,1)}, u32[]{:S(2)}, u32[]{:S(2)}) collective-permute-start(bf16[128,1024]{1,0:T(8,128)(2,1)S(1)} %get-tuple-element.349), channel_id=1, source_target_pairs={{0,2},{2,0},{1,3},{3,1},{4,6},{6,4},{5,7},{7,5},{8,10},{10,8},{9,1... | collective-permute-start | bytes 786440 | tf_op jit(solution)/shard_map/cond/branch_1_fun/ppermute | solution.py:17
  200.4 10.8 %collective-permute-start.14 = (bf16[128,1024]{1,0:T(8,128)(2,1)S(1)}, bf16[128,1024]{1,0:T(8,128)(2,1)S(1)}, u32[]{:S(2)}, u32[]{:S(2)}) collective-permute-start(bf16[128,1024]{1,0:T(8,128)(2,1)S(1)} %branch_1_fun.39.own), channel_id=1, source_target_pairs={{0,1},{1,0},{2,3},{3,2},{4,5},{5,4},{6,7},{7,6},{8,9},{9,8},{10,11... | collective-permute-start | bytes 786440 | tf_op jit(solution)/shard_map/cond/branch_1_fun/ppermute | solution.py:17
  200.4 10.8 %collective-permute-start.13 = (bf16[128,1024]{1,0:T(8,128)(2,1)S(1)}, bf16[128,1024]{1,0:T(8,128)(2,1)S(1)}, u32[]{:S(2)}, u32[]{:S(2)}) collective-permute-start(bf16[128,1024]{1,0:T(8,128)(2,1)S(1)} %branch_1_fun.39.own), channel_id=1, source_target_pairs={{0,2},{2,0},{1,3},{3,1},{4,6},{6,4},{5,7},{7,5},{8,10},{10,8},{9,1... | collective-permute-start | bytes 786440 | tf_op jit(solution)/shard_map/cond/branch_1_fun/ppermute | solution.py:17
  (64 other events, 432.4 us)
Sparse Core Ops, SparseCore 0:
  33.1 65.1 all-gather.1
  115.4 71.1 reduce-scatter.2
  188.9 24.0 reduce-scatter.4
